TPU v7x, 32 devices: a whole 2x2x4 slice. The times are simulated.
32 devices in a mesh: own: 8 (over y, x, core), qry: 4 (over z).
Axes of the slice: x: 2, y: 2, z: 4, core: 2. Of those that a mesh axis runs over, the one named last changes fastest.
Arguments:
- queries: bfloat16 [4, 64, 8192], P('qry', 'own'), may hold values from -6 to 6
- block_ids: int32 [4, 64], P('qry', 'own'), may hold values from 0 to 1
- left_factor: bfloat16 [2, 64, 64], P(None, 'qry'), may hold values from -0.75 to 0.75
- right_factor: bfloat16 [2, 128, 128], P(None, 'qry'), may hold values from -0.5 to 0.5
- clip_grads: bfloat16 [4096, 8192], P('own'), may hold values from -6 to 6
- lengths: int32 [4096], P('own'), may hold values from 1 to 64
Outputs:
- scores: float32 [4, 64, 4096], P('qry', 'own')
All inputs are finite; a program needn't handle non-finite values.
Results may differ from a plain program's by a relative error of at most 0.0029.
Values may be sent and summed in bfloat16 or wider, within the bound.
No kernel may reach another device: no remote copies, remote signals or barrier semaphores. Data moves between devices by JAX's collectives and lax.ppermute only.
A program may use at most 64 MiB of HBM per device.

v0:
```python
import jax
import jax.numpy as jnp
from jax import lax
from jax.sharding import PartitionSpec as P


def precondition(rows, id_values, left_full, right_full):
    blocks = left_full.shape[0]
    order_a = left_full.shape[1]
    order_b = right_full.shape[1]
    labels = jnp.arange(blocks)
    onehot = (id_values[:, :, None] == labels[None, None, :]).astype(jnp.float32)
    left_rows = jnp.einsum(
        "srk,kac->srac", onehot, left_full.astype(jnp.float32), precision=lax.Precision.HIGHEST
    )
    right_rows = jnp.einsum(
        "srk,kde->srde", onehot, right_full.astype(jnp.float32), precision=lax.Precision.HIGHEST
    )
    matrix = rows.reshape(rows.shape[0], rows.shape[1], order_a, order_b).astype(jnp.float32)
    inner = jnp.einsum("srac,srcd->srad", left_rows, matrix, precision=lax.Precision.HIGHEST)
    outer = jnp.einsum("srad,srde->srae", inner, right_rows, precision=lax.Precision.HIGHEST)
    return outer.reshape(rows.shape).astype(jnp.bfloat16)


def per_device(queries, block_ids, left_factor, right_factor, clip_grads, lengths):
    left_full, right_full = (
        lax.all_gather(left_factor, "qry", axis=1, tiled=True),
        lax.all_gather(right_factor, "qry", axis=1, tiled=True),
    )
    width_all = queries.shape[2]
    prepared = precondition(queries, block_ids, left_full, right_full)
    tiles = jnp.einsum(
        "srw,cw->src",
        lax.all_gather(prepared, "own", axis=1, tiled=True),
        clip_grads,
        preferred_element_type=jnp.float32,
    )
    returned = lax.all_to_all(tiles, "own", split_axis=1, concat_axis=2, tiled=True)
    all_lengths = lax.all_gather(lengths, "own", axis=0, tiled=True)
    whole_factor = lax.rsqrt(jnp.float32(width_all) * all_lengths.astype(jnp.float32))
    returned = returned * whole_factor[None, None, :]
    return returned


def solution(mesh):
    in_specs = (
        P("qry", "own", None),
        P("qry", "own"),
        P(None, "qry", None),
        P(None, "qry", None),
        P("own", None),
        P("own"),
    )
    out_specs = P("qry", "own", None)
    return jax.shard_map(
        per_device, mesh=mesh, in_specs=in_specs, out_specs=out_specs, check_vma=False
    )
```

profile of v0, /device:TPU:0, one launch (start us, length us, event | category | flops | bytes accessed | tf_op | source)
XLA Modules:
  0.0 86.9 jit_solution(7908328669690137945)
XLA Ops:
  6.5 0.0 copy-start
  6.5 0.0 all-gather.3.cloned.1.call-start
  6.5 15.2 %all_gather.13 = bf16[2,128,128]{2,1,0:T(8,128)(2,1)S(1)} all-gather(bf16[2,32,128]{2,1,0:T(8,128)(2,1)} %param.9), channel_id=1, replica_groups=mesh['own'=8,'qry'=4] {'qry'}, dimensions={1}, use_global_device_ids=true | all-gather | bytes 81920 | tf_op jit(solution)/shard_map/all_gather | solution.py:28
  21.8 13.3 %all_gather.12 = bf16[2,64,64]{2,1,0:T(8,128)(2,1)S(1)} all-gather(bf16[2,16,64]{2,1,0:T(8,128)(2,1)} %param.8), channel_id=1, replica_groups=mesh['own'=8,'qry'=4] {'qry'}, dimensions={1}, use_global_device_ids=true | all-gather | bytes 20480 | tf_op jit(solution)/shard_map/all_gather | solution.py:27
  35.1 0.9 %fusion.5 = f32[8,128,128]{2,0,1:T(8,128)S(1)} fusion(bf16[2,128,128]{2,1,0:T(8,128)(2,1)S(1)} %all_gather.13, s32[8]{0:T(128)} %bitcast.24), kind=kOutput, calls=%fused_computation.7 | convolution fusion | flops 524304 | bytes 589856 | tf_op jit(solution)/shard_map/srk,kde->srde/dot_general | solution.py:16
  36.0 0.9 %fusion.7 = f32[8,64,64]{2,0,1:T(8,128)S(1)} fusion(bf16[2,64,64]{2,1,0:T(8,128)(2,1)S(1)} %all_gather.12, s32[8]{0:T(128)} %bitcast.25), kind=kOutput, calls=%fused_computation.10 | convolution fusion | flops 131088 | bytes 147488 | tf_op jit(solution)/shard_map/srk,kac->srac/dot_general | solution.py:13
  36.9 0.0 copy-done
  36.9 0.3 fusion.2
  37.2 0.6 convolution_convert_fusion
  37.8 0.7 convert_element_type.22
  38.5 0.0 all-gather.3.cloned.1.call-update
  38.6 9.0 %all-gather = s32[8,1,512]{2,1,0:T(1,128)S(1)} all-gather(s32[1,1,512]{2,1,0:T(1,128)} %bitcast.23), channel_id=1, replica_groups=mesh['own'=8,'qry'=4] {'own'}, dimensions={0}, use_global_device_ids=true | all-gather | bytes 18432 | tf_op jit(solution)/shard_map/all_gather | solution.py:39
  47.6 15.8 %all-gather.3.cloned.1.call-done = bf16[1,64,8192]{2,1,0:T(8,128)(2,1)} async-done(((bf16[1,8,8192]{2,1,0:T(8,128)(2,1)}), bf16[1,64,8192]{2,1,0:T(8,128)(2,1)}) %all-gather.3.cloned.1.call-update) | async-done | bytes 1048592 | tf_op jit(solution)/shard_map/all_gather | solution.py:34
  63.4 6.4 %convolution_bitcast_fusion = f32[1,64,512]{2,1,0:T(8,128)S(1)} fusion(bf16[512,8192]{1,0:T(8,128)(2,1)} %param.10, bf16[1,64,8192]{2,1,0:T(8,128)(2,1)} %all-gather.3.cloned.1.call-done), kind=kOutput, calls=%fused_computation.1 | convolution fusion | flops 536870912 | bytes 9568256 | tf_op jit(solution)/shard_map/srw,cw->src/dot_general | solution.py:32
  69.7 0.8 copy.7
  70.5 3.4 %all-to-all-start = ((f32[1,64,512]{2,0,1:T(1,128)}), f32[1,64,512]{2,0,1:T(1,128)S(1)}, u32[]{:S(2)}, u32[]{:S(2)}) async-start(f32[1,64,512]{2,0,1:T(1,128)} %copy.7), calls=%async_computation | async-start | bytes 262144 | tf_op jit(solution)/shard_map/all_to_all | solution.py:38
  73.9 5.4 %all-to-all-done = f32[1,64,512]{2,0,1:T(1,128)S(1)} async-done(((f32[1,64,512]{2,0,1:T(1,128)}), f32[1,64,512]{2,0,1:T(1,128)S(1)}, u32[]{:S(2)}, u32[]{:S(2)}) %all-to-all-start) | async-done | bytes 131104 | tf_op jit(solution)/shard_map/all_to_all | solution.py:38
  79.4 0.7 broadcast_multiply_fusion
  (2 shorter events, 0.0 us)
Async XLA Ops:
  6.5 30.4 %copy-start = (bf16[1,8,8192]{2,1,0:T(8,128)(2,1)S(1)}, bf16[1,8,8192]{2,1,0:T(8,128)(2,1)}, u32[]{:S(2)}) copy-start(bf16[1,8,8192]{2,1,0:T(8,128)(2,1)} %param.6) | copy-start | bytes 393220
  6.5 56.8 %all-gather.3.cloned.1.call-start = ((), (), s32[]{:S(2)}) async-start(), calls=%async_computation.1 | async-start | bytes 1179648 | tf_op jit(solution)/shard_map/all_gather | solution.py:34
  70.5 8.8 %all-to-all-start = ((f32[1,64,512]{2,0,1:T(1,128)}), f32[1,64,512]{2,0,1:T(1,128)S(1)}, u32[]{:S(2)}, u32[]{:S(2)}) async-start(f32[1,64,512]{2,0,1:T(1,128)} %copy.7), calls=%async_computation | async-start | bytes 262144 | tf_op jit(solution)/shard_map/all_to_all | solution.py:38
Sparse Core Ops, SparseCore 0:
  38.7 24.6 all-gather.2
where the time goes:
time: 87.2 us; the launch traced here: 86.9 us
  blocking collectives  37.6 us (43%)
  waiting for transfers between devices  21.2 us (24%)
  between operations  13.4 us (15%)
  matrix products  9.09 us (10%)
  starting transfers between devices  3.37 us (4%)
  local copies, waits for them, and re-layouts  1.52 us (2%)
    all_gather x1, waiting for transfers between devices, per_device(): lax.all_gather(prepared, 'own', axis=1, tiled=True)  15.8 us
    all_gather x1, blocking collectives, per_device(): lax.all_gather(right_factor, 'qry', axis=1, tiled=True)  15.2 us
    all_gather x1, blocking collectives, per_device(): lax.all_gather(left_factor, 'qry', axis=1, tiled=True)  13.3 us
    all_gather x1, blocking collectives, per_device(): all_lengths = lax.all_gather(lengths, 'own', axis=0, tiled=True)  9.04 us
    dot_general x1, matrix products, per_device(): jnp.einsum('srw,cw->src', lax.all_gather(prepared, 'own', axis=1, tiled=T...  6.37 us
    all_to_all x1, waiting for transfers between devices, per_device(): lax.all_to_all(tiles, 'own', split_axis=1, concat_axis=2, tiled=True)  5.43 us
    all_to_all x1, starting transfers between devices, per_device(): lax.all_to_all(tiles, 'own', split_axis=1, concat_axis=2, tiled=True)  3.37 us
  transfers between devices with their start and end apart: 2, of which 2 were waited for; matrix products, arithmetic and copies ran while one was open for 0% of the time, Pallas kernels for 0%

commit v1 on v0

v1 whole, which is shorter than its diff:
```python
import jax
import jax.numpy as jnp
from jax import lax
from jax.experimental import pallas as pl
from jax.experimental.pallas import tpu as pltpu
from jax.sharding import PartitionSpec as P

LANES = 128
CORES = 2
VMEM = pl.BlockSpec(memory_space=pltpu.VMEM)
HBM = pl.BlockSpec(memory_space=pltpu.HBM)
F32 = jnp.float32
BF16 = jnp.bfloat16


def precondition(rows, id_values, left_full, right_full):
    blocks = left_full.shape[0]
    order_a = left_full.shape[1]
    order_b = right_full.shape[1]
    labels = jnp.arange(blocks)
    onehot = (id_values[:, :, None] == labels[None, None, :]).astype(F32)
    left_rows = jnp.einsum("srk,kac->srac", onehot, left_full.astype(F32), precision=lax.Precision.HIGHEST)
    right_rows = jnp.einsum("srk,kde->srde", onehot, right_full.astype(F32), precision=lax.Precision.HIGHEST)
    matrix = rows.reshape(rows.shape[0], rows.shape[1], order_a, order_b).astype(F32)
    inner = jnp.einsum("srac,srcd->srad", left_rows, matrix, precision=lax.Precision.HIGHEST)
    outer = jnp.einsum("srad,srde->srae", inner, right_rows, precision=lax.Precision.HIGHEST)
    return outer.reshape(rows.shape).astype(BF16)


def per_device_gathered(queries, block_ids, left_factor, right_factor, clip_grads, lengths):
    left_full = lax.all_gather(left_factor, "qry", axis=1, tiled=True)
    right_full = lax.all_gather(right_factor, "qry", axis=1, tiled=True)
    prepared = precondition(queries, block_ids, left_full, right_full)
    tiles = jnp.einsum(
        "srw,cw->src",
        lax.all_gather(prepared, "own", axis=1, tiled=True),
        clip_grads,
        preferred_element_type=F32,
    )
    factor = lax.rsqrt(F32(queries.shape[2]) * lengths.astype(F32))
    return lax.all_to_all(tiles * factor[None, None, :], "own", split_axis=1, concat_axis=2, tiled=True)


def pack_kernel(q_hbm, ids_ref, left_ref, right_ref, row_ref, fac_ref, sem):
    width = q_hbm.shape[1]
    cut = left_ref.shape[1]
    copy = pltpu.make_async_copy(q_hbm, row_ref.at[:, :width], sem)
    copy.start()
    row_ref[:, width:] = jnp.broadcast_to(ids_ref[...].astype(F32), (row_ref.shape[0], LANES)).astype(BF16)
    fac_ref[0, :, :cut, : left_ref.shape[2]] = left_ref[...]
    fac_ref[0, :, :cut, left_ref.shape[2] :] = jnp.zeros(
        (left_ref.shape[0], cut, LANES - left_ref.shape[2]), BF16
    )
    fac_ref[0, :, cut:, :] = right_ref[...]
    copy.wait()


def pack(queries, block_ids, left, right):
    rows, width = queries.shape
    blocks, cut = left.shape[:2]
    depth = cut + right.shape[1]
    return pl.pallas_call(
        pack_kernel,
        out_shape=(
            jax.ShapeDtypeStruct((rows, width + LANES), BF16),
            jax.ShapeDtypeStruct((1, blocks, depth, LANES), BF16),
        ),
        in_specs=[HBM, VMEM, VMEM, VMEM],
        out_specs=(VMEM, VMEM),
        scratch_shapes=[pltpu.SemaphoreType.DMA(())],
        compiler_params=pltpu.CompilerParams(vmem_limit_bytes=8 << 20),
    )(queries, block_ids.reshape(rows, 1), left, right)


def score_kernel(order_a, order_b, steps, *refs):
    nslots = 8
    slots = refs[:nslots]
    fac_refs = refs[nslots : nslots + steps + 1]
    clips_ref, len_ref, mine_ref, other_ref, left_s, right_s, in_s, out_s, prep_s = refs[nslots + steps + 1 :]
    rows = slots[0].shape[0]
    blocks = fac_refs[0].shape[1]
    planes = 2**steps
    cut_a, cut_b = order_a // planes, order_b // planes
    plane = lax.axis_index("qry")
    for m in range(planes):
        step = m.bit_length()
        piece = fac_refs[step][m - (1 << (step - 1)) if step else 0]
        at = lax.bitwise_xor(plane, m)
        for k in range(blocks):
            left_s[pl.ds(pl.multiple_of(k * order_a + at * cut_a, 16), cut_a), :] = piece[k, :cut_a, :order_a]
            for half in range(2):
                right_s[
                    pl.ds(pl.multiple_of(half * order_b + at * cut_b, 16), cut_b),
                    k * order_b : (k + 1) * order_b,
                ] = piece[k, cut_a:, :]
    left_all = left_s[...]
    right_all = right_s[...]
    width = order_a * order_b
    pair = 2 * rows
    for group in range(nslots // 2):
        for half in range(2):
            ref = slots[2 * group + half]
            for a in range(order_a):
                in_s[a * pair + half * rows : a * pair + half * rows + rows, :] = ref[
                    :, a * order_b : (a + 1) * order_b
                ].astype(F32)
        for n in range(0, pair, 2):
            ref = slots[2 * group + n // rows]
            x = jnp.concatenate(
                [in_s[pl.ds(n + j, order_a, stride=pair), :].astype(BF16) for j in range(2)], axis=1
            )
            inner = jnp.dot(left_all, x, preferred_element_type=F32)
            split = []
            ids = []
            for j in range(2):
                label = ref[(n + j) % rows : (n + j) % rows + 1, width:].astype(F32)
                ids.append(label)
                one = inner[:order_a, j * order_b : (j + 1) * order_b]
                for k in range(1, blocks):
                    one = jnp.where(
                        label > k - 0.5,
                        inner[k * order_a : (k + 1) * order_a, j * order_b : (j + 1) * order_b],
                        one,
                    )
                high = one.astype(BF16)
                low = (one - high.astype(F32)).astype(BF16)
                split.append(jnp.concatenate([high, low], axis=1))
            outer = jnp.dot(jnp.concatenate(split, axis=0), right_all, preferred_element_type=F32)
            for j in range(2):
                one = outer[j * order_a : (j + 1) * order_a, :order_b]
                for k in range(1, blocks):
                    one = jnp.where(
                        ids[j] > k - 0.5,
                        outer[j * order_a : (j + 1) * order_a, k * order_b : (k + 1) * order_b],
                        one,
                    )
                out_s[pl.ds(n + j, order_a, stride=pair), :] = one
        for a in range(order_a):
            prep_s[group * pair : (group + 1) * pair, a * order_b : (a + 1) * order_b] = out_s[
                a * pair : (a + 1) * pair, :
            ].astype(BF16)
    raw = lax.dot_general(
        clips_ref[...], prep_s[...], (((1,), (1,)), ((), ())), preferred_element_type=F32
    )
    factor = lax.rsqrt(F32(width) * len_ref[...].astype(F32))
    scores = raw.T * factor
    for m in range(nslots // 2):
        mine_ref[m] = scores[m * rows : (m + 1) * rows]
        other_ref[m] = scores[(m + nslots // 2) * rows : (m + nslots // 2 + 1) * rows]


def score(slots, factors, clip_grads, lengths, order_a, order_b):
    rows = slots[0].shape[0]
    clips, width = clip_grads.shape
    blocks = factors[0].shape[1]
    steps = len(factors) - 1
    half = len(slots) // 2
    kernel = lambda *refs: score_kernel(order_a, order_b, steps, *refs)
    return pl.pallas_call(
        kernel,
        out_shape=(jax.ShapeDtypeStruct((half, rows, clips), F32),) * 2,
        in_specs=[VMEM] * (len(slots) + len(factors) + 2),
        out_specs=(VMEM, VMEM),
        scratch_shapes=[
            pltpu.VMEM((blocks * order_a, order_a), BF16),
            pltpu.VMEM((2 * order_b, blocks * order_b), BF16),
            pltpu.VMEM((order_a * 2 * rows, order_b), F32),
            pltpu.VMEM((order_a * 2 * rows, order_b), F32),
            pltpu.VMEM((len(slots) * rows, width), BF16),
        ],
        compiler_params=pltpu.CompilerParams(vmem_limit_bytes=24 << 20),
        cost_estimate=pl.CostEstimate(
            flops=2 * len(slots) * rows * width * (clips + 1000), bytes_accessed=clips * width * 2, transcendentals=0
        ),
    )(*slots, *factors, clip_grads, lengths.reshape(1, clips))


def place_kernel(mine_ref, got_ref, a_ref, b_ref, d_ref, out_ref, sems):
    clips = mine_ref.shape[2]
    index = lax.axis_index("own")
    core = lax.rem(index, CORES)
    chip = lax.div(index, CORES)
    copies = []

    def put(source, chip_of, core_of, sem):
        at = pl.multiple_of((chip_of * CORES + core_of) * clips, clips)
        copy = pltpu.make_async_copy(source, out_ref.at[:, pl.ds(at, clips)], sem)
        copy.start()
        copies.append(copy)

    put(mine_ref.at[0], chip, core, sems.at[0])
    put(got_ref.at[0], chip, 1 - core, sems.at[1])
    for j, (ref, flip) in enumerate(((a_ref, 1 + core), (b_ref, 2 - core), (d_ref, 3))):
        there = lax.bitwise_xor(chip, flip)
        put(ref.at[0], there, core, sems.at[2 + 2 * j])
        put(ref.at[1], there, 1 - core, sems.at[3 + 2 * j])
    for copy in copies:
        copy.wait()


def place(mine, got, a, b, d):
    _, rows, clips = mine.shape
    return pl.pallas_call(
        place_kernel,
        out_shape=jax.ShapeDtypeStruct((rows, 8 * clips), F32),
        in_specs=[VMEM] * 5,
        out_specs=HBM,
        scratch_shapes=[pltpu.SemaphoreType.DMA((8,))],
        compiler_params=pltpu.CompilerParams(vmem_limit_bytes=8 << 20),
    )(mine, got, a, b, d)


def per_device_exchanged(planes, queries, block_ids, left_factor, right_factor, clip_grads, lengths):
    size = 4 * CORES

    def move(x, to):
        return lax.ppermute(x, "own", [(i, to(i // CORES, i % CORES)) for i in range(size)])

    def sibling(x):
        return move(x, lambda chip, core: chip * CORES + 1 - core)

    def across(x, flips):
        return move(x, lambda chip, core: (chip ^ flips[core]) * CORES + core)

    flips_a, flips_b, flips_d = (1, 2), (2, 1), (3, 3)
    row, fac = pack(queries[0], block_ids[0], left_factor, right_factor)
    slot_d = across(row, flips_d)
    slot_a = across(row, flips_a)
    slot_b = across(row, flips_b)
    factors = [fac]
    held = fac
    step = 1
    while step < planes:
        got = lax.ppermute(held, "qry", [(i, i ^ step) for i in range(planes)])
        factors.append(got)
        if step * 2 < planes:
            held = jnp.concatenate([held, got])
        step *= 2
    own = [row, slot_a, slot_b, slot_d]
    slots = own + [sibling(x) for x in own]
    order_a, order_b = left_factor.shape[2], right_factor.shape[2]
    mine, other = score(slots, factors, clip_grads, lengths, order_a, order_b)
    got = sibling(other)
    back = [
        across(jnp.stack([mine[j], got[j]]), flips) for j, flips in ((1, flips_a), (2, flips_b), (3, flips_d))
    ]
    return place(mine, got, *back)[None]


def solution(mesh):
    owners, planes = mesh.shape["own"], mesh.shape["qry"]

    def per_device(queries, block_ids, left_factor, right_factor, clip_grads, lengths):
        whole_tiles = left_factor.shape[1] % 16 == 0 and right_factor.shape[1] % 16 == 0
        if owners == 4 * CORES and planes & (planes - 1) == 0 and whole_tiles:
            return per_device_exchanged(
                planes, queries, block_ids, left_factor, right_factor, clip_grads, lengths
            )
        return per_device_gathered(queries, block_ids, left_factor, right_factor, clip_grads, lengths)

    in_specs = (
        P("qry", "own", None),
        P("qry", "own"),
        P(None, "qry", None),
        P(None, "qry", None),
        P("own", None),
        P("own"),
    )
    out_specs = P("qry", "own", None)
    return jax.shard_map(
        per_device, mesh=mesh, in_specs=in_specs, out_specs=out_specs, check_vma=False
    )
```

time: 87.2 us -> 39.3 us (0.45)
  blocking collectives: 37.6 us -> 0 us
  between operations: 13.4 us -> 0.08 us
  starting transfers between devices: 3.37 us -> 13.6 us
  matrix products: 9.09 us -> 0 us
  waiting for transfers between devices: 21.2 us -> 12.7 us
  local copies, waits for them, and re-layouts: 1.52 us -> 7.11 us
  Pallas kernels: 0 us -> 5.41 us
    all_gather x3 -> x0, blocking collectives: 37.6 us -> none  [the longest x1 15.2 us: per_device(): lax.all_gather(right_factor, 'qry', axis=1, tiled=True)]
    all_gather x1 -> x0, waiting for transfers between devices: 15.8 us -> none  [per_device(): lax.all_gather(prepared, 'own', axis=1, tiled=True)]
    ppermute x0 -> x13, starting transfers between devices: none -> 13.6 us  [the longest x11 8.78 us: move(): lax.ppermute(x, 'own', [(i, to(i // CORES, i % CORES)) for i in range(siz...]
    ppermute x0 -> x13, waiting for transfers between devices: none -> 12.7 us  [the longest x11 10 us: move(): lax.ppermute(x, 'own', [(i, to(i // CORES, i % CORES)) for i in range(siz...]
    dot_general x5 -> x0, matrix products: 9.09 us -> none  [the longest x1 6.37 us: per_device(): jnp.einsum('srw,cw->src', lax.all_gather(prepared, 'own', axis=1, tiled=T...]
    unnamed x2 -> x10, local copies, waits for them, and re-layouts: 0.01 us -> 6.37 us
    all_to_all x1 -> x0, waiting for transfers between devices: 5.43 us -> none  [per_device(): lax.all_to_all(tiles, 'own', split_axis=1, concat_axis=2, tiled=True)]
    pallas_call x0 -> x3, Pallas kernels: none -> 5.41 us  [the longest x1 4.48 us: score(): pl.pallas_call(kernel, out_shape=(jax.ShapeDtypeStruct((half, rows, clips...]
  transfers between devices with their start and end apart: 2 -> 13, of which waited for: 2 -> 8; matrix products, arithmetic and copies ran while one was open for 0% -> 0% of each run, Pallas kernels for 0% -> 0%
where the time goes in v1:
time: 39.3 us; the launch traced here: 39 us
  starting transfers between devices  13.6 us (35%)
  waiting for transfers between devices  12.7 us (32%)
  local copies, waits for them, and re-layouts  7.11 us (18%)
  Pallas kernels  5.41 us (14%)
    ppermute x11, waiting for transfers between devices, move(): lax.ppermute(x, 'own', [(i, to(i // CORES, i % CORES)) for i in range(siz...  10 us
    ppermute x11, starting transfers between devices, move(): lax.ppermute(x, 'own', [(i, to(i // CORES, i % CORES)) for i in range(siz...  8.78 us
    unnamed x10, local copies, waits for them, and re-layouts  6.37 us
    ppermute x2, starting transfers between devices, per_device_exchanged(): got = lax.ppermute(held, 'qry', [(i, i ^ step) for i in range(planes)])  4.82 us
    pallas_call x1, Pallas kernels, score(): pl.pallas_call(kernel, out_shape=(jax.ShapeDtypeStruct((half, rows, clips...  4.48 us
    ppermute x2, waiting for transfers between devices, per_device_exchanged(): got = lax.ppermute(held, 'qry', [(i, i ^ step) for i in range(planes)])  2.74 us
  transfers between devices with their start and end apart: 13, of which 8 were waited for; matrix products, arithmetic and copies ran while one was open for 0% of the time, Pallas kernels for 0%

profile of v1, /device:TPU:0, one launch (start us, length us, event | category | flops | bytes accessed | tf_op | source)
XLA Modules:
  0.0 39.0 jit_solution(5895070259471079077)
XLA Ops:
  0.0 0.7 %copy.7.ids_ref = s32[8,1]{1,0:T(8,128)S(1)} copy(s32[8,1]{0,1:T(1,128)} %bitcast.6) | data formatting | bytes 64 | tf_op jit(solution)/shard_map/reshape;squeeze | solution.py:72
  0.7 0.9 %copy-done.1 = bf16[1,8,8192]{2,1,0:T(8,128)(2,1)S(1)} copy-done((bf16[1,8,8192]{2,1,0:T(8,128)(2,1)S(1)}, bf16[1,8,8192]{2,1,0:T(8,128)(2,1)}, u32[]{:S(2)}) %copy-start.1) | copy-done | bytes 131096
  1.6 0.7 %copy-done.2 = bf16[2,32,128]{2,1,0:T(8,128)(2,1)S(1)} copy-done((bf16[2,32,128]{2,1,0:T(8,128)(2,1)S(1)}, bf16[2,32,128]{2,1,0:T(8,128)(2,1)}, u32[]{:S(2)}) %copy-start.2) | copy-done | bytes 16408
  2.4 0.7 %copy-done.3 = bf16[2,16,64]{2,1,0:T(8,128)(2,1)S(1)} copy-done((bf16[2,16,64]{2,1,0:T(8,128)(2,1)S(1)}, bf16[2,16,64]{2,1,0:T(8,128)(2,1)}, u32[]{:S(2)}) %copy-start.3) | copy-done | bytes 4120
  3.0 0.2 shard_map.64
  3.3 4.0 %collective-permute-start.2 = (bf16[8,8320]{1,0:T(8,128)(2,1)S(1)}, bf16[8,8320]{1,0:T(8,128)(2,1)S(1)}, u32[]{:S(2)}, u32[]{:S(2)}) collective-permute-start(bf16[8,8320]{1,0:T(8,128)(2,1)S(1)} %get-tuple-element.9.refs_0_), channel_id=1, source_target_pairs={{0,24},{4,28},{8,16},{12,20},{16,8},{20,12},{24,0},{28,4},{1,25},{... | collective-permute-start | bytes 399368 | tf_op jit(solution)/shard_map/ppermute | solution.py:217
  7.2 0.5 %collective-permute-start.1 = (bf16[8,8320]{1,0:T(8,128)(2,1)S(1)}, bf16[8,8320]{1,0:T(8,128)(2,1)S(1)}, u32[]{:S(2)}, u32[]{:S(2)}) collective-permute-start(bf16[8,8320]{1,0:T(8,128)(2,1)S(1)} %get-tuple-element.9.refs_0_), channel_id=1, source_target_pairs={{0,16},{4,12},{8,24},{12,4},{16,0},{20,28},{24,8},{28,20},{1,17},{... | collective-permute-start | bytes 399368 | tf_op jit(solution)/shard_map/ppermute | solution.py:217
  7.9 2.0 %collective-permute-start.7 = (bf16[1,2,48,128]{3,2,1,0:T(8,128)(2,1)S(1)}, bf16[1,2,48,128]{3,2,1,0:T(8,128)(2,1)S(1)}, u32[]{:S(2)}, u32[]{:S(2)}) collective-permute-start(bf16[1,2,48,128]{3,2,1,0:T(8,128)(2,1)S(1)} %get-tuple-element.10.refs_8_), channel_id=1, source_target_pairs={{0,1},{1,0},{2,3},{3,2},{4,5},{5,4},{6,7},{7,6},{8,9},{9,8},{10,11... | collective-permute-start | bytes 73736 | tf_op jit(solution)/shard_map/ppermute | solution.py:234
  9.9 1.7 %collective-permute-done.2.refs_3_ = bf16[8,8320]{1,0:T(8,128)(2,1)S(1)} collective-permute-done((bf16[8,8320]{1,0:T(8,128)(2,1)S(1)}, bf16[8,8320]{1,0:T(8,128)(2,1)S(1)}, u32[]{:S(2)}, u32[]{:S(2)}) %collective-permute-start.2) | collective-permute-done | bytes 133152 | tf_op jit(solution)/shard_map/ppermute | solution.py:217
  11.6 2.0 %collective-permute-done.1.refs_2_ = bf16[8,8320]{1,0:T(8,128)(2,1)S(1)} collective-permute-done((bf16[8,8320]{1,0:T(8,128)(2,1)S(1)}, bf16[8,8320]{1,0:T(8,128)(2,1)S(1)}, u32[]{:S(2)}, u32[]{:S(2)}) %collective-permute-start.1) | collective-permute-done | bytes 133152 | tf_op jit(solution)/shard_map/ppermute | solution.py:217
  13.6 0.2 collective-permute-done.refs_1_
  13.9 0.3 collective-permute-start.4
  14.2 2.8 %collective-permute-start.8 = (bf16[2,2,48,128]{3,2,1,0:T(8,128)(2,1)S(1)}, bf16[2,2,48,128]{3,2,1,0:T(8,128)(2,1)S(1)}, u32[]{:S(2)}, u32[]{:S(2)}) collective-permute-start(bf16[2,2,48,128]{3,2,1,0:T(8,128)(2,1)S(1)} %pad_maximum_fusion), channel_id=1, source_target_pairs={{0,2},{1,3},{2,0},{3,1},{4,6},{5,7},{6,4},{7,5},{8,10},{9,11},{10,... | collective-permute-start | bytes 147464 | tf_op jit(solution)/shard_map/ppermute | solution.py:234
  17.0 2.7 %collective-permute-done.8.refs_10_ = bf16[2,2,48,128]{3,2,1,0:T(8,128)(2,1)S(1)} collective-permute-done((bf16[2,2,48,128]{3,2,1,0:T(8,128)(2,1)S(1)}, bf16[2,2,48,128]{3,2,1,0:T(8,128)(2,1)S(1)}, u32[]{:S(2)}, u32[]{:S(2)}) %collective-permute-start.8) | collective-permute-done | bytes 49184 | tf_op jit(solution)/shard_map/ppermute | solution.py:234
  19.8 3.4 %copy-done = bf16[512,8192]{1,0:T(8,128)(2,1)S(1)} copy-done((bf16[512,8192]{1,0:T(8,128)(2,1)S(1)}, bf16[512,8192]{1,0:T(8,128)(2,1)}, u32[]{:S(2)}) %copy-start) | copy-done | bytes 8388632
  23.1 0.7 %copy-done.4 = s32[512]{0:T(512)S(1)} copy-done((s32[512]{0:T(512)S(1)}, s32[512]{0:T(512)}, u32[]{:S(2)}) %copy-start.4) | copy-done | bytes 2072
  23.8 4.5 %shard_map.65 = (f32[4,8,512]{2,1,0:T(8,128)S(1)}, f32[4,8,512]{2,1,0:T(8,128)S(1)}) custom-call(bf16[8,8320]{1,0:T(8,128)(2,1)S(1)} %get-tuple-element.9.refs_0_, bf16[8,8320]{1,0:T(8,128)(2,1)S(1)} %collective-permute-done.refs_1_, bf16[8,8320]{1,0:T(8,128)(2,1)S(1)} %collective-permute-done.1.refs_2_, bf16[8,8320]{1,0:T(8,128)(2,1)S(1)} %collective-permute-done.2.refs_3_, ...), custom_call_target="tpu_custom_call" | custom-call | flops 1585446912 | bytes 8388608 | tf_op jit(solution)/shard_map/pallas_call | solution.py:159
  28.4 1.2 %collective-permute-done.9.got_ref = f32[4,8,512]{2,1,0:T(8,128)S(1)} collective-permute-done((f32[4,8,512]{2,1,0:T(8,128)S(1)}, f32[4,8,512]{2,1,0:T(8,128)S(1)}, u32[]{:S(2)}, u32[]{:S(2)}) %collective-permute-start.9) | collective-permute-done | bytes 65568 | tf_op jit(solution)/shard_map/ppermute | solution.py:217
  29.6 2.3 %collective-permute-start.10 = (f32[2,8,512]{2,1,0:T(8,128)S(1)}, f32[2,8,512]{2,1,0:T(8,128)S(1)}, u32[]{:S(2)}, u32[]{:S(2)}) collective-permute-start(f32[2,8,512]{2,1,0:T(8,128)S(1)} %pad_maximum_fusion.1), channel_id=1, source_target_pairs={{0,8},{4,20},{8,0},{12,28},{16,24},{20,4},{24,16},{28,12},{1,9},{5... | collective-permute-start | bytes 98312 | tf_op jit(solution)/shard_map/ppermute | solution.py:217
  31.9 1.5 %collective-permute-start.11 = (f32[2,8,512]{2,1,0:T(8,128)S(1)}, f32[2,8,512]{2,1,0:T(8,128)S(1)}, u32[]{:S(2)}, u32[]{:S(2)}) collective-permute-start(f32[2,8,512]{2,1,0:T(8,128)S(1)} %pad_maximum_fusion.2), channel_id=1, source_target_pairs={{0,16},{4,12},{8,24},{12,4},{16,0},{20,28},{24,8},{28,20},{1,17},{... | collective-permute-start | bytes 98312 | tf_op jit(solution)/shard_map/ppermute | solution.py:217
  33.5 0.3 collective-permute-done.10.a_ref
  33.8 2.0 %collective-permute-done.11.b_ref = f32[2,8,512]{2,1,0:T(8,128)S(1)} collective-permute-done((f32[2,8,512]{2,1,0:T(8,128)S(1)}, f32[2,8,512]{2,1,0:T(8,128)S(1)}, u32[]{:S(2)}, u32[]{:S(2)}) %collective-permute-start.11) | collective-permute-done | bytes 32800 | tf_op jit(solution)/shard_map/ppermute | solution.py:217
  35.8 2.4 %collective-permute-done.12.d_ref = f32[2,8,512]{2,1,0:T(8,128)S(1)} collective-permute-done((f32[2,8,512]{2,1,0:T(8,128)S(1)}, f32[2,8,512]{2,1,0:T(8,128)S(1)}, u32[]{:S(2)}, u32[]{:S(2)}) %collective-permute-start.12) | collective-permute-done | bytes 32800 | tf_op jit(solution)/shard_map/ppermute | solution.py:217
  38.2 0.7 %shard_map.66 = f32[8,4096]{1,0:T(8,128)} custom-call(f32[4,8,512]{2,1,0:T(8,128)S(1)} %get-tuple-element.11.mine_ref, f32[4,8,512]{2,1,0:T(8,128)S(1)} %collective-permute-done.9.got_ref, f32[2,8,512]{2,1,0:T(8,128)S(1)} %collective-permute-done.10.a_ref, f32[2,8,512]{2,1,0:T(8,128)S(1)} %collective-permute-done.11.b_ref, ...), custom_call_target="tpu_custom_call" | custom-call | tf_op jit(solution)/shard_map/pallas_call | solution.py:203
  (22 shorter events, 0.3 us)
Async XLA Ops:
  0.7 0.9 %copy-start.1 = (bf16[1,8,8192]{2,1,0:T(8,128)(2,1)S(1)}, bf16[1,8,8192]{2,1,0:T(8,128)(2,1)}, u32[]{:S(2)}) copy-start(bf16[1,8,8192]{2,1,0:T(8,128)(2,1)} %param.6) | copy-start | bytes 393220
  1.6 0.7 %copy-start.2 = (bf16[2,32,128]{2,1,0:T(8,128)(2,1)S(1)}, bf16[2,32,128]{2,1,0:T(8,128)(2,1)}, u32[]{:S(2)}) copy-start(bf16[2,32,128]{2,1,0:T(8,128)(2,1)} %right_ref.1) | copy-start | bytes 49156
  2.4 0.7 %copy-start.3 = (bf16[2,16,64]{2,1,0:T(8,128)(2,1)S(1)}, bf16[2,16,64]{2,1,0:T(8,128)(2,1)}, u32[]{:S(2)}) copy-start(bf16[2,16,64]{2,1,0:T(8,128)(2,1)} %left_ref.1) | copy-start | bytes 12292
  3.3 8.3 %collective-permute-start.2 = (bf16[8,8320]{1,0:T(8,128)(2,1)S(1)}, bf16[8,8320]{1,0:T(8,128)(2,1)S(1)}, u32[]{:S(2)}, u32[]{:S(2)}) collective-permute-start(bf16[8,8320]{1,0:T(8,128)(2,1)S(1)} %get-tuple-element.9.refs_0_), channel_id=1, source_target_pairs={{0,24},{4,28},{8,16},{12,20},{16,8},{20,12},{24,0},{28,4},{1,25},{... | collective-permute-start | bytes 399368 | tf_op jit(solution)/shard_map/ppermute | solution.py:217
  7.2 6.4 %collective-permute-start.1 = (bf16[8,8320]{1,0:T(8,128)(2,1)S(1)}, bf16[8,8320]{1,0:T(8,128)(2,1)S(1)}, u32[]{:S(2)}, u32[]{:S(2)}) collective-permute-start(bf16[8,8320]{1,0:T(8,128)(2,1)S(1)} %get-tuple-element.9.refs_0_), channel_id=1, source_target_pairs={{0,16},{4,12},{8,24},{12,4},{16,0},{20,28},{24,8},{28,20},{1,17},{... | collective-permute-start | bytes 399368 | tf_op jit(solution)/shard_map/ppermute | solution.py:217
  7.7 6.1 %collective-permute-start = (bf16[8,8320]{1,0:T(8,128)(2,1)S(1)}, bf16[8,8320]{1,0:T(8,128)(2,1)S(1)}, u32[]{:S(2)}, u32[]{:S(2)}) collective-permute-start(bf16[8,8320]{1,0:T(8,128)(2,1)S(1)} %get-tuple-element.9.refs_0_), channel_id=1, source_target_pairs={{0,8},{4,20},{8,0},{12,28},{16,24},{20,4},{24,16},{28,12},{1,9},{5... | collective-permute-start | bytes 399368 | tf_op jit(solution)/shard_map/ppermute | solution.py:217
  7.9 6.3 %collective-permute-start.7 = (bf16[1,2,48,128]{3,2,1,0:T(8,128)(2,1)S(1)}, bf16[1,2,48,128]{3,2,1,0:T(8,128)(2,1)S(1)}, u32[]{:S(2)}, u32[]{:S(2)}) collective-permute-start(bf16[1,2,48,128]{3,2,1,0:T(8,128)(2,1)S(1)} %get-tuple-element.10.refs_8_), channel_id=1, source_target_pairs={{0,1},{1,0},{2,3},{3,2},{4,5},{5,4},{6,7},{7,6},{8,9},{9,8},{10,11... | collective-permute-start | bytes 73736 | tf_op jit(solution)/shard_map/ppermute | solution.py:234
  9.9 9.9 %collective-permute-start.3 = (bf16[8,8320]{1,0:T(8,128)(2,1)S(1)}, bf16[8,8320]{1,0:T(8,128)(2,1)S(1)}, u32[]{:S(2)}, u32[]{:S(2)}) collective-permute-start(bf16[8,8320]{1,0:T(8,128)(2,1)S(1)} %get-tuple-element.9.refs_0_), channel_id=1, source_target_pairs={{0,4},{4,0},{8,12},{12,8},{16,20},{20,16},{24,28},{28,24},{1,5},{5... | collective-permute-start | bytes 399368 | tf_op jit(solution)/shard_map/ppermute | solution.py:217
  11.6 8.1 %collective-permute-start.6 = (bf16[8,8320]{1,0:T(8,128)(2,1)S(1)}, bf16[8,8320]{1,0:T(8,128)(2,1)S(1)}, u32[]{:S(2)}, u32[]{:S(2)}) collective-permute-start(bf16[8,8320]{1,0:T(8,128)(2,1)S(1)} %collective-permute-done.2.refs_3_), channel_id=1, source_target_pairs={{0,4},{4,0},{8,12},{12,8},{16,20},{20,16},{24,28},{28,24},{1,5},{5... | collective-permute-start | bytes 399368 | tf_op jit(solution)/shard_map/ppermute | solution.py:217
  13.6 6.1 %collective-permute-start.5 = (bf16[8,8320]{1,0:T(8,128)(2,1)S(1)}, bf16[8,8320]{1,0:T(8,128)(2,1)S(1)}, u32[]{:S(2)}, u32[]{:S(2)}) collective-permute-start(bf16[8,8320]{1,0:T(8,128)(2,1)S(1)} %collective-permute-done.1.refs_2_), channel_id=1, source_target_pairs={{0,4},{4,0},{8,12},{12,8},{16,20},{20,16},{24,28},{28,24},{1,5},{5... | collective-permute-start | bytes 399368 | tf_op jit(solution)/shard_map/ppermute | solution.py:217
  13.9 5.9 %collective-permute-start.4 = (bf16[8,8320]{1,0:T(8,128)(2,1)S(1)}, bf16[8,8320]{1,0:T(8,128)(2,1)S(1)}, u32[]{:S(2)}, u32[]{:S(2)}) collective-permute-start(bf16[8,8320]{1,0:T(8,128)(2,1)S(1)} %collective-permute-done.refs_1_), channel_id=1, source_target_pairs={{0,4},{4,0},{8,12},{12,8},{16,20},{20,16},{24,28},{28,24},{1,5},{5... | collective-permute-start | bytes 399368 | tf_op jit(solution)/shard_map/ppermute | solution.py:217
  14.2 5.6 %collective-permute-start.8 = (bf16[2,2,48,128]{3,2,1,0:T(8,128)(2,1)S(1)}, bf16[2,2,48,128]{3,2,1,0:T(8,128)(2,1)S(1)}, u32[]{:S(2)}, u32[]{:S(2)}) collective-permute-start(bf16[2,2,48,128]{3,2,1,0:T(8,128)(2,1)S(1)} %pad_maximum_fusion), channel_id=1, source_target_pairs={{0,2},{1,3},{2,0},{3,1},{4,6},{5,7},{6,4},{7,5},{8,10},{9,11},{10,... | collective-permute-start | bytes 147464 | tf_op jit(solution)/shard_map/ppermute | solution.py:234
  19.8 3.4 %copy-start = (bf16[512,8192]{1,0:T(8,128)(2,1)S(1)}, bf16[512,8192]{1,0:T(8,128)(2,1)}, u32[]{:S(2)}) copy-start(bf16[512,8192]{1,0:T(8,128)(2,1)} %refs_11_.1) | copy-start | bytes 25165828
  23.1 0.7 %copy-start.4 = (s32[512]{0:T(512)S(1)}, s32[512]{0:T(512)}, u32[]{:S(2)}) copy-start(s32[512]{0:T(512)} %param.11) | copy-start | bytes 6148
  28.3 1.3 %collective-permute-start.9 = (f32[4,8,512]{2,1,0:T(8,128)S(1)}, f32[4,8,512]{2,1,0:T(8,128)S(1)}, u32[]{:S(2)}, u32[]{:S(2)}) collective-permute-start(f32[4,8,512]{2,1,0:T(8,128)S(1)} %get-tuple-element.12), channel_id=1, source_target_pairs={{0,4},{4,0},{8,12},{12,8},{16,20},{20,16},{24,28},{28,24},{1,5},{5... | collective-permute-start | bytes 196616 | tf_op jit(solution)/shard_map/ppermute | solution.py:217
  29.6 4.2 %collective-permute-start.10 = (f32[2,8,512]{2,1,0:T(8,128)S(1)}, f32[2,8,512]{2,1,0:T(8,128)S(1)}, u32[]{:S(2)}, u32[]{:S(2)}) collective-permute-start(f32[2,8,512]{2,1,0:T(8,128)S(1)} %pad_maximum_fusion.1), channel_id=1, source_target_pairs={{0,8},{4,20},{8,0},{12,28},{16,24},{20,4},{24,16},{28,12},{1,9},{5... | collective-permute-start | bytes 98312 | tf_op jit(solution)/shard_map/ppermute | solution.py:217
  31.9 3.9 %collective-permute-start.11 = (f32[2,8,512]{2,1,0:T(8,128)S(1)}, f32[2,8,512]{2,1,0:T(8,128)S(1)}, u32[]{:S(2)}, u32[]{:S(2)}) collective-permute-start(f32[2,8,512]{2,1,0:T(8,128)S(1)} %pad_maximum_fusion.2), channel_id=1, source_target_pairs={{0,16},{4,12},{8,24},{12,4},{16,0},{20,28},{24,8},{28,20},{1,17},{... | collective-permute-start | bytes 98312 | tf_op jit(solution)/shard_map/ppermute | solution.py:217
  33.4 4.8 %collective-permute-start.12 = (f32[2,8,512]{2,1,0:T(8,128)S(1)}, f32[2,8,512]{2,1,0:T(8,128)S(1)}, u32[]{:S(2)}, u32[]{:S(2)}) collective-permute-start(f32[2,8,512]{2,1,0:T(8,128)S(1)} %pad_maximum_fusion.3), channel_id=1, source_target_pairs={{0,24},{4,28},{8,16},{12,20},{16,8},{20,12},{24,0},{28,4},{1,25},{... | collective-permute-start | bytes 98312 | tf_op jit(solution)/shard_map/ppermute | solution.py:217

commit v2 on v1

--- a/solution.py
+++ b/solution.py
@@ -7,6 +7,8 @@
 
 LANES = 128
 CORES = 2
+HEAD = 256
+SOME_VMEM = 16 << 20
 VMEM = pl.BlockSpec(memory_space=pltpu.VMEM)
 HBM = pl.BlockSpec(memory_space=pltpu.HBM)
 F32 = jnp.float32
@@ -41,18 +43,29 @@
     return lax.all_to_all(tiles * factor[None, None, :], "own", split_axis=1, concat_axis=2, tiled=True)
 
 
-def pack_kernel(q_hbm, ids_ref, left_ref, right_ref, row_ref, fac_ref, sem):
-    width = q_hbm.shape[1]
-    cut = left_ref.shape[1]
-    copy = pltpu.make_async_copy(q_hbm, row_ref.at[:, :width], sem)
-    copy.start()
-    row_ref[:, width:] = jnp.broadcast_to(ids_ref[...].astype(F32), (row_ref.shape[0], LANES)).astype(BF16)
-    fac_ref[0, :, :cut, : left_ref.shape[2]] = left_ref[...]
-    fac_ref[0, :, :cut, left_ref.shape[2] :] = jnp.zeros(
-        (left_ref.shape[0], cut, LANES - left_ref.shape[2]), BF16
-    )
-    fac_ref[0, :, cut:, :] = right_ref[...]
-    copy.wait()
+def pack_kernel(q_hbm, ids_hbm, left_hbm, right_hbm, row_ref, fac_ref, ids_s, left_s, right_s, sems):
+    rows, width = q_hbm.shape
+    blocks, cut, order_a = left_s.shape
+    copies = [
+        pltpu.make_async_copy(left_hbm, left_s, sems.at[0]),
+        pltpu.make_async_copy(right_hbm, right_s, sems.at[1]),
+        pltpu.make_async_copy(ids_hbm, ids_s, sems.at[2]),
+        pltpu.make_async_copy(q_hbm, row_ref.at[:, :width], sems.at[3]),
+    ]
+    for copy in copies:
+        copy.start()
+    copies[2].wait()
+    square = (rows, rows)
+    diagonal = lax.broadcasted_iota(jnp.int32, square, 0) == lax.broadcasted_iota(jnp.int32, square, 1)
+    labels = jnp.where(diagonal, jnp.broadcast_to(ids_s[...].astype(F32), square), 0.0)
+    column = jnp.sum(labels, axis=1, keepdims=True)
+    row_ref[:, width:] = jnp.broadcast_to(column, (rows, LANES)).astype(BF16)
+    copies[0].wait()
+    copies[1].wait()
+    fac_ref[0, :, :cut, :order_a] = left_s[...]
+    fac_ref[0, :, :cut, order_a:] = jnp.zeros((blocks, cut, LANES - order_a), BF16)
+    fac_ref[0, :, cut:, :] = right_s[...]
+    copies[3].wait()
 
 
 def pack(queries, block_ids, left, right):
@@ -65,19 +78,21 @@
             jax.ShapeDtypeStruct((rows, width + LANES), BF16),
             jax.ShapeDtypeStruct((1, blocks, depth, LANES), BF16),
         ),
-        in_specs=[HBM, VMEM, VMEM, VMEM],
+        in_specs=[HBM] * 4,
         out_specs=(VMEM, VMEM),
-        scratch_shapes=[pltpu.SemaphoreType.DMA(())],
-        compiler_params=pltpu.CompilerParams(vmem_limit_bytes=8 << 20),
-    )(queries, block_ids.reshape(rows, 1), left, right)
-
-
-def score_kernel(order_a, order_b, steps, *refs):
-    nslots = 8
-    slots = refs[:nslots]
-    fac_refs = refs[nslots : nslots + steps + 1]
-    clips_ref, len_ref, mine_ref, other_ref, left_s, right_s, in_s, out_s, prep_s = refs[nslots + steps + 1 :]
-    rows = slots[0].shape[0]
+        scratch_shapes=[
+            pltpu.VMEM(block_ids.shape, block_ids.dtype),
+            pltpu.VMEM(left.shape, left.dtype),
+            pltpu.VMEM(right.shape, right.dtype),
+            pltpu.SemaphoreType.DMA((4,)),
+        ],
+        compiler_params=pltpu.CompilerParams(vmem_limit_bytes=SOME_VMEM),
+    )(*(pltpu.with_memory_space_constraint(x, pltpu.HBM) for x in (queries, block_ids, left, right)))
+
+
+def factor_kernel(order_a, order_b, steps, *refs):
+    fac_refs = refs[: steps + 1]
+    left_ref, right_ref = refs[steps + 1 :]
     blocks = fac_refs[0].shape[1]
     planes = 2**steps
     cut_a, cut_b = order_a // planes, order_b // planes
@@ -87,14 +102,39 @@
         piece = fac_refs[step][m - (1 << (step - 1)) if step else 0]
         at = lax.bitwise_xor(plane, m)
         for k in range(blocks):
-            left_s[pl.ds(pl.multiple_of(k * order_a + at * cut_a, 16), cut_a), :] = piece[k, :cut_a, :order_a]
+            left_ref[pl.ds(pl.multiple_of(k * order_a + at * cut_a, 16), cut_a), :] = piece[k, :cut_a, :order_a]
             for half in range(2):
-                right_s[
+                right_ref[
                     pl.ds(pl.multiple_of(half * order_b + at * cut_b, 16), cut_b),
                     k * order_b : (k + 1) * order_b,
                 ] = piece[k, cut_a:, :]
-    left_all = left_s[...]
-    right_all = right_s[...]
+
+
+def place_factors(factors, order_a, order_b):
+    blocks = factors[0].shape[1]
+    return pl.pallas_call(
+        lambda *refs: factor_kernel(order_a, order_b, len(factors) - 1, *refs),
+        out_shape=(
+            jax.ShapeDtypeStruct((blocks * order_a, order_a), BF16),
+            jax.ShapeDtypeStruct((2 * order_b, blocks * order_b), BF16),
+        ),
+        in_specs=[VMEM] * len(factors),
+        out_specs=(VMEM, VMEM),
+        compiler_params=pltpu.CompilerParams(vmem_limit_bytes=8 << 20),
+        cost_estimate=pl.CostEstimate(flops=10**10, bytes_accessed=10**6, transcendentals=0),
+    )(*factors)
+
+
+def score_kernel(order_a, order_b, *refs):
+    nslots = 8
+    slots = refs[:nslots]
+    (left_ref, right_ref, first_ref, len_ref, mine_ref, other_ref, in_s, out_s, prep_s) = refs[
+        nslots:
+    ]
+    rows = slots[0].shape[0]
+    blocks = left_ref.shape[0] // order_a
+    left_all = left_ref[...]
+    right_all = right_ref[...]
     width = order_a * order_b
     pair = 2 * rows
     for group in range(nslots // 2):
@@ -139,43 +179,46 @@
             prep_s[group * pair : (group + 1) * pair, a * order_b : (a + 1) * order_b] = out_s[
                 a * pair : (a + 1) * pair, :
             ].astype(BF16)
-    raw = lax.dot_general(
-        clips_ref[...], prep_s[...], (((1,), (1,)), ((), ())), preferred_element_type=F32
-    )
-    factor = lax.rsqrt(F32(width) * len_ref[...].astype(F32))
-    scores = raw.T * factor
-    for m in range(nslots // 2):
-        mine_ref[m] = scores[m * rows : (m + 1) * rows]
-        other_ref[m] = scores[(m + nslots // 2) * rows : (m + nslots // 2 + 1) * rows]
-
-
-def score(slots, factors, clip_grads, lengths, order_a, order_b):
+    def multiply(clips_ref, start):
+        count = clips_ref.shape[0]
+        raw = lax.dot_general(
+            clips_ref[...], prep_s[...], (((1,), (1,)), ((), ())), preferred_element_type=F32
+        )
+        factor = lax.rsqrt(F32(width) * len_ref[:, start : start + count].astype(F32))
+        scores = raw.T * factor
+        for m in range(nslots // 2):
+            mine_ref[m, :, start : start + count] = scores[m * rows : (m + 1) * rows]
+            other_ref[m, :, start : start + count] = scores[(m + nslots // 2) * rows : (m + nslots // 2 + 1) * rows]
+
+    multiply(first_ref, 0)
+
+
+def in_hbm(x):
+    return pltpu.with_memory_space_constraint(x, pltpu.HBM)
+
+
+def score(slots, left_all, right_all, clip_grads, lengths, order_a, order_b):
     rows = slots[0].shape[0]
     clips, width = clip_grads.shape
-    blocks = factors[0].shape[1]
-    steps = len(factors) - 1
     half = len(slots) // 2
-    kernel = lambda *refs: score_kernel(order_a, order_b, steps, *refs)
     return pl.pallas_call(
-        kernel,
+        lambda *refs: score_kernel(order_a, order_b, *refs),
         out_shape=(jax.ShapeDtypeStruct((half, rows, clips), F32),) * 2,
-        in_specs=[VMEM] * (len(slots) + len(factors) + 2),
+        in_specs=[VMEM] * (len(slots) + 4),
         out_specs=(VMEM, VMEM),
         scratch_shapes=[
-            pltpu.VMEM((blocks * order_a, order_a), BF16),
-            pltpu.VMEM((2 * order_b, blocks * order_b), BF16),
             pltpu.VMEM((order_a * 2 * rows, order_b), F32),
             pltpu.VMEM((order_a * 2 * rows, order_b), F32),
             pltpu.VMEM((len(slots) * rows, width), BF16),
         ],
-        compiler_params=pltpu.CompilerParams(vmem_limit_bytes=24 << 20),
+        compiler_params=pltpu.CompilerParams(vmem_limit_bytes=SOME_VMEM),
         cost_estimate=pl.CostEstimate(
             flops=2 * len(slots) * rows * width * (clips + 1000), bytes_accessed=clips * width * 2, transcendentals=0
         ),
-    )(*slots, *factors, clip_grads, lengths.reshape(1, clips))
-
-
-def place_kernel(mine_ref, got_ref, a_ref, b_ref, d_ref, out_ref, sems):
+    )(*slots, left_all, right_all, clip_grads, lengths.reshape(1, clips))
+
+
+def place_kernel(mine_ref, got_ref, d_ref, a_ref, b_ref, out_ref, sems):
     clips = mine_ref.shape[2]
     index = lax.axis_index("own")
     core = lax.rem(index, CORES)
@@ -198,7 +241,7 @@
         copy.wait()
 
 
-def place(mine, got, a, b, d):
+def place(mine, got, d, a, b):
     _, rows, clips = mine.shape
     return pl.pallas_call(
         place_kernel,
@@ -207,7 +250,7 @@
         out_specs=HBM,
         scratch_shapes=[pltpu.SemaphoreType.DMA((8,))],
         compiler_params=pltpu.CompilerParams(vmem_limit_bytes=8 << 20),
-    )(mine, got, a, b, d)
+    )(mine, got, d, a, b)
 
 
 def per_device_exchanged(planes, queries, block_ids, left_factor, right_factor, clip_grads, lengths):
@@ -223,7 +266,7 @@
         return move(x, lambda chip, core: (chip ^ flips[core]) * CORES + core)
 
     flips_a, flips_b, flips_d = (1, 2), (2, 1), (3, 3)
-    row, fac = pack(queries[0], block_ids[0], left_factor, right_factor)
+    row, fac = pack(queries[0], block_ids, left_factor, right_factor)
     slot_d = across(row, flips_d)
     slot_a = across(row, flips_a)
     slot_b = across(row, flips_b)
@@ -239,10 +282,11 @@
     own = [row, slot_a, slot_b, slot_d]
     slots = own + [sibling(x) for x in own]
     order_a, order_b = left_factor.shape[2], right_factor.shape[2]
-    mine, other = score(slots, factors, clip_grads, lengths, order_a, order_b)
+    left_all, right_all = place_factors(factors, order_a, order_b)
+    mine, other = score(slots, left_all, right_all, clip_grads, lengths, order_a, order_b)
     got = sibling(other)
     back = [
-        across(jnp.stack([mine[j], got[j]]), flips) for j, flips in ((1, flips_a), (2, flips_b), (3, flips_d))
+        across(jnp.stack([mine[j], got[j]]), flips) for j, flips in ((3, flips_d), (1, flips_a), (2, flips_b))
     ]
     return place(mine, got, *back)[None]
 

time: 39.3 us -> 28.1 us (0.72)
  local copies, waits for them, and re-layouts: 7.11 us -> 0.03 us
  waiting for transfers between devices: 12.7 us -> 7.87 us
  Pallas kernels: 5.41 us -> 6.24 us
    unnamed x10 -> x6, local copies, waits for them, and re-layouts: 6.37 us -> 0.02 us
    ppermute x2, waiting for transfers between devices: 2.74 us -> 0.01 us  [per_device_exchanged(): got = lax.ppermute(held, 'qry', [(i, i ^ step) for i in range(planes)])]
    ppermute x11, waiting for transfers between devices: 10 us -> 7.87 us  [move(): lax.ppermute(x, 'own', [(i, to(i // CORES, i % CORES)) for i in range(siz...]
    ppermute x2, starting transfers between devices: 4.82 us -> 5.74 us  [per_device_exchanged(): got = lax.ppermute(held, 'qry', [(i, i ^ step) for i in range(planes)])]
    ppermute x11, starting transfers between devices: 8.78 us -> 7.95 us  [move(): lax.ppermute(x, 'own', [(i, to(i // CORES, i % CORES)) for i in range(siz...]
    pallas_call x1, Pallas kernels: 0.21 us -> 0.99 us  [pack(): pl.pallas_call(pack_kernel, out_shape=(jax.ShapeDtypeStruct((rows, width...]
    another operation x1 -> x0, local copies, waits for them, and re-layouts: 0.73 us -> none  [pack(): block_ids.reshape(rows, 1)]
    pallas_call x1 -> x2, Pallas kernels: 4.48 us -> 4.54 us  [the longest x1 4.51 us: score(): pl.pallas_call(lambda *refs: score_kernel(order_a, order_b, *refs), out_s...]
where the time goes in v2:
time: 28.1 us; the launch traced here: 27.9 us
  starting transfers between devices  13.7 us (49%)
  waiting for transfers between devices  7.87 us (28%)
  Pallas kernels  6.24 us (22%)
    ppermute x11, starting transfers between devices, move(): lax.ppermute(x, 'own', [(i, to(i // CORES, i % CORES)) for i in range(siz...  7.95 us
    ppermute x11, waiting for transfers between devices, move(): lax.ppermute(x, 'own', [(i, to(i // CORES, i % CORES)) for i in range(siz...  7.87 us
    ppermute x2, starting transfers between devices, per_device_exchanged(): got = lax.ppermute(held, 'qry', [(i, i ^ step) for i in range(planes)])  5.74 us
    pallas_call x1, Pallas kernels, score(): pl.pallas_call(lambda *refs: score_kernel(order_a, order_b, *refs), out_s...  4.51 us
    pallas_call x1, Pallas kernels, pack(): pl.pallas_call(pack_kernel, out_shape=(jax.ShapeDtypeStruct((rows, width...  0.99 us
    pallas_call x1, Pallas kernels, place(): pl.pallas_call(place_kernel, out_shape=jax.ShapeDtypeStruct((rows, 8 * cl...  0.71 us
  transfers between devices with their start and end apart: 13, of which 8 were waited for; matrix products, arithmetic and copies ran while one was open for 0% of the time, Pallas kernels for 0%

profile of v2, /device:TPU:0, one launch (start us, length us, event | category | flops | bytes accessed | tf_op | source)
XLA Modules:
  0.0 27.9 jit_solution(1421130188866020750)
XLA Ops:
  0.0 1.0 %shard_map.64 = (bf16[8,8320]{1,0:T(8,128)(2,1)S(1)}, bf16[1,2,48,128]{3,2,1,0:T(8,128)(2,1)S(1)}) custom-call(bf16[8,8192]{1,0:T(8,128)(2,1)} %bitcast.6, s32[1,8]{1,0:T(1,128)} %ids_hbm.1, bf16[2,16,64]{2,1,0:T(8,128)(2,1)} %left_hbm.1, bf16[2,32,128]{2,1,0:T(8,128)(2,1)} %right_hbm.1), custom_call_target="tpu_custom_call" | custom-call | tf_op jit(solution)/shard_map/pallas_call | solution.py:75
  1.0 3.1 %collective-permute-start.7 = (bf16[1,2,48,128]{3,2,1,0:T(8,128)(2,1)S(1)}, bf16[1,2,48,128]{3,2,1,0:T(8,128)(2,1)S(1)}, u32[]{:S(2)}, u32[]{:S(2)}) collective-permute-start(bf16[1,2,48,128]{3,2,1,0:T(8,128)(2,1)S(1)} %get-tuple-element.12.refs_0_), channel_id=1, source_target_pairs={{0,1},{1,0},{2,3},{3,2},{4,5},{5,4},{6,7},{7,6},{8,9},{9,8},{10,11... | collective-permute-start | bytes 73736 | tf_op jit(solution)/shard_map/ppermute | solution.py:277
  4.1 2.4 %collective-permute-start.2 = (bf16[8,8320]{1,0:T(8,128)(2,1)S(1)}, bf16[8,8320]{1,0:T(8,128)(2,1)S(1)}, u32[]{:S(2)}, u32[]{:S(2)}) collective-permute-start(bf16[8,8320]{1,0:T(8,128)(2,1)S(1)} %get-tuple-element.11.refs_0_), channel_id=1, source_target_pairs={{0,24},{4,28},{8,16},{12,20},{16,8},{20,12},{24,0},{28,4},{1,25},{... | collective-permute-start | bytes 399368 | tf_op jit(solution)/shard_map/ppermute | solution.py:260
  6.5 0.5 %collective-permute-start.1 = (bf16[8,8320]{1,0:T(8,128)(2,1)S(1)}, bf16[8,8320]{1,0:T(8,128)(2,1)S(1)}, u32[]{:S(2)}, u32[]{:S(2)}) collective-permute-start(bf16[8,8320]{1,0:T(8,128)(2,1)S(1)} %get-tuple-element.11.refs_0_), channel_id=1, source_target_pairs={{0,16},{4,12},{8,24},{12,4},{16,0},{20,28},{24,8},{28,20},{1,17},{... | collective-permute-start | bytes 399368 | tf_op jit(solution)/shard_map/ppermute | solution.py:260
  7.0 0.5 %collective-permute-start = (bf16[8,8320]{1,0:T(8,128)(2,1)S(1)}, bf16[8,8320]{1,0:T(8,128)(2,1)S(1)}, u32[]{:S(2)}, u32[]{:S(2)}) collective-permute-start(bf16[8,8320]{1,0:T(8,128)(2,1)S(1)} %get-tuple-element.11.refs_0_), channel_id=1, source_target_pairs={{0,8},{4,20},{8,0},{12,28},{16,24},{20,4},{24,16},{28,12},{1,9},{5... | collective-permute-start | bytes 399368 | tf_op jit(solution)/shard_map/ppermute | solution.py:260
  7.6 0.0 collective-permute-done.7.refs_1_
  7.6 0.0 slice-start.1
  7.6 0.0 copy-start
  7.6 2.7 %collective-permute-start.8 = (bf16[2,2,48,128]{3,2,1,0:T(8,128)(2,1)S(1)}, bf16[2,2,48,128]{3,2,1,0:T(8,128)(2,1)S(1)}, u32[]{:S(2)}, u32[]{:S(2)}) collective-permute-start(bf16[2,2,48,128]{3,2,1,0:T(8,128)(2,1)S(1)} %pad_maximum_fusion), channel_id=1, source_target_pairs={{0,2},{1,3},{2,0},{3,1},{4,6},{5,7},{6,4},{7,5},{8,10},{9,11},{10,... | collective-permute-start | bytes 147464 | tf_op jit(solution)/shard_map/ppermute | solution.py:277
  10.3 1.2 %collective-permute-done.2.refs_3_ = bf16[8,8320]{1,0:T(8,128)(2,1)S(1)} collective-permute-done((bf16[8,8320]{1,0:T(8,128)(2,1)S(1)}, bf16[8,8320]{1,0:T(8,128)(2,1)S(1)}, u32[]{:S(2)}, u32[]{:S(2)}) %collective-permute-start.2) | collective-permute-done | bytes 133152 | tf_op jit(solution)/shard_map/ppermute | solution.py:260
  11.5 1.4 %collective-permute-done.1.refs_2_ = bf16[8,8320]{1,0:T(8,128)(2,1)S(1)} collective-permute-done((bf16[8,8320]{1,0:T(8,128)(2,1)S(1)}, bf16[8,8320]{1,0:T(8,128)(2,1)S(1)}, u32[]{:S(2)}, u32[]{:S(2)}) %collective-permute-start.1) | collective-permute-done | bytes 133152 | tf_op jit(solution)/shard_map/ppermute | solution.py:260
  12.9 0.5 %collective-permute-start.4 = (bf16[8,8320]{1,0:T(8,128)(2,1)S(1)}, bf16[8,8320]{1,0:T(8,128)(2,1)S(1)}, u32[]{:S(2)}, u32[]{:S(2)}) collective-permute-start(bf16[8,8320]{1,0:T(8,128)(2,1)S(1)} %collective-permute-done.refs_1_), channel_id=1, source_target_pairs={{0,4},{4,0},{8,12},{12,8},{16,20},{20,16},{24,28},{28,24},{1,5},{5... | collective-permute-start | bytes 399368 | tf_op jit(solution)/shard_map/ppermute | solution.py:260
  13.5 0.8 %collective-permute-done.5.refs_6_ = bf16[8,8320]{1,0:T(8,128)(2,1)S(1)} collective-permute-done((bf16[8,8320]{1,0:T(8,128)(2,1)S(1)}, bf16[8,8320]{1,0:T(8,128)(2,1)S(1)}, u32[]{:S(2)}, u32[]{:S(2)}) %collective-permute-start.5) | collective-permute-done | bytes 133152 | tf_op jit(solution)/shard_map/ppermute | solution.py:260
  14.3 0.2 collective-permute-done.4.refs_5_
  14.5 4.5 %shard_map.66 = (f32[4,8,512]{2,1,0:T(8,128)S(1)}, f32[4,8,512]{2,1,0:T(8,128)S(1)}) custom-call(bf16[8,8320]{1,0:T(8,128)(2,1)S(1)} %get-tuple-element.11.refs_0_, bf16[8,8320]{1,0:T(8,128)(2,1)S(1)} %collective-permute-done.refs_1_, bf16[8,8320]{1,0:T(8,128)(2,1)S(1)} %collective-permute-done.1.refs_2_, ...), custom_call_target="tpu_custom_call" | custom-call | flops 1585446912 | bytes 8388608 | tf_op jit(solution)/shard_map/pallas_call | solution.py:204
  19.0 0.4 %collective-permute-start.9 = (f32[4,8,512]{2,1,0:T(8,128)S(1)}, f32[4,8,512]{2,1,0:T(8,128)S(1)}, u32[]{:S(2)}, u32[]{:S(2)}) collective-permute-start(f32[4,8,512]{2,1,0:T(8,128)S(1)} %get-tuple-element.16), channel_id=1, source_target_pairs={{0,4},{4,0},{8,12},{12,8},{16,20},{20,16},{24,28},{28,24},{1,5},{5... | collective-permute-start | bytes 196616 | tf_op jit(solution)/shard_map/ppermute | solution.py:260
  19.4 0.9 %collective-permute-done.9.got_ref = f32[4,8,512]{2,1,0:T(8,128)S(1)} collective-permute-done((f32[4,8,512]{2,1,0:T(8,128)S(1)}, f32[4,8,512]{2,1,0:T(8,128)S(1)}, u32[]{:S(2)}, u32[]{:S(2)}) %collective-permute-start.9) | collective-permute-done | bytes 65568 | tf_op jit(solution)/shard_map/ppermute | solution.py:260
  20.3 2.4 %collective-permute-start.10 = (f32[2,8,512]{2,1,0:T(8,128)S(1)}, f32[2,8,512]{2,1,0:T(8,128)S(1)}, u32[]{:S(2)}, u32[]{:S(2)}) collective-permute-start(f32[2,8,512]{2,1,0:T(8,128)S(1)} %pad_maximum_fusion.1), channel_id=1, source_target_pairs={{0,24},{4,28},{8,16},{12,20},{16,8},{20,12},{24,0},{28,4},{1,25},{... | collective-permute-start | bytes 98312 | tf_op jit(solution)/shard_map/ppermute | solution.py:260
  22.8 0.5 %collective-permute-start.11 = (f32[2,8,512]{2,1,0:T(8,128)S(1)}, f32[2,8,512]{2,1,0:T(8,128)S(1)}, u32[]{:S(2)}, u32[]{:S(2)}) collective-permute-start(f32[2,8,512]{2,1,0:T(8,128)S(1)} %pad_maximum_fusion.2), channel_id=1, source_target_pairs={{0,8},{4,20},{8,0},{12,28},{16,24},{20,4},{24,16},{28,12},{1,9},{5... | collective-permute-start | bytes 98312 | tf_op jit(solution)/shard_map/ppermute | solution.py:260
  23.3 0.6 %collective-permute-start.12 = (f32[2,8,512]{2,1,0:T(8,128)S(1)}, f32[2,8,512]{2,1,0:T(8,128)S(1)}, u32[]{:S(2)}, u32[]{:S(2)}) collective-permute-start(f32[2,8,512]{2,1,0:T(8,128)S(1)} %pad_maximum_fusion.3), channel_id=1, source_target_pairs={{0,16},{4,12},{8,24},{12,4},{16,0},{20,28},{24,8},{28,20},{1,17},{... | collective-permute-start | bytes 98312 | tf_op jit(solution)/shard_map/ppermute | solution.py:260
  23.9 1.3 %collective-permute-done.10.d_ref = f32[2,8,512]{2,1,0:T(8,128)S(1)} collective-permute-done((f32[2,8,512]{2,1,0:T(8,128)S(1)}, f32[2,8,512]{2,1,0:T(8,128)S(1)}, u32[]{:S(2)}, u32[]{:S(2)}) %collective-permute-start.10) | collective-permute-done | bytes 32800 | tf_op jit(solution)/shard_map/ppermute | solution.py:260
  25.2 1.5 %collective-permute-done.11.a_ref = f32[2,8,512]{2,1,0:T(8,128)S(1)} collective-permute-done((f32[2,8,512]{2,1,0:T(8,128)S(1)}, f32[2,8,512]{2,1,0:T(8,128)S(1)}, u32[]{:S(2)}, u32[]{:S(2)}) %collective-permute-start.11) | collective-permute-done | bytes 32800 | tf_op jit(solution)/shard_map/ppermute | solution.py:260
  26.7 0.5 %collective-permute-done.12.b_ref = f32[2,8,512]{2,1,0:T(8,128)S(1)} collective-permute-done((f32[2,8,512]{2,1,0:T(8,128)S(1)}, f32[2,8,512]{2,1,0:T(8,128)S(1)}, u32[]{:S(2)}, u32[]{:S(2)}) %collective-permute-start.12) | collective-permute-done | bytes 32800 | tf_op jit(solution)/shard_map/ppermute | solution.py:260
  27.2 0.7 %shard_map.67 = f32[8,4096]{1,0:T(8,128)} custom-call(f32[4,8,512]{2,1,0:T(8,128)S(1)} %get-tuple-element.15.mine_ref, f32[4,8,512]{2,1,0:T(8,128)S(1)} %collective-permute-done.9.got_ref, f32[2,8,512]{2,1,0:T(8,128)S(1)} %collective-permute-done.10.d_ref, f32[2,8,512]{2,1,0:T(8,128)S(1)} %collective-permute-done.11.a_ref, ...), custom_call_target="tpu_custom_call" | custom-call | tf_op jit(solution)/shard_map/pallas_call | solution.py:246
  (19 shorter events, 0.1 us)
Async XLA Ops:
  1.0 6.6 %collective-permute-start.7 = (bf16[1,2,48,128]{3,2,1,0:T(8,128)(2,1)S(1)}, bf16[1,2,48,128]{3,2,1,0:T(8,128)(2,1)S(1)}, u32[]{:S(2)}, u32[]{:S(2)}) collective-permute-start(bf16[1,2,48,128]{3,2,1,0:T(8,128)(2,1)S(1)} %get-tuple-element.12.refs_0_), channel_id=1, source_target_pairs={{0,1},{1,0},{2,3},{3,2},{4,5},{5,4},{6,7},{7,6},{8,9},{9,8},{10,11... | collective-permute-start | bytes 73736 | tf_op jit(solution)/shard_map/ppermute | solution.py:277
  4.1 7.4 %collective-permute-start.2 = (bf16[8,8320]{1,0:T(8,128)(2,1)S(1)}, bf16[8,8320]{1,0:T(8,128)(2,1)S(1)}, u32[]{:S(2)}, u32[]{:S(2)}) collective-permute-start(bf16[8,8320]{1,0:T(8,128)(2,1)S(1)} %get-tuple-element.11.refs_0_), channel_id=1, source_target_pairs={{0,24},{4,28},{8,16},{12,20},{16,8},{20,12},{24,0},{28,4},{1,25},{... | collective-permute-start | bytes 399368 | tf_op jit(solution)/shard_map/ppermute | solution.py:260
  6.5 6.4 %collective-permute-start.1 = (bf16[8,8320]{1,0:T(8,128)(2,1)S(1)}, bf16[8,8320]{1,0:T(8,128)(2,1)S(1)}, u32[]{:S(2)}, u32[]{:S(2)}) collective-permute-start(bf16[8,8320]{1,0:T(8,128)(2,1)S(1)} %get-tuple-element.11.refs_0_), channel_id=1, source_target_pairs={{0,16},{4,12},{8,24},{12,4},{16,0},{20,28},{24,8},{28,20},{1,17},{... | collective-permute-start | bytes 399368 | tf_op jit(solution)/shard_map/ppermute | solution.py:260
  7.0 5.9 %collective-permute-start = (bf16[8,8320]{1,0:T(8,128)(2,1)S(1)}, bf16[8,8320]{1,0:T(8,128)(2,1)S(1)}, u32[]{:S(2)}, u32[]{:S(2)}) collective-permute-start(bf16[8,8320]{1,0:T(8,128)(2,1)S(1)} %get-tuple-element.11.refs_0_), channel_id=1, source_target_pairs={{0,8},{4,20},{8,0},{12,28},{16,24},{20,4},{24,16},{28,12},{1,9},{5... | collective-permute-start | bytes 399368 | tf_op jit(solution)/shard_map/ppermute | solution.py:260
  7.6 6.9 %slice-start = ((s8[8388608]{0:T(1024)(128)(4,1)}), s8[4194304]{0:T(1024)(128)(4,1)S(1)}, s32[]{:S(2)}) async-start(s8[8388608]{0:T(1024)(128)(4,1)} %bitcast.3), calls=%async_computation | async-start | bytes 8388608
  7.6 6.9 %slice-start.1 = ((s8[8388608]{0:T(1024)(128)(4,1)}), s8[4194304]{0:T(1024)(128)(4,1)S(1)}, s32[]{:S(2)}) async-start(s8[8388608]{0:T(1024)(128)(4,1)} %bitcast.3), calls=%async_computation.1 | async-start | bytes 8388608
  7.6 6.9 %copy-start = (s32[512]{0:T(512)S(1)}, s32[512]{0:T(512)}, u32[]{:S(2)}) copy-start(s32[512]{0:T(512)} %param.11) | copy-start | bytes 6148
  7.6 5.8 %collective-permute-start.8 = (bf16[2,2,48,128]{3,2,1,0:T(8,128)(2,1)S(1)}, bf16[2,2,48,128]{3,2,1,0:T(8,128)(2,1)S(1)}, u32[]{:S(2)}, u32[]{:S(2)}) collective-permute-start(bf16[2,2,48,128]{3,2,1,0:T(8,128)(2,1)S(1)} %pad_maximum_fusion), channel_id=1, source_target_pairs={{0,2},{1,3},{2,0},{3,1},{4,6},{5,7},{6,4},{7,5},{8,10},{9,11},{10,... | collective-permute-start | bytes 147464 | tf_op jit(solution)/shard_map/ppermute | solution.py:277
  10.3 3.2 %collective-permute-start.3 = (bf16[8,8320]{1,0:T(8,128)(2,1)S(1)}, bf16[8,8320]{1,0:T(8,128)(2,1)S(1)}, u32[]{:S(2)}, u32[]{:S(2)}) collective-permute-start(bf16[8,8320]{1,0:T(8,128)(2,1)S(1)} %get-tuple-element.11.refs_0_), channel_id=1, source_target_pairs={{0,4},{4,0},{8,12},{12,8},{16,20},{20,16},{24,28},{28,24},{1,5},{5... | collective-permute-start | bytes 399368 | tf_op jit(solution)/shard_map/ppermute | solution.py:260
  11.5 2.0 %collective-permute-start.6 = (bf16[8,8320]{1,0:T(8,128)(2,1)S(1)}, bf16[8,8320]{1,0:T(8,128)(2,1)S(1)}, u32[]{:S(2)}, u32[]{:S(2)}) collective-permute-start(bf16[8,8320]{1,0:T(8,128)(2,1)S(1)} %collective-permute-done.2.refs_3_), channel_id=1, source_target_pairs={{0,4},{4,0},{8,12},{12,8},{16,20},{20,16},{24,28},{28,24},{1,5},{5... | collective-permute-start | bytes 399368 | tf_op jit(solution)/shard_map/ppermute | solution.py:260
  12.9 1.4 %collective-permute-start.5 = (bf16[8,8320]{1,0:T(8,128)(2,1)S(1)}, bf16[8,8320]{1,0:T(8,128)(2,1)S(1)}, u32[]{:S(2)}, u32[]{:S(2)}) collective-permute-start(bf16[8,8320]{1,0:T(8,128)(2,1)S(1)} %collective-permute-done.1.refs_2_), channel_id=1, source_target_pairs={{0,4},{4,0},{8,12},{12,8},{16,20},{20,16},{24,28},{28,24},{1,5},{5... | collective-permute-start | bytes 399368 | tf_op jit(solution)/shard_map/ppermute | solution.py:260
  12.9 1.5 %collective-permute-start.4 = (bf16[8,8320]{1,0:T(8,128)(2,1)S(1)}, bf16[8,8320]{1,0:T(8,128)(2,1)S(1)}, u32[]{:S(2)}, u32[]{:S(2)}) collective-permute-start(bf16[8,8320]{1,0:T(8,128)(2,1)S(1)} %collective-permute-done.refs_1_), channel_id=1, source_target_pairs={{0,4},{4,0},{8,12},{12,8},{16,20},{20,16},{24,28},{28,24},{1,5},{5... | collective-permute-start | bytes 399368 | tf_op jit(solution)/shard_map/ppermute | solution.py:260
  19.0 1.3 %collective-permute-start.9 = (f32[4,8,512]{2,1,0:T(8,128)S(1)}, f32[4,8,512]{2,1,0:T(8,128)S(1)}, u32[]{:S(2)}, u32[]{:S(2)}) collective-permute-start(f32[4,8,512]{2,1,0:T(8,128)S(1)} %get-tuple-element.16), channel_id=1, source_target_pairs={{0,4},{4,0},{8,12},{12,8},{16,20},{20,16},{24,28},{28,24},{1,5},{5... | collective-permute-start | bytes 196616 | tf_op jit(solution)/shard_map/ppermute | solution.py:260
  20.3 4.9 %collective-permute-start.10 = (f32[2,8,512]{2,1,0:T(8,128)S(1)}, f32[2,8,512]{2,1,0:T(8,128)S(1)}, u32[]{:S(2)}, u32[]{:S(2)}) collective-permute-start(f32[2,8,512]{2,1,0:T(8,128)S(1)} %pad_maximum_fusion.1), channel_id=1, source_target_pairs={{0,24},{4,28},{8,16},{12,20},{16,8},{20,12},{24,0},{28,4},{1,25},{... | collective-permute-start | bytes 98312 | tf_op jit(solution)/shard_map/ppermute | solution.py:260
  22.8 3.9 %collective-permute-start.11 = (f32[2,8,512]{2,1,0:T(8,128)S(1)}, f32[2,8,512]{2,1,0:T(8,128)S(1)}, u32[]{:S(2)}, u32[]{:S(2)}) collective-permute-start(f32[2,8,512]{2,1,0:T(8,128)S(1)} %pad_maximum_fusion.2), channel_id=1, source_target_pairs={{0,8},{4,20},{8,0},{12,28},{16,24},{20,4},{24,16},{28,12},{1,9},{5... | collective-permute-start | bytes 98312 | tf_op jit(solution)/shard_map/ppermute | solution.py:260
  23.3 3.9 %collective-permute-start.12 = (f32[2,8,512]{2,1,0:T(8,128)S(1)}, f32[2,8,512]{2,1,0:T(8,128)S(1)}, u32[]{:S(2)}, u32[]{:S(2)}) collective-permute-start(f32[2,8,512]{2,1,0:T(8,128)S(1)} %pad_maximum_fusion.3), channel_id=1, source_target_pairs={{0,16},{4,12},{8,24},{12,4},{16,0},{20,28},{24,8},{28,20},{1,17},{... | collective-permute-start | bytes 98312 | tf_op jit(solution)/shard_map/ppermute | solution.py:260

commit v3 on v2

v3 whole, which is shorter than its diff:
```python
import jax
import jax.numpy as jnp
from jax import lax
from jax.experimental import pallas as pl
from jax.experimental.pallas import tpu as pltpu
from jax.sharding import PartitionSpec as P

LANES = 128
CORES = 2
HEAD = 256
SOME_VMEM = 16 << 20
VMEM = pl.BlockSpec(memory_space=pltpu.VMEM)
HBM = pl.BlockSpec(memory_space=pltpu.HBM)
ANY = pl.BlockSpec(memory_space=pl.ANY)
F32 = jnp.float32
BF16 = jnp.bfloat16


def precondition(rows, id_values, left_full, right_full):
    blocks = left_full.shape[0]
    order_a = left_full.shape[1]
    order_b = right_full.shape[1]
    labels = jnp.arange(blocks)
    onehot = (id_values[:, :, None] == labels[None, None, :]).astype(F32)
    left_rows = jnp.einsum("srk,kac->srac", onehot, left_full.astype(F32), precision=lax.Precision.HIGHEST)
    right_rows = jnp.einsum("srk,kde->srde", onehot, right_full.astype(F32), precision=lax.Precision.HIGHEST)
    matrix = rows.reshape(rows.shape[0], rows.shape[1], order_a, order_b).astype(F32)
    inner = jnp.einsum("srac,srcd->srad", left_rows, matrix, precision=lax.Precision.HIGHEST)
    outer = jnp.einsum("srad,srde->srae", inner, right_rows, precision=lax.Precision.HIGHEST)
    return outer.reshape(rows.shape).astype(BF16)


def per_device_gathered(queries, block_ids, left_factor, right_factor, clip_grads, lengths):
    left_full = lax.all_gather(left_factor, "qry", axis=1, tiled=True)
    right_full = lax.all_gather(right_factor, "qry", axis=1, tiled=True)
    prepared = precondition(queries, block_ids, left_full, right_full)
    tiles = jnp.einsum(
        "srw,cw->src",
        lax.all_gather(prepared, "own", axis=1, tiled=True),
        clip_grads,
        preferred_element_type=F32,
    )
    factor = lax.rsqrt(F32(queries.shape[2]) * lengths.astype(F32))
    return lax.all_to_all(tiles * factor[None, None, :], "own", split_axis=1, concat_axis=2, tiled=True)


def pack_kernel(q_hbm, ids_hbm, left_hbm, right_hbm, row_ref, again_ref, fac_ref, ids_s, left_s, right_s, sems):
    rows, width = q_hbm.shape
    blocks, cut, order_a = left_s.shape
    copies = [
        pltpu.make_async_copy(left_hbm, left_s, sems.at[0]),
        pltpu.make_async_copy(right_hbm, right_s, sems.at[1]),
        pltpu.make_async_copy(ids_hbm, ids_s, sems.at[2]),
        pltpu.make_async_copy(q_hbm, row_ref.at[:, :width], sems.at[3]),
        pltpu.make_async_copy(q_hbm, again_ref.at[:, :width], sems.at[4]),
    ]
    for copy in copies:
        copy.start()
    copies[2].wait()
    square = (rows, rows)
    diagonal = lax.broadcasted_iota(jnp.int32, square, 0) == lax.broadcasted_iota(jnp.int32, square, 1)
    labels = jnp.where(diagonal, jnp.broadcast_to(ids_s[...].astype(F32), square), 0.0)
    column = jnp.sum(labels, axis=1, keepdims=True)
    column = jnp.broadcast_to(column, (rows, LANES)).astype(BF16)
    row_ref[:, width:] = column
    again_ref[:, width:] = column
    copies[0].wait()
    copies[1].wait()
    fac_ref[0, :, :cut, :order_a] = left_s[...]
    fac_ref[0, :, :cut, order_a:] = jnp.zeros((blocks, cut, LANES - order_a), BF16)
    fac_ref[0, :, cut:, :] = right_s[...]
    copies[3].wait()
    copies[4].wait()


def pack(queries, block_ids, left, right):
    rows, width = queries.shape
    blocks, cut = left.shape[:2]
    depth = cut + right.shape[1]
    return pl.pallas_call(
        pack_kernel,
        out_shape=(
            jax.ShapeDtypeStruct((rows, width + LANES), BF16),
            jax.ShapeDtypeStruct((rows, width + LANES), BF16),
            jax.ShapeDtypeStruct((1, blocks, depth, LANES), BF16),
        ),
        in_specs=[HBM] * 4,
        out_specs=(VMEM,) * 3,
        scratch_shapes=[
            pltpu.VMEM(block_ids.shape, block_ids.dtype),
            pltpu.VMEM(left.shape, left.dtype),
            pltpu.VMEM(right.shape, right.dtype),
            pltpu.SemaphoreType.DMA((5,)),
        ],
        compiler_params=pltpu.CompilerParams(vmem_limit_bytes=SOME_VMEM),
    )(*(pltpu.with_memory_space_constraint(x, pltpu.HBM) for x in (queries, block_ids, left, right)))


def prepare(slots, left_all, right_all, in_s, out_s, prep_ref):
    rows = slots[0].shape[0]
    order_a = left_all.shape[1]
    blocks = left_all.shape[0] // order_a
    order_b = right_all.shape[1] // blocks
    width = order_a * order_b
    pair = 2 * rows
    for group in range(len(slots) // 2):
        for half in range(2):
            ref = slots[2 * group + half]
            for a in range(order_a):
                in_s[a * pair + half * rows : a * pair + half * rows + rows, :] = ref[
                    :, a * order_b : (a + 1) * order_b
                ].astype(F32)
        for n in range(0, pair, 2):
            ref = slots[2 * group + n // rows]
            x = jnp.concatenate(
                [in_s[pl.ds(n + j, order_a, stride=pair), :].astype(BF16) for j in range(2)], axis=1
            )
            inner = jnp.dot(left_all, x, preferred_element_type=F32)
            split = []
            ids = []
            for j in range(2):
                label = ref[(n + j) % rows : (n + j) % rows + 1, width:].astype(F32)
                ids.append(label)
                one = inner[:order_a, j * order_b : (j + 1) * order_b]
                for k in range(1, blocks):
                    one = jnp.where(
                        label > k - 0.5,
                        inner[k * order_a : (k + 1) * order_a, j * order_b : (j + 1) * order_b],
                        one,
                    )
                high = one.astype(BF16)
                low = (one - high.astype(F32)).astype(BF16)
                split.append(jnp.concatenate([high, low], axis=1))
            outer = jnp.dot(jnp.concatenate(split, axis=0), right_all, preferred_element_type=F32)
            for j in range(2):
                one = outer[j * order_a : (j + 1) * order_a, :order_b]
                for k in range(1, blocks):
                    one = jnp.where(
                        ids[j] > k - 0.5,
                        outer[j * order_a : (j + 1) * order_a, k * order_b : (k + 1) * order_b],
                        one,
                    )
                out_s[pl.ds(n + j, order_a, stride=pair), :] = one
        for a in range(order_a):
            prep_ref[group * pair : (group + 1) * pair, a * order_b : (a + 1) * order_b] = out_s[
                a * pair : (a + 1) * pair, :
            ].astype(BF16)


def factor_kernel(order_a, order_b, steps, *refs):
    fac_refs = refs[: steps + 1]
    left_ref, right_ref = refs[steps + 1 :]
    blocks = fac_refs[0].shape[1]
    planes = 2**steps
    cut_a, cut_b = order_a // planes, order_b // planes
    plane = lax.axis_index("qry")
    for m in range(planes):
        step = m.bit_length()
        piece = fac_refs[step][m - (1 << (step - 1)) if step else 0]
        at = lax.bitwise_xor(plane, m)
        for k in range(blocks):
            left_ref[pl.ds(pl.multiple_of(k * order_a + at * cut_a, 16), cut_a), :] = piece[k, :cut_a, :order_a]
            for half in range(2):
                right_ref[
                    pl.ds(pl.multiple_of(half * order_b + at * cut_b, 16), cut_b),
                    k * order_b : (k + 1) * order_b,
                ] = piece[k, cut_a:, :]


def place_factors(factors, order_a, order_b):
    blocks = factors[0].shape[1]
    return pl.pallas_call(
        lambda *refs: factor_kernel(order_a, order_b, len(factors) - 1, *refs),
        out_shape=(
            jax.ShapeDtypeStruct((blocks * order_a, order_a), BF16),
            jax.ShapeDtypeStruct((2 * order_b, blocks * order_b), BF16),
        ),
        in_specs=[VMEM] * len(factors),
        out_specs=(VMEM, VMEM),
        compiler_params=pltpu.CompilerParams(vmem_limit_bytes=8 << 20),
        cost_estimate=pl.CostEstimate(flops=10**10, bytes_accessed=10**6, transcendentals=0),
    )(*factors)


def early_kernel(nslots, *refs):
    slots = refs[:nslots]
    left_ref, right_ref, prep_ref, in_s, out_s = refs[nslots:]
    prepare(slots, left_ref[...], right_ref[...], in_s, out_s, prep_ref)


def early(slots, left_all, right_all, order_a, order_b):
    rows = slots[0].shape[0]
    total = len(slots) * rows
    width = order_a * order_b
    return pl.pallas_call(
        lambda *refs: early_kernel(len(slots), *refs),
        out_shape=jax.ShapeDtypeStruct((total, width), BF16),
        in_specs=[VMEM] * (len(slots) + 2),
        out_specs=VMEM,
        scratch_shapes=[pltpu.VMEM((order_a * 2 * rows, order_b), F32)] * 2,
        compiler_params=pltpu.CompilerParams(vmem_limit_bytes=SOME_VMEM),
        cost_estimate=pl.CostEstimate(flops=8 * total * width * order_b, bytes_accessed=4 * total * width, transcendentals=0),
    )(*slots, left_all, right_all)


def score_kernel(nslots, *refs):
    slots = refs[:nslots]
    early_ref, left_ref, right_ref, clips_ref, len_ref = refs[nslots : nslots + 5]
    home_ref, near_ref, x_ref, cross_ref, y_ref, d_ref, in_s, out_s, prep_s, all_s = refs[nslots + 5 :]
    width = clips_ref.shape[1]
    rows = slots[0].shape[0]
    prepare(slots, left_ref[...], right_ref[...], in_s, out_s, prep_s)
    queries = jnp.concatenate([early_ref[...], prep_s[...]], axis=0)
    raw = lax.dot_general(clips_ref[...], queries, (((1,), (1,)), ((), ())), preferred_element_type=F32)
    factor = lax.rsqrt(F32(width) * len_ref[...].astype(F32))
    scores = raw.T * factor
    core = lax.rem(lax.axis_index("own"), CORES)
    for j, (mine, other) in enumerate(((0, 0), (3, 3), (1 + core, 2 - core), (2 - core, 1 + core))):
        at = 2 * j * rows
        all_s[mine, core] = scores[at : at + rows].astype(BF16)
        all_s[other, 1 - core] = scores[at + rows : at + 2 * rows].astype(BF16)
    home_ref[...] = scores[:rows]
    near_ref[...] = all_s[0, 1 - core]
    x_ref[...] = all_s[1, core]
    cross_ref[...] = all_s[1, 1 - core]
    y_ref[...] = all_s[2]
    d_ref[...] = all_s[3]


def score(slots, prepared, left_all, right_all, clip_grads, lengths):
    rows = slots[0].shape[0]
    clips, width = clip_grads.shape
    order_a = left_all.shape[1]
    total = prepared.shape[0] + len(slots) * rows
    return pl.pallas_call(
        lambda *refs: score_kernel(len(slots), *refs),
        out_shape=(
            jax.ShapeDtypeStruct((rows, clips), F32),
            *(jax.ShapeDtypeStruct((rows, clips), BF16),) * 3,
            *(jax.ShapeDtypeStruct((2, rows, clips), BF16),) * 2,
        ),
        in_specs=[VMEM] * (len(slots) + 5),
        out_specs=(VMEM,) * 6,
        scratch_shapes=[pltpu.VMEM((order_a * 2 * rows, width // order_a), F32)] * 2
        + [pltpu.VMEM((len(slots) * rows, width), BF16), pltpu.VMEM((4, 2, rows, clips), BF16)],
        compiler_params=pltpu.CompilerParams(vmem_limit_bytes=SOME_VMEM),
        cost_estimate=pl.CostEstimate(
            flops=2 * total * width * (clips + 1000), bytes_accessed=clips * width * 2, transcendentals=0
        ),
    )(*slots, prepared, left_all, right_all, clip_grads, lengths.reshape(1, clips))


def in_hbm(x):
    return pltpu.with_memory_space_constraint(x, pltpu.HBM)


def join_kernel(first_ref, second_ref, row_ref, both_ref, same_ref):
    del row_ref, same_ref
    count = first_ref.shape[0]
    both_ref[:count] = first_ref[...]
    both_ref[count:] = second_ref[...]


def join(first, second, row):
    return pl.pallas_call(
        join_kernel,
        out_shape=(
            jax.ShapeDtypeStruct((2 * first.shape[0],) + first.shape[1:], first.dtype),
            jax.ShapeDtypeStruct(row.shape, row.dtype),
        ),
        in_specs=[VMEM, VMEM, ANY],
        out_specs=(VMEM, ANY),
        input_output_aliases={2: 1},
        compiler_params=pltpu.CompilerParams(vmem_limit_bytes=8 << 20),
    )(first, second, row)


def relay_kernel(d_ref, y_ref, near_ref, out_ref):
    other = 1 - lax.rem(lax.axis_index("own"), CORES)
    out_ref[0] = d_ref[other]
    out_ref[1] = y_ref[other]
    out_ref[2] = near_ref[...]


def relay(d, y, near):
    return pl.pallas_call(
        relay_kernel,
        out_shape=jax.ShapeDtypeStruct((3,) + near.shape, near.dtype),
        in_specs=[VMEM] * 3,
        out_specs=VMEM,
        compiler_params=pltpu.CompilerParams(vmem_limit_bytes=8 << 20),
    )(d, y, near)


def widen_kernel(home_ref, x_ref, cross_ref, out_ref):
    for j, ref in enumerate((home_ref, x_ref, cross_ref)):
        out_ref[j] = ref[...].astype(F32)


def widen(*parts):
    return pl.pallas_call(
        widen_kernel,
        out_shape=jax.ShapeDtypeStruct((len(parts),) + parts[0].shape, F32),
        in_specs=[VMEM] * len(parts),
        out_specs=VMEM,
        compiler_params=pltpu.CompilerParams(vmem_limit_bytes=8 << 20),
        cost_estimate=pl.CostEstimate(flops=10**10, bytes_accessed=10**6, transcendentals=0),
    )(*parts)


def place_kernel(wide_ref, d_ref, y_ref, relayed_ref, out_ref, wide_s, sem):
    _, rows, clips = wide_ref.shape
    index = lax.axis_index("own")
    core = lax.rem(index, CORES)
    chip = lax.div(index, CORES)

    def put(value, flip, core_of):
        at = pl.multiple_of((lax.bitwise_xor(chip, flip) * CORES + core_of) * clips, clips)
        wide_s[:, pl.ds(at, clips)] = value.astype(F32)

    put(wide_ref[0], 0, core)
    put(wide_ref[1], 1, core)
    put(wide_ref[2], 1, 1 - core)
    put(y_ref[core], 2, core)
    put(d_ref[core], 3, core)
    put(relayed_ref[0], 3, 1 - core)
    put(relayed_ref[1], 2, 1 - core)
    put(relayed_ref[2], 0, 1 - core)
    copy = pltpu.make_async_copy(wide_s, out_ref, sem)
    copy.start()
    copy.wait()


def place(*parts):
    rows, clips = parts[0].shape[1:]
    wide = (rows, 8 * clips)
    return pl.pallas_call(
        place_kernel,
        out_shape=jax.ShapeDtypeStruct(wide, F32),
        in_specs=[VMEM] * len(parts),
        out_specs=HBM,
        scratch_shapes=[pltpu.VMEM(wide, F32), pltpu.SemaphoreType.DMA(())],
        compiler_params=pltpu.CompilerParams(vmem_limit_bytes=8 << 20),
    )(*parts)


def per_device_exchanged(planes, queries, block_ids, left_factor, right_factor, clip_grads, lengths):
    size = 4 * CORES

    def move(x, to):
        return lax.ppermute(x, "own", [(i, to(i // CORES, i % CORES)) for i in range(size)])

    def sibling(x):
        return move(x, lambda chip, core: chip * CORES + 1 - core)

    def across(x, flips):
        return move(x, lambda chip, core: (chip ^ flips[core]) * CORES + core)

    flips_a, flips_b = (1, 2), (2, 1)
    row, again, fac = pack(queries[0], block_ids, left_factor, right_factor)
    slot_d = across(row, (3, 3))
    slot_a = across(row, flips_a)
    factors = [fac]
    held = fac
    step = 1
    while step < planes:
        got = lax.ppermute(held, "qry", [(i, i ^ step) for i in range(planes)])
        factors.append(got)
        if step * 2 < planes:
            held, again = join(held, got, again)
        step *= 2
    slot_b = across(again, flips_b)
    order_a, order_b = left_factor.shape[2], right_factor.shape[2]
    left_all, right_all = place_factors(factors, order_a, order_b)
    prepared = early(
        [row, sibling(row), slot_d, sibling(slot_d)], left_all, right_all, order_a, order_b
    )
    home, near, x, cross, y, d = score([slot_a, sibling(slot_a), slot_b, sibling(slot_b)], prepared, left_all, right_all, clip_grads, lengths)
    y, d = across(y, (2, 2)), across(d, (3, 3))
    x, cross = across(x, (1, 1)), move(cross, lambda chip, core: (chip ^ 1) * CORES + 1 - core)
    return place(widen(home, x, cross), d, y, sibling(relay(d, y, near)))[None]


def solution(mesh):
    owners, planes = mesh.shape["own"], mesh.shape["qry"]

    def per_device(queries, block_ids, left_factor, right_factor, clip_grads, lengths):
        whole_tiles = left_factor.shape[1] % 16 == 0 and right_factor.shape[1] % 16 == 0
        if owners == 4 * CORES and planes & (planes - 1) == 0 and whole_tiles:
            return per_device_exchanged(
                planes, queries, block_ids, left_factor, right_factor, clip_grads, lengths
            )
        return per_device_gathered(queries, block_ids, left_factor, right_factor, clip_grads, lengths)

    in_specs = (
        P("qry", "own", None),
        P("qry", "own"),
        P(None, "qry", None),
        P(None, "qry", None),
        P("own", None),
        P("own"),
    )
    out_specs = P("qry", "own", None)
    return jax.shard_map(
        per_device, mesh=mesh, in_specs=in_specs, out_specs=out_specs, check_vma=False
    )
```

time: 28.1 us -> 26.3 us (0.936)
  waiting for transfers between devices: 7.87 us -> 4.91 us
  starting transfers between devices: 13.7 us -> 14.7 us
    ppermute x11 -> x12, waiting for transfers between devices: 7.87 us -> 4.9 us  [move(): lax.ppermute(x, 'own', [(i, to(i // CORES, i % CORES)) for i in range(siz...]
    ppermute x11 -> x12, starting transfers between devices: 7.95 us -> 9.01 us  [move(): lax.ppermute(x, 'own', [(i, to(i // CORES, i % CORES)) for i in range(siz...]
    pallas_call x2 -> x6, Pallas kernels: 5.22 us -> 5.34 us  [the longest x1 3.54 us: score(): pl.pallas_call(lambda *refs: score_kernel(len(slots), *refs), out_shape=(...]
  transfers between devices with their start and end apart: 13 -> 14, of which waited for: 8 -> 7; matrix products, arithmetic and copies ran while one was open for 0% -> 0% of each run, Pallas kernels for 0% -> 4%
where the time goes in v3:
time: 26.3 us; the launch traced here: 26.1 us
  starting transfers between devices  14.7 us (56%)
  Pallas kernels  6.43 us (24%)
  waiting for transfers between devices  4.91 us (19%)
    ppermute x12, starting transfers between devices, move(): lax.ppermute(x, 'own', [(i, to(i // CORES, i % CORES)) for i in range(siz...  9.01 us
    ppermute x2, starting transfers between devices, per_device_exchanged(): got = lax.ppermute(held, 'qry', [(i, i ^ step) for i in range(planes)])  5.68 us
    ppermute x12, waiting for transfers between devices, move(): lax.ppermute(x, 'own', [(i, to(i // CORES, i % CORES)) for i in range(siz...  4.9 us
    pallas_call x1, Pallas kernels, score(): pl.pallas_call(lambda *refs: score_kernel(len(slots), *refs), out_shape=(...  3.54 us
    pallas_call x1, Pallas kernels, early(): pl.pallas_call(lambda *refs: early_kernel(len(slots), *refs), out_shape=j...  1.1 us
    pallas_call x1, Pallas kernels, pack(): pl.pallas_call(pack_kernel, out_shape=(jax.ShapeDtypeStruct((rows, width...  1.06 us
    pallas_call x1, Pallas kernels, place(): pl.pallas_call(place_kernel, out_shape=jax.ShapeDtypeStruct(wide, F32), i...  0.68 us
  transfers between devices with their start and end apart: 14, of which 7 were waited for; matrix products, arithmetic and copies ran while one was open for 0% of the time, Pallas kernels for 4%

profile of v3, /device:TPU:0, one launch (start us, length us, event | category | flops | bytes accessed | tf_op | source)
XLA Modules:
  0.0 26.1 jit_solution(13529305581527748282)
XLA Ops:
  0.0 1.1 %shard_map.64 = (bf16[8,8320]{1,0:T(8,128)(2,1)S(1)}, bf16[8,8320]{1,0:T(8,128)(2,1)S(1)}, bf16[1,2,48,128]{3,2,1,0:T(8,128)(2,1)S(1)}) custom-call(bf16[8,8192]{1,0:T(8,128)(2,1)} %bitcast.6, s32[1,8]{1,0:T(1,128)} %ids_hbm.1, bf16[2,16,64]{2,1,0:T(8,128)(2,1)} %left_hbm.1, bf16[2,32,128]{2,1,0:T(8,128)(2,1)} %right_hbm.1), custom_call_target="tpu_custom_call" | custom-call | tf_op jit(solution)/shard_map/pallas_call | solution.py:80
  1.1 3.1 %collective-permute-start.2 = (bf16[1,2,48,128]{3,2,1,0:T(8,128)(2,1)S(1)}, bf16[1,2,48,128]{3,2,1,0:T(8,128)(2,1)S(1)}, u32[]{:S(2)}, u32[]{:S(2)}) collective-permute-start(bf16[1,2,48,128]{3,2,1,0:T(8,128)(2,1)S(1)} %get-tuple-element.19.first_ref.refs_0_), channel_id=1, source_target_pairs={{0,1},{1,0},{2,3},{3,2},{4,5},{5,4},{6,7},{7,6},{8,9},{9,8},{10,11... | collective-permute-start | bytes 73736 | tf_op jit(solution)/shard_map/ppermute | solution.py:367
  4.2 2.4 %collective-permute-start.6 = (bf16[8,8320]{1,0:T(8,128)(2,1)S(1)}, bf16[8,8320]{1,0:T(8,128)(2,1)S(1)}, u32[]{:S(2)}, u32[]{:S(2)}) collective-permute-start(bf16[8,8320]{1,0:T(8,128)(2,1)S(1)} %get-tuple-element.18.refs_0_), channel_id=1, source_target_pairs={{0,24},{4,28},{8,16},{12,20},{16,8},{20,12},{24,0},{28,4},{1,25},{... | collective-permute-start | bytes 399368 | tf_op jit(solution)/shard_map/ppermute | solution.py:351
  6.6 0.5 %collective-permute-start = (bf16[8,8320]{1,0:T(8,128)(2,1)S(1)}, bf16[8,8320]{1,0:T(8,128)(2,1)S(1)}, u32[]{:S(2)}, u32[]{:S(2)}) collective-permute-start(bf16[8,8320]{1,0:T(8,128)(2,1)S(1)} %get-tuple-element.18.refs_0_), channel_id=1, source_target_pairs={{0,8},{4,20},{8,0},{12,28},{16,24},{20,4},{24,16},{28,12},{1,9},{5... | collective-permute-start | bytes 399368 | tf_op jit(solution)/shard_map/ppermute | solution.py:351
  7.1 0.8 %collective-permute-start.3 = (bf16[8,8320]{1,0:T(8,128)(2,1)S(1)}, bf16[8,8320]{1,0:T(8,128)(2,1)S(1)}, u32[]{:S(2)}, u32[]{:S(2)}) collective-permute-start(bf16[8,8320]{1,0:T(8,128)(2,1)S(1)} %get-tuple-element.21), channel_id=1, source_target_pairs={{0,16},{4,12},{8,24},{12,4},{16,0},{20,28},{24,8},{28,20},{1,17},{... | collective-permute-start | bytes 399368 | tf_op jit(solution)/shard_map/ppermute | solution.py:351
  7.9 2.6 %collective-permute-start.8 = (bf16[2,2,48,128]{3,2,1,0:T(8,128)(2,1)S(1)}, bf16[2,2,48,128]{3,2,1,0:T(8,128)(2,1)S(1)}, u32[]{:S(2)}, u32[]{:S(2)}) collective-permute-start(bf16[2,2,48,128]{3,2,1,0:T(8,128)(2,1)S(1)} %get-tuple-element.22), channel_id=1, source_target_pairs={{0,2},{1,3},{2,0},{3,1},{4,6},{5,7},{6,4},{7,5},{8,10},{9,11},{10,... | collective-permute-start | bytes 147464 | tf_op jit(solution)/shard_map/ppermute | solution.py:367
  10.5 0.0 collective-permute-start.5
  10.5 0.1 collective-permute-done.6.refs_2_
  10.6 0.5 %collective-permute-start.7 = (bf16[8,8320]{1,0:T(8,128)(2,1)S(1)}, bf16[8,8320]{1,0:T(8,128)(2,1)S(1)}, u32[]{:S(2)}, u32[]{:S(2)}) collective-permute-start(bf16[8,8320]{1,0:T(8,128)(2,1)S(1)} %collective-permute-done.6.refs_2_), channel_id=1, source_target_pairs={{0,4},{4,0},{8,12},{12,8},{16,20},{20,16},{24,28},{28,24},{1,5},{5... | collective-permute-start | bytes 399368 | tf_op jit(solution)/shard_map/ppermute | solution.py:351
  11.0 1.9 %collective-permute-done.refs_0_ = bf16[8,8320]{1,0:T(8,128)(2,1)S(1)} collective-permute-done((bf16[8,8320]{1,0:T(8,128)(2,1)S(1)}, bf16[8,8320]{1,0:T(8,128)(2,1)S(1)}, u32[]{:S(2)}, u32[]{:S(2)}) %collective-permute-start) | collective-permute-done | bytes 133152 | tf_op jit(solution)/shard_map/ppermute | solution.py:351
  13.0 0.0 collective-permute-start.1
  13.0 0.5 %collective-permute-start.4 = (bf16[8,8320]{1,0:T(8,128)(2,1)S(1)}, bf16[8,8320]{1,0:T(8,128)(2,1)S(1)}, u32[]{:S(2)}, u32[]{:S(2)}) collective-permute-start(bf16[8,8320]{1,0:T(8,128)(2,1)S(1)} %collective-permute-done.3.refs_2_), channel_id=1, source_target_pairs={{0,4},{4,0},{8,12},{12,8},{16,20},{20,16},{24,28},{28,24},{1,5},{5... | collective-permute-start | bytes 399368 | tf_op jit(solution)/shard_map/ppermute | solution.py:351
  13.5 0.0 collective-permute-done.5.refs_1_
  13.5 1.1 %shard_map.67.refs_4_ = bf16[32,8192]{1,0:T(8,128)(2,1)S(1)} custom-call(bf16[8,8320]{1,0:T(8,128)(2,1)S(1)} %get-tuple-element.18.refs_0_, bf16[8,8320]{1,0:T(8,128)(2,1)S(1)} %collective-permute-done.5.refs_1_, bf16[8,8320]{1,0:T(8,128)(2,1)S(1)} %collective-permute-done.6.refs_2_, bf16[8,8320]{1,0:T(8,128)(2,1)S(1)} %collective-permute-done.7.refs_3_, ...), custom_call_target="tpu_custom_call" | custom-call | flops 268435456 | bytes 1048576 | tf_op jit(solution)/shard_map/pallas_call | solution.py:195
  14.7 3.5 %shard_map.68 = (f32[8,512]{1,0:T(8,128)S(1)}, bf16[8,512]{1,0:T(8,128)(2,1)S(1)}, bf16[8,512]{1,0:T(8,128)(2,1)S(1)}, bf16[8,512]{1,0:T(8,128)(2,1)S(1)}, bf16[...) custom-call(bf16[8,8320]{1,0:T(8,128)(2,1)S(1)} %collective-permute-done.refs_0_, ...), custom_call_target="tpu_custom_call" | custom-call | flops 1585446912 | bytes 8388608 | tf_op jit(solution)/shard_map/pallas_call | solution.py:235
  18.3 2.3 %collective-permute-start.11 = (bf16[2,8,512]{2,1,0:T(8,128)(2,1)S(1)}, bf16[2,8,512]{2,1,0:T(8,128)(2,1)S(1)}, u32[]{:S(2)}, u32[]{:S(2)}) collective-permute-start(bf16[2,8,512]{2,1,0:T(8,128)(2,1)S(1)} %get-tuple-element.28), channel_id=1, source_target_pairs={{0,24},{4,28},{8,16},{12,20},{16,8},{20,12},{24,0},{28,4},{1,25},{... | collective-permute-start | bytes 49160 | tf_op jit(solution)/shard_map/ppermute | solution.py:351
  20.5 0.8 %collective-permute-start.12 = (bf16[2,8,512]{2,1,0:T(8,128)(2,1)S(1)}, bf16[2,8,512]{2,1,0:T(8,128)(2,1)S(1)}, u32[]{:S(2)}, u32[]{:S(2)}) collective-permute-start(bf16[2,8,512]{2,1,0:T(8,128)(2,1)S(1)} %get-tuple-element.29), channel_id=1, source_target_pairs={{0,16},{4,20},{8,24},{12,28},{16,0},{20,4},{24,8},{28,12},{1,17},{... | collective-permute-start | bytes 49160 | tf_op jit(solution)/shard_map/ppermute | solution.py:351
  21.3 1.2 %collective-permute-start.9 = (bf16[8,512]{1,0:T(8,128)(2,1)S(1)}, bf16[8,512]{1,0:T(8,128)(2,1)S(1)}, u32[]{:S(2)}, u32[]{:S(2)}) collective-permute-start(bf16[8,512]{1,0:T(8,128)(2,1)S(1)} %get-tuple-element.26), channel_id=1, source_target_pairs={{0,8},{4,12},{8,0},{12,4},{16,24},{20,28},{24,16},{28,20},{1,9},{5... | collective-permute-start | bytes 24584 | tf_op jit(solution)/shard_map/ppermute | solution.py:351
  22.5 0.4 %collective-permute-done.11.d_ref = bf16[2,8,512]{2,1,0:T(8,128)(2,1)S(1)} collective-permute-done((bf16[2,8,512]{2,1,0:T(8,128)(2,1)S(1)}, bf16[2,8,512]{2,1,0:T(8,128)(2,1)S(1)}, u32[]{:S(2)}, u32[]{:S(2)}) %collective-permute-start.11) | collective-permute-done | bytes 16416 | tf_op jit(solution)/shard_map/ppermute | solution.py:351
  23.0 1.3 %collective-permute-done.12.y_ref = bf16[2,8,512]{2,1,0:T(8,128)(2,1)S(1)} collective-permute-done((bf16[2,8,512]{2,1,0:T(8,128)(2,1)S(1)}, bf16[2,8,512]{2,1,0:T(8,128)(2,1)S(1)}, u32[]{:S(2)}, u32[]{:S(2)}) %collective-permute-start.12) | collective-permute-done | bytes 16416 | tf_op jit(solution)/shard_map/ppermute | solution.py:351
  24.3 0.1 collective-permute-done.10.cross_ref
  24.4 0.6 %collective-permute-done.9.x_ref = bf16[8,512]{1,0:T(8,128)(2,1)S(1)} collective-permute-done((bf16[8,512]{1,0:T(8,128)(2,1)S(1)}, bf16[8,512]{1,0:T(8,128)(2,1)S(1)}, u32[]{:S(2)}, u32[]{:S(2)}) %collective-permute-start.9) | collective-permute-done | bytes 8224 | tf_op jit(solution)/shard_map/ppermute | solution.py:351
  25.0 0.5 %collective-permute-done.13.relayed_ref = bf16[3,8,512]{2,1,0:T(8,128)(2,1)S(1)} collective-permute-done((bf16[3,8,512]{2,1,0:T(8,128)(2,1)S(1)}, bf16[3,8,512]{2,1,0:T(8,128)(2,1)S(1)}, u32[]{:S(2)}, u32[]{:S(2)}) %collective-permute-start.13) | collective-permute-done | bytes 24608 | tf_op jit(solution)/shard_map/ppermute | solution.py:351
  25.5 0.7 %shard_map.71 = f32[8,4096]{1,0:T(8,128)} custom-call(f32[3,8,512]{2,1,0:T(8,128)S(1)} %shard_map.69.wide_ref, bf16[2,8,512]{2,1,0:T(8,128)(2,1)S(1)} %collective-permute-done.11.d_ref, bf16[2,8,512]{2,1,0:T(8,128)(2,1)S(1)} %collective-permute-done.12.y_ref, bf16[3,8,512]{2,1,0:T(8,128)(2,1)S(1)} %collective-permute-done.13.relayed_ref), custom_call_target="tpu_custom_call" | custom-call | tf_op jit(solution)/shard_map/pallas_call | solution.py:337
  (19 shorter events, 0.1 us)
Async XLA Ops:
  1.1 6.1 %collective-permute-start.2 = (bf16[1,2,48,128]{3,2,1,0:T(8,128)(2,1)S(1)}, bf16[1,2,48,128]{3,2,1,0:T(8,128)(2,1)S(1)}, u32[]{:S(2)}, u32[]{:S(2)}) collective-permute-start(bf16[1,2,48,128]{3,2,1,0:T(8,128)(2,1)S(1)} %get-tuple-element.19.first_ref.refs_0_), channel_id=1, source_target_pairs={{0,1},{1,0},{2,3},{3,2},{4,5},{5,4},{6,7},{7,6},{8,9},{9,8},{10,11... | collective-permute-start | bytes 73736 | tf_op jit(solution)/shard_map/ppermute | solution.py:367
  4.2 6.4 %collective-permute-start.6 = (bf16[8,8320]{1,0:T(8,128)(2,1)S(1)}, bf16[8,8320]{1,0:T(8,128)(2,1)S(1)}, u32[]{:S(2)}, u32[]{:S(2)}) collective-permute-start(bf16[8,8320]{1,0:T(8,128)(2,1)S(1)} %get-tuple-element.18.refs_0_), channel_id=1, source_target_pairs={{0,24},{4,28},{8,16},{12,20},{16,8},{20,12},{24,0},{28,4},{1,25},{... | collective-permute-start | bytes 399368 | tf_op jit(solution)/shard_map/ppermute | solution.py:351
  6.6 6.4 %collective-permute-start = (bf16[8,8320]{1,0:T(8,128)(2,1)S(1)}, bf16[8,8320]{1,0:T(8,128)(2,1)S(1)}, u32[]{:S(2)}, u32[]{:S(2)}) collective-permute-start(bf16[8,8320]{1,0:T(8,128)(2,1)S(1)} %get-tuple-element.18.refs_0_), channel_id=1, source_target_pairs={{0,8},{4,20},{8,0},{12,28},{16,24},{20,4},{24,16},{28,12},{1,9},{5... | collective-permute-start | bytes 399368 | tf_op jit(solution)/shard_map/ppermute | solution.py:351
  7.1 5.8 %collective-permute-start.3 = (bf16[8,8320]{1,0:T(8,128)(2,1)S(1)}, bf16[8,8320]{1,0:T(8,128)(2,1)S(1)}, u32[]{:S(2)}, u32[]{:S(2)}) collective-permute-start(bf16[8,8320]{1,0:T(8,128)(2,1)S(1)} %get-tuple-element.21), channel_id=1, source_target_pairs={{0,16},{4,12},{8,24},{12,4},{16,0},{20,28},{24,8},{28,20},{1,17},{... | collective-permute-start | bytes 399368 | tf_op jit(solution)/shard_map/ppermute | solution.py:351
  7.9 6.7 %slice-start = ((s8[8388608]{0:T(1024)(128)(4,1)}), s8[4194304]{0:T(1024)(128)(4,1)S(1)}, s32[]{:S(2)}) async-start(s8[8388608]{0:T(1024)(128)(4,1)} %bitcast.3), calls=%async_computation | async-start | bytes 8388608
  7.9 6.8 %slice-start.1 = ((s8[8388608]{0:T(1024)(128)(4,1)}), s8[4194304]{0:T(1024)(128)(4,1)S(1)}, s32[]{:S(2)}) async-start(s8[8388608]{0:T(1024)(128)(4,1)} %bitcast.3), calls=%async_computation.1 | async-start | bytes 8388608
  7.9 6.8 %copy-start = (s32[512]{0:T(512)S(1)}, s32[512]{0:T(512)}, u32[]{:S(2)}) copy-start(s32[512]{0:T(512)} %param.11) | copy-start | bytes 6148
  7.9 5.5 %collective-permute-start.8 = (bf16[2,2,48,128]{3,2,1,0:T(8,128)(2,1)S(1)}, bf16[2,2,48,128]{3,2,1,0:T(8,128)(2,1)S(1)}, u32[]{:S(2)}, u32[]{:S(2)}) collective-permute-start(bf16[2,2,48,128]{3,2,1,0:T(8,128)(2,1)S(1)} %get-tuple-element.22), channel_id=1, source_target_pairs={{0,2},{1,3},{2,0},{3,1},{4,6},{5,7},{6,4},{7,5},{8,10},{9,11},{10,... | collective-permute-start | bytes 147464 | tf_op jit(solution)/shard_map/ppermute | solution.py:367
  10.5 3.0 %collective-permute-start.5 = (bf16[8,8320]{1,0:T(8,128)(2,1)S(1)}, bf16[8,8320]{1,0:T(8,128)(2,1)S(1)}, u32[]{:S(2)}, u32[]{:S(2)}) collective-permute-start(bf16[8,8320]{1,0:T(8,128)(2,1)S(1)} %get-tuple-element.18.refs_0_), channel_id=1, source_target_pairs={{0,4},{4,0},{8,12},{12,8},{16,20},{20,16},{24,28},{28,24},{1,5},{5... | collective-permute-start | bytes 399368 | tf_op jit(solution)/shard_map/ppermute | solution.py:351
  10.6 2.9 %collective-permute-start.7 = (bf16[8,8320]{1,0:T(8,128)(2,1)S(1)}, bf16[8,8320]{1,0:T(8,128)(2,1)S(1)}, u32[]{:S(2)}, u32[]{:S(2)}) collective-permute-start(bf16[8,8320]{1,0:T(8,128)(2,1)S(1)} %collective-permute-done.6.refs_2_), channel_id=1, source_target_pairs={{0,4},{4,0},{8,12},{12,8},{16,20},{20,16},{24,28},{28,24},{1,5},{5... | collective-permute-start | bytes 399368 | tf_op jit(solution)/shard_map/ppermute | solution.py:351
  13.0 1.7 %collective-permute-start.1 = (bf16[8,8320]{1,0:T(8,128)(2,1)S(1)}, bf16[8,8320]{1,0:T(8,128)(2,1)S(1)}, u32[]{:S(2)}, u32[]{:S(2)}) collective-permute-start(bf16[8,8320]{1,0:T(8,128)(2,1)S(1)} %collective-permute-done.refs_0_), channel_id=1, source_target_pairs={{0,4},{4,0},{8,12},{12,8},{16,20},{20,16},{24,28},{28,24},{1,5},{5... | collective-permute-start | bytes 399368 | tf_op jit(solution)/shard_map/ppermute | solution.py:351
  13.0 1.7 %collective-permute-start.4 = (bf16[8,8320]{1,0:T(8,128)(2,1)S(1)}, bf16[8,8320]{1,0:T(8,128)(2,1)S(1)}, u32[]{:S(2)}, u32[]{:S(2)}) collective-permute-start(bf16[8,8320]{1,0:T(8,128)(2,1)S(1)} %collective-permute-done.3.refs_2_), channel_id=1, source_target_pairs={{0,4},{4,0},{8,12},{12,8},{16,20},{20,16},{24,28},{28,24},{1,5},{5... | collective-permute-start | bytes 399368 | tf_op jit(solution)/shard_map/ppermute | solution.py:351
  18.3 4.7 %collective-permute-start.11 = (bf16[2,8,512]{2,1,0:T(8,128)(2,1)S(1)}, bf16[2,8,512]{2,1,0:T(8,128)(2,1)S(1)}, u32[]{:S(2)}, u32[]{:S(2)}) collective-permute-start(bf16[2,8,512]{2,1,0:T(8,128)(2,1)S(1)} %get-tuple-element.28), channel_id=1, source_target_pairs={{0,24},{4,28},{8,16},{12,20},{16,8},{20,12},{24,0},{28,4},{1,25},{... | collective-permute-start | bytes 49160 | tf_op jit(solution)/shard_map/ppermute | solution.py:351
  20.5 3.7 %collective-permute-start.12 = (bf16[2,8,512]{2,1,0:T(8,128)(2,1)S(1)}, bf16[2,8,512]{2,1,0:T(8,128)(2,1)S(1)}, u32[]{:S(2)}, u32[]{:S(2)}) collective-permute-start(bf16[2,8,512]{2,1,0:T(8,128)(2,1)S(1)} %get-tuple-element.29), channel_id=1, source_target_pairs={{0,16},{4,20},{8,24},{12,28},{16,0},{20,4},{24,8},{28,12},{1,17},{... | collective-permute-start | bytes 49160 | tf_op jit(solution)/shard_map/ppermute | solution.py:351
  21.3 3.1 %collective-permute-start.10 = (bf16[8,512]{1,0:T(8,128)(2,1)S(1)}, bf16[8,512]{1,0:T(8,128)(2,1)S(1)}, u32[]{:S(2)}, u32[]{:S(2)}) collective-permute-start(bf16[8,512]{1,0:T(8,128)(2,1)S(1)} %get-tuple-element.27), channel_id=1, source_target_pairs={{0,12},{4,8},{8,4},{12,0},{16,28},{20,24},{24,20},{28,16},{1,13},{... | collective-permute-start | bytes 24584 | tf_op jit(solution)/shard_map/ppermute | solution.py:351
  21.3 3.7 %collective-permute-start.9 = (bf16[8,512]{1,0:T(8,128)(2,1)S(1)}, bf16[8,512]{1,0:T(8,128)(2,1)S(1)}, u32[]{:S(2)}, u32[]{:S(2)}) collective-permute-start(bf16[8,512]{1,0:T(8,128)(2,1)S(1)} %get-tuple-element.26), channel_id=1, source_target_pairs={{0,8},{4,12},{8,0},{12,4},{16,24},{20,28},{24,16},{28,20},{1,9},{5... | collective-permute-start | bytes 24584 | tf_op jit(solution)/shard_map/ppermute | solution.py:351
  24.3 1.2 %collective-permute-start.13 = (bf16[3,8,512]{2,1,0:T(8,128)(2,1)S(1)}, bf16[3,8,512]{2,1,0:T(8,128)(2,1)S(1)}, u32[]{:S(2)}, u32[]{:S(2)}) collective-permute-start(bf16[3,8,512]{2,1,0:T(8,128)(2,1)S(1)} %shard_map.70), channel_id=1, source_target_pairs={{0,4},{4,0},{8,12},{12,8},{16,20},{20,16},{24,28},{28,24},{1,5},{5... | collective-permute-start | bytes 73736 | tf_op jit(solution)/shard_map/ppermute | solution.py:351

commit v4 on v3

--- a/solution.py
+++ b/solution.py
@@ -54,7 +54,7 @@
         pltpu.make_async_copy(q_hbm, row_ref.at[:, :width], sems.at[3]),
         pltpu.make_async_copy(q_hbm, again_ref.at[:, :width], sems.at[4]),
     ]
-    for copy in copies:
+    for copy in copies[::-1]:
         copy.start()
     copies[2].wait()
     square = (rows, rows)
@@ -96,31 +96,30 @@
     )(*(pltpu.with_memory_space_constraint(x, pltpu.HBM) for x in (queries, block_ids, left, right)))
 
 
-def prepare(slots, left_all, right_all, in_s, out_s, prep_ref):
+def prepare(slots, left_all, right_all, in_s, mid_s, out_s, prep_ref):
     rows = slots[0].shape[0]
     order_a = left_all.shape[1]
     blocks = left_all.shape[0] // order_a
     order_b = right_all.shape[1] // blocks
     width = order_a * order_b
     pair = 2 * rows
+
+    def label_of(group, n):
+        row = slots[2 * group + n // rows][n % rows : n % rows + 1, width:]
+        return row.astype(F32)
+
     for group in range(len(slots) // 2):
-        for half in range(2):
-            ref = slots[2 * group + half]
-            for a in range(order_a):
-                in_s[a * pair + half * rows : a * pair + half * rows + rows, :] = ref[
-                    :, a * order_b : (a + 1) * order_b
-                ].astype(F32)
+        both = slots[2 * group : 2 * group + 2]
+        tiles = [
+            jnp.concatenate([ref[:, a * order_b : (a + 1) * order_b] for ref in both], axis=0) for a in range(order_a)
+        ]
+        in_s[group] = jnp.swapaxes(jnp.stack(tiles), 0, 1)
+    for group in range(len(slots) // 2):
         for n in range(0, pair, 2):
-            ref = slots[2 * group + n // rows]
-            x = jnp.concatenate(
-                [in_s[pl.ds(n + j, order_a, stride=pair), :].astype(BF16) for j in range(2)], axis=1
-            )
+            x = jnp.concatenate([in_s[group, n + j] for j in range(2)], axis=1)
             inner = jnp.dot(left_all, x, preferred_element_type=F32)
-            split = []
-            ids = []
             for j in range(2):
-                label = ref[(n + j) % rows : (n + j) % rows + 1, width:].astype(F32)
-                ids.append(label)
+                label = label_of(group, n + j)
                 one = inner[:order_a, j * order_b : (j + 1) * order_b]
                 for k in range(1, blocks):
                     one = jnp.where(
@@ -129,22 +128,23 @@
                         one,
                     )
                 high = one.astype(BF16)
-                low = (one - high.astype(F32)).astype(BF16)
-                split.append(jnp.concatenate([high, low], axis=1))
-            outer = jnp.dot(jnp.concatenate(split, axis=0), right_all, preferred_element_type=F32)
-            for j in range(2):
-                one = outer[j * order_a : (j + 1) * order_a, :order_b]
-                for k in range(1, blocks):
-                    one = jnp.where(
-                        ids[j] > k - 0.5,
-                        outer[j * order_a : (j + 1) * order_a, k * order_b : (k + 1) * order_b],
-                        one,
-                    )
-                out_s[pl.ds(n + j, order_a, stride=pair), :] = one
+                mid_s[group, n + j, :, :order_b] = high
+                mid_s[group, n + j, :, order_b:] = (one - high.astype(F32)).astype(BF16)
+    for group in range(len(slots) // 2):
+        middle = mid_s[group].reshape(pair * order_a, 2 * order_b)
+        outer = jnp.dot(middle, right_all, preferred_element_type=F32)
+        for n in range(pair):
+            label = label_of(group, n)
+            one = outer[n * order_a : (n + 1) * order_a, :order_b]
+            for k in range(1, blocks):
+                one = jnp.where(
+                    label > k - 0.5, outer[n * order_a : (n + 1) * order_a, k * order_b : (k + 1) * order_b], one
+                )
+            out_s[group, n] = one.astype(BF16)
+    for group in range(len(slots) // 2):
+        turned = jnp.swapaxes(out_s[group], 0, 1)
         for a in range(order_a):
-            prep_ref[group * pair : (group + 1) * pair, a * order_b : (a + 1) * order_b] = out_s[
-                a * pair : (a + 1) * pair, :
-            ].astype(BF16)
+            prep_ref[group * pair : (group + 1) * pair, a * order_b : (a + 1) * order_b] = turned[a]
 
 
 def factor_kernel(order_a, order_b, steps, *refs):
@@ -178,14 +178,14 @@
         in_specs=[VMEM] * len(factors),
         out_specs=(VMEM, VMEM),
         compiler_params=pltpu.CompilerParams(vmem_limit_bytes=8 << 20),
-        cost_estimate=pl.CostEstimate(flops=10**10, bytes_accessed=10**6, transcendentals=0),
+        cost_estimate=pl.CostEstimate(flops=6*10**9, bytes_accessed=10**6, transcendentals=0),
     )(*factors)
 
 
 def early_kernel(nslots, *refs):
     slots = refs[:nslots]
-    left_ref, right_ref, prep_ref, in_s, out_s = refs[nslots:]
-    prepare(slots, left_ref[...], right_ref[...], in_s, out_s, prep_ref)
+    left_ref, right_ref, prep_ref, in_s, mid_s, out_s = refs[nslots:]
+    prepare(slots, left_ref[...], right_ref[...], in_s, mid_s, out_s, prep_ref)
 
 
 def early(slots, left_all, right_all, order_a, order_b):
@@ -197,7 +197,9 @@
         out_shape=jax.ShapeDtypeStruct((total, width), BF16),
         in_specs=[VMEM] * (len(slots) + 2),
         out_specs=VMEM,
-        scratch_shapes=[pltpu.VMEM((order_a * 2 * rows, order_b), F32)] * 2,
+        scratch_shapes=[
+            pltpu.VMEM((len(slots) // 2, 2 * rows, order_a, wide * order_b), BF16) for wide in (1, 2, 1)
+        ],
         compiler_params=pltpu.CompilerParams(vmem_limit_bytes=SOME_VMEM),
         cost_estimate=pl.CostEstimate(flops=8 * total * width * order_b, bytes_accessed=4 * total * width, transcendentals=0),
     )(*slots, left_all, right_all)
@@ -206,25 +208,27 @@
 def score_kernel(nslots, *refs):
     slots = refs[:nslots]
     early_ref, left_ref, right_ref, clips_ref, len_ref = refs[nslots : nslots + 5]
-    home_ref, near_ref, x_ref, cross_ref, y_ref, d_ref, in_s, out_s, prep_s, all_s = refs[nslots + 5 :]
+    home_ref, near_ref, x_ref, cross_ref, y_ref, d_ref, in_s, mid_s, out_s, prep_s, all_s = refs[nslots + 5 :]
     width = clips_ref.shape[1]
     rows = slots[0].shape[0]
-    prepare(slots, left_ref[...], right_ref[...], in_s, out_s, prep_s)
-    queries = jnp.concatenate([early_ref[...], prep_s[...]], axis=0)
-    raw = lax.dot_general(clips_ref[...], queries, (((1,), (1,)), ((), ())), preferred_element_type=F32)
-    factor = lax.rsqrt(F32(width) * len_ref[...].astype(F32))
-    scores = raw.T * factor
-    core = lax.rem(lax.axis_index("own"), CORES)
-    for j, (mine, other) in enumerate(((0, 0), (3, 3), (1 + core, 2 - core), (2 - core, 1 + core))):
-        at = 2 * j * rows
-        all_s[mine, core] = scores[at : at + rows].astype(BF16)
-        all_s[other, 1 - core] = scores[at + rows : at + 2 * rows].astype(BF16)
-    home_ref[...] = scores[:rows]
-    near_ref[...] = all_s[0, 1 - core]
-    x_ref[...] = all_s[1, core]
-    cross_ref[...] = all_s[1, 1 - core]
-    y_ref[...] = all_s[2]
-    d_ref[...] = all_s[3]
+    prepare(slots, left_ref[...], right_ref[...], in_s, mid_s, out_s, prep_s)
+    @pl.when(lax.axis_index("qry") >= 0)
+    def _():
+        queries = jnp.concatenate([early_ref[...], prep_s[...]], axis=0)
+        raw = lax.dot_general(clips_ref[...], queries, (((1,), (1,)), ((), ())), preferred_element_type=F32)
+        factor = lax.rsqrt(F32(width) * len_ref[...].astype(F32))
+        scores = raw.T * factor
+        core = lax.rem(lax.axis_index("own"), CORES)
+        for j, (mine, other) in enumerate(((0, 0), (3, 3), (1 + core, 2 - core), (2 - core, 1 + core))):
+            at = 2 * j * rows
+            all_s[mine, core] = scores[at : at + rows].astype(BF16)
+            all_s[other, 1 - core] = scores[at + rows : at + 2 * rows].astype(BF16)
+        home_ref[...] = scores[:rows]
+        near_ref[...] = all_s[0, 1 - core]
+        x_ref[...] = all_s[1, core]
+        cross_ref[...] = all_s[1, 1 - core]
+        y_ref[...] = all_s[2]
+        d_ref[...] = all_s[3]
 
 
 def score(slots, prepared, left_all, right_all, clip_grads, lengths):
@@ -241,7 +245,9 @@
         ),
         in_specs=[VMEM] * (len(slots) + 5),
         out_specs=(VMEM,) * 6,
-        scratch_shapes=[pltpu.VMEM((order_a * 2 * rows, width // order_a), F32)] * 2
+        scratch_shapes=[
+            pltpu.VMEM((len(slots) // 2, 2 * rows, order_a, wide * width // order_a), BF16) for wide in (1, 2, 1)
+        ]
         + [pltpu.VMEM((len(slots) * rows, width), BF16), pltpu.VMEM((4, 2, rows, clips), BF16)],
         compiler_params=pltpu.CompilerParams(vmem_limit_bytes=SOME_VMEM),
         cost_estimate=pl.CostEstimate(

time: 26.3 us -> 25.8 us (0.981)
  Pallas kernels: 6.43 us -> 5.88 us
    pallas_call x1, Pallas kernels: 3.54 us -> 3.25 us  [score(): pl.pallas_call(lambda *refs: score_kernel(len(slots), *refs), out_shape=(...]
  transfers between devices with their start and end apart: 14 -> 14, of which waited for: 7 -> 8; matrix products, arithmetic and copies ran while one was open for 0% -> 0% of each run, Pallas kernels for 4% -> 4%
where the time goes in v4:
time: 25.8 us; the launch traced here: 25.6 us
  starting transfers between devices  14.9 us (58%)
  Pallas kernels  5.88 us (23%)
  waiting for transfers between devices  4.76 us (18%)
    ppermute x12, starting transfers between devices, move(): lax.ppermute(x, 'own', [(i, to(i // CORES, i % CORES)) for i in range(siz...  9.19 us
    ppermute x2, starting transfers between devices, per_device_exchanged(): got = lax.ppermute(held, 'qry', [(i, i ^ step) for i in range(planes)])  5.68 us
    ppermute x12, waiting for transfers between devices, move(): lax.ppermute(x, 'own', [(i, to(i // CORES, i % CORES)) for i in range(siz...  4.75 us
    pallas_call x1, Pallas kernels, score(): pl.pallas_call(lambda *refs: score_kernel(len(slots), *refs), out_shape=(...  3.25 us
    pallas_call x1, Pallas kernels, pack(): pl.pallas_call(pack_kernel, out_shape=(jax.ShapeDtypeStruct((rows, width...  1.02 us
    pallas_call x1, Pallas kernels, early(): pl.pallas_call(lambda *refs: early_kernel(len(slots), *refs), out_shape=j...  0.88 us
    pallas_call x1, Pallas kernels, place(): pl.pallas_call(place_kernel, out_shape=jax.ShapeDtypeStruct(wide, F32), i...  0.68 us
  transfers between devices with their start and end apart: 14, of which 8 were waited for; matrix products, arithmetic and copies ran while one was open for 0% of the time, Pallas kernels for 4%

profile of v4, /device:TPU:0, one launch (start us, length us, event | category | flops | bytes accessed | tf_op | source)
XLA Modules:
  0.0 25.6 jit_solution(6067923429980958327)
XLA Ops:
  0.0 1.0 %shard_map.64 = (bf16[8,8320]{1,0:T(8,128)(2,1)S(1)}, bf16[8,8320]{1,0:T(8,128)(2,1)S(1)}, bf16[1,2,48,128]{3,2,1,0:T(8,128)(2,1)S(1)}) custom-call(bf16[8,8192]{1,0:T(8,128)(2,1)} %bitcast.6, s32[1,8]{1,0:T(1,128)} %ids_hbm.1, bf16[2,16,64]{2,1,0:T(8,128)(2,1)} %left_hbm.1, bf16[2,32,128]{2,1,0:T(8,128)(2,1)} %right_hbm.1), custom_call_target="tpu_custom_call" | custom-call | tf_op jit(solution)/shard_map/pallas_call | solution.py:80
  1.0 3.1 %collective-permute-start.2 = (bf16[1,2,48,128]{3,2,1,0:T(8,128)(2,1)S(1)}, bf16[1,2,48,128]{3,2,1,0:T(8,128)(2,1)S(1)}, u32[]{:S(2)}, u32[]{:S(2)}) collective-permute-start(bf16[1,2,48,128]{3,2,1,0:T(8,128)(2,1)S(1)} %get-tuple-element.19.first_ref.refs_0_), channel_id=1, source_target_pairs={{0,1},{1,0},{2,3},{3,2},{4,5},{5,4},{6,7},{7,6},{8,9},{9,8},{10,11... | collective-permute-start | bytes 73736 | tf_op jit(solution)/shard_map/ppermute | solution.py:373
  4.1 2.4 %collective-permute-start.6 = (bf16[8,8320]{1,0:T(8,128)(2,1)S(1)}, bf16[8,8320]{1,0:T(8,128)(2,1)S(1)}, u32[]{:S(2)}, u32[]{:S(2)}) collective-permute-start(bf16[8,8320]{1,0:T(8,128)(2,1)S(1)} %get-tuple-element.18.refs_0_), channel_id=1, source_target_pairs={{0,24},{4,28},{8,16},{12,20},{16,8},{20,12},{24,0},{28,4},{1,25},{... | collective-permute-start | bytes 399368 | tf_op jit(solution)/shard_map/ppermute | solution.py:357
  6.6 0.5 %collective-permute-start = (bf16[8,8320]{1,0:T(8,128)(2,1)S(1)}, bf16[8,8320]{1,0:T(8,128)(2,1)S(1)}, u32[]{:S(2)}, u32[]{:S(2)}) collective-permute-start(bf16[8,8320]{1,0:T(8,128)(2,1)S(1)} %get-tuple-element.18.refs_0_), channel_id=1, source_target_pairs={{0,8},{4,20},{8,0},{12,28},{16,24},{20,4},{24,16},{28,12},{1,9},{5... | collective-permute-start | bytes 399368 | tf_op jit(solution)/shard_map/ppermute | solution.py:357
  7.1 0.8 %collective-permute-start.3 = (bf16[8,8320]{1,0:T(8,128)(2,1)S(1)}, bf16[8,8320]{1,0:T(8,128)(2,1)S(1)}, u32[]{:S(2)}, u32[]{:S(2)}) collective-permute-start(bf16[8,8320]{1,0:T(8,128)(2,1)S(1)} %get-tuple-element.21), channel_id=1, source_target_pairs={{0,16},{4,12},{8,24},{12,4},{16,0},{20,28},{24,8},{28,20},{1,17},{... | collective-permute-start | bytes 399368 | tf_op jit(solution)/shard_map/ppermute | solution.py:357
  7.9 2.6 %collective-permute-start.8 = (bf16[2,2,48,128]{3,2,1,0:T(8,128)(2,1)S(1)}, bf16[2,2,48,128]{3,2,1,0:T(8,128)(2,1)S(1)}, u32[]{:S(2)}, u32[]{:S(2)}) collective-permute-start(bf16[2,2,48,128]{3,2,1,0:T(8,128)(2,1)S(1)} %get-tuple-element.22), channel_id=1, source_target_pairs={{0,2},{1,3},{2,0},{3,1},{4,6},{5,7},{6,4},{7,5},{8,10},{9,11},{10,... | collective-permute-start | bytes 147464 | tf_op jit(solution)/shard_map/ppermute | solution.py:373
  10.5 0.1 collective-permute-done.6.refs_2_
  10.6 0.5 %collective-permute-start.7 = (bf16[8,8320]{1,0:T(8,128)(2,1)S(1)}, bf16[8,8320]{1,0:T(8,128)(2,1)S(1)}, u32[]{:S(2)}, u32[]{:S(2)}) collective-permute-start(bf16[8,8320]{1,0:T(8,128)(2,1)S(1)} %collective-permute-done.6.refs_2_), channel_id=1, source_target_pairs={{0,4},{4,0},{8,12},{12,8},{16,20},{20,16},{24,28},{28,24},{1,5},{5... | collective-permute-start | bytes 399368 | tf_op jit(solution)/shard_map/ppermute | solution.py:357
  11.0 1.9 %collective-permute-done.refs_0_ = bf16[8,8320]{1,0:T(8,128)(2,1)S(1)} collective-permute-done((bf16[8,8320]{1,0:T(8,128)(2,1)S(1)}, bf16[8,8320]{1,0:T(8,128)(2,1)S(1)}, u32[]{:S(2)}, u32[]{:S(2)}) %collective-permute-start) | collective-permute-done | bytes 133152 | tf_op jit(solution)/shard_map/ppermute | solution.py:357
  12.9 0.0 collective-permute-start.1
  12.9 0.0 collective-permute-done.3.refs_2_
  12.9 0.5 %collective-permute-start.4 = (bf16[8,8320]{1,0:T(8,128)(2,1)S(1)}, bf16[8,8320]{1,0:T(8,128)(2,1)S(1)}, u32[]{:S(2)}, u32[]{:S(2)}) collective-permute-start(bf16[8,8320]{1,0:T(8,128)(2,1)S(1)} %collective-permute-done.3.refs_2_), channel_id=1, source_target_pairs={{0,4},{4,0},{8,12},{12,8},{16,20},{20,16},{24,28},{28,24},{1,5},{5... | collective-permute-start | bytes 399368 | tf_op jit(solution)/shard_map/ppermute | solution.py:357
  13.5 0.9 %shard_map.67.refs_4_ = bf16[32,8192]{1,0:T(8,128)(2,1)S(1)} custom-call(bf16[8,8320]{1,0:T(8,128)(2,1)S(1)} %get-tuple-element.18.refs_0_, bf16[8,8320]{1,0:T(8,128)(2,1)S(1)} %collective-permute-done.5.refs_1_, bf16[8,8320]{1,0:T(8,128)(2,1)S(1)} %collective-permute-done.6.refs_2_, bf16[8,8320]{1,0:T(8,128)(2,1)S(1)} %collective-permute-done.7.refs_3_, ...), custom_call_target="tpu_custom_call" | custom-call | flops 268435456 | bytes 1048576 | tf_op jit(solution)/shard_map/pallas_call | solution.py:195
  14.4 0.1 collective-permute-done.4.refs_3_
  14.5 3.3 %shard_map.68 = (f32[8,512]{1,0:T(8,128)S(1)}, bf16[8,512]{1,0:T(8,128)(2,1)S(1)}, bf16[8,512]{1,0:T(8,128)(2,1)S(1)}, bf16[8,512]{1,0:T(8,128)(2,1)S(1)}, bf16[...) custom-call(bf16[8,8320]{1,0:T(8,128)(2,1)S(1)} %collective-permute-done.refs_0_, ...), custom_call_target="tpu_custom_call" | custom-call | flops 1585446912 | bytes 8388608 | tf_op jit(solution)/shard_map/pallas_call | solution.py:239
  17.7 2.2 %collective-permute-start.11 = (bf16[2,8,512]{2,1,0:T(8,128)(2,1)S(1)}, bf16[2,8,512]{2,1,0:T(8,128)(2,1)S(1)}, u32[]{:S(2)}, u32[]{:S(2)}) collective-permute-start(bf16[2,8,512]{2,1,0:T(8,128)(2,1)S(1)} %get-tuple-element.28), channel_id=1, source_target_pairs={{0,24},{4,28},{8,16},{12,20},{16,8},{20,12},{24,0},{28,4},{1,25},{... | collective-permute-start | bytes 49160 | tf_op jit(solution)/shard_map/ppermute | solution.py:357
  20.0 0.8 %collective-permute-start.12 = (bf16[2,8,512]{2,1,0:T(8,128)(2,1)S(1)}, bf16[2,8,512]{2,1,0:T(8,128)(2,1)S(1)}, u32[]{:S(2)}, u32[]{:S(2)}) collective-permute-start(bf16[2,8,512]{2,1,0:T(8,128)(2,1)S(1)} %get-tuple-element.29), channel_id=1, source_target_pairs={{0,16},{4,20},{8,24},{12,28},{16,0},{20,4},{24,8},{28,12},{1,17},{... | collective-permute-start | bytes 49160 | tf_op jit(solution)/shard_map/ppermute | solution.py:357
  20.8 1.4 %collective-permute-start.9 = (bf16[8,512]{1,0:T(8,128)(2,1)S(1)}, bf16[8,512]{1,0:T(8,128)(2,1)S(1)}, u32[]{:S(2)}, u32[]{:S(2)}) collective-permute-start(bf16[8,512]{1,0:T(8,128)(2,1)S(1)} %get-tuple-element.26), channel_id=1, source_target_pairs={{0,8},{4,12},{8,0},{12,4},{16,24},{20,28},{24,16},{28,20},{1,9},{5... | collective-permute-start | bytes 24584 | tf_op jit(solution)/shard_map/ppermute | solution.py:357
  22.2 0.2 collective-permute-done.11.d_ref
  22.5 1.3 %collective-permute-done.12.y_ref = bf16[2,8,512]{2,1,0:T(8,128)(2,1)S(1)} collective-permute-done((bf16[2,8,512]{2,1,0:T(8,128)(2,1)S(1)}, bf16[2,8,512]{2,1,0:T(8,128)(2,1)S(1)}, u32[]{:S(2)}, u32[]{:S(2)}) %collective-permute-start.12) | collective-permute-done | bytes 16416 | tf_op jit(solution)/shard_map/ppermute | solution.py:357
  23.7 0.2 collective-permute-done.10.cross_ref
  23.9 0.6 %collective-permute-done.9.x_ref = bf16[8,512]{1,0:T(8,128)(2,1)S(1)} collective-permute-done((bf16[8,512]{1,0:T(8,128)(2,1)S(1)}, bf16[8,512]{1,0:T(8,128)(2,1)S(1)}, u32[]{:S(2)}, u32[]{:S(2)}) %collective-permute-start.9) | collective-permute-done | bytes 8224 | tf_op jit(solution)/shard_map/ppermute | solution.py:357
  24.5 0.4 %collective-permute-done.13.relayed_ref = bf16[3,8,512]{2,1,0:T(8,128)(2,1)S(1)} collective-permute-done((bf16[3,8,512]{2,1,0:T(8,128)(2,1)S(1)}, bf16[3,8,512]{2,1,0:T(8,128)(2,1)S(1)}, u32[]{:S(2)}, u32[]{:S(2)}) %collective-permute-start.13) | collective-permute-done | bytes 24608 | tf_op jit(solution)/shard_map/ppermute | solution.py:357
  24.9 0.7 %shard_map.71 = f32[8,4096]{1,0:T(8,128)} custom-call(f32[3,8,512]{2,1,0:T(8,128)S(1)} %shard_map.69.wide_ref, bf16[2,8,512]{2,1,0:T(8,128)(2,1)S(1)} %collective-permute-done.11.d_ref, bf16[2,8,512]{2,1,0:T(8,128)(2,1)S(1)} %collective-permute-done.12.y_ref, bf16[3,8,512]{2,1,0:T(8,128)(2,1)S(1)} %collective-permute-done.13.relayed_ref), custom_call_target="tpu_custom_call" | custom-call | tf_op jit(solution)/shard_map/pallas_call | solution.py:343
  (19 shorter events, 0.1 us)
Async XLA Ops:
  1.0 6.1 %collective-permute-start.2 = (bf16[1,2,48,128]{3,2,1,0:T(8,128)(2,1)S(1)}, bf16[1,2,48,128]{3,2,1,0:T(8,128)(2,1)S(1)}, u32[]{:S(2)}, u32[]{:S(2)}) collective-permute-start(bf16[1,2,48,128]{3,2,1,0:T(8,128)(2,1)S(1)} %get-tuple-element.19.first_ref.refs_0_), channel_id=1, source_target_pairs={{0,1},{1,0},{2,3},{3,2},{4,5},{5,4},{6,7},{7,6},{8,9},{9,8},{10,11... | collective-permute-start | bytes 73736 | tf_op jit(solution)/shard_map/ppermute | solution.py:373
  4.1 6.4 %collective-permute-start.6 = (bf16[8,8320]{1,0:T(8,128)(2,1)S(1)}, bf16[8,8320]{1,0:T(8,128)(2,1)S(1)}, u32[]{:S(2)}, u32[]{:S(2)}) collective-permute-start(bf16[8,8320]{1,0:T(8,128)(2,1)S(1)} %get-tuple-element.18.refs_0_), channel_id=1, source_target_pairs={{0,24},{4,28},{8,16},{12,20},{16,8},{20,12},{24,0},{28,4},{1,25},{... | collective-permute-start | bytes 399368 | tf_op jit(solution)/shard_map/ppermute | solution.py:357
  6.6 6.4 %collective-permute-start = (bf16[8,8320]{1,0:T(8,128)(2,1)S(1)}, bf16[8,8320]{1,0:T(8,128)(2,1)S(1)}, u32[]{:S(2)}, u32[]{:S(2)}) collective-permute-start(bf16[8,8320]{1,0:T(8,128)(2,1)S(1)} %get-tuple-element.18.refs_0_), channel_id=1, source_target_pairs={{0,8},{4,20},{8,0},{12,28},{16,24},{20,4},{24,16},{28,12},{1,9},{5... | collective-permute-start | bytes 399368 | tf_op jit(solution)/shard_map/ppermute | solution.py:357
  7.1 5.8 %collective-permute-start.3 = (bf16[8,8320]{1,0:T(8,128)(2,1)S(1)}, bf16[8,8320]{1,0:T(8,128)(2,1)S(1)}, u32[]{:S(2)}, u32[]{:S(2)}) collective-permute-start(bf16[8,8320]{1,0:T(8,128)(2,1)S(1)} %get-tuple-element.21), channel_id=1, source_target_pairs={{0,16},{4,12},{8,24},{12,4},{16,0},{20,28},{24,8},{28,20},{1,17},{... | collective-permute-start | bytes 399368 | tf_op jit(solution)/shard_map/ppermute | solution.py:357
  7.9 6.6 %slice-start = ((s8[8388608]{0:T(1024)(128)(4,1)}), s8[4194304]{0:T(1024)(128)(4,1)S(1)}, s32[]{:S(2)}) async-start(s8[8388608]{0:T(1024)(128)(4,1)} %bitcast.3), calls=%async_computation | async-start | bytes 8388608
  7.9 6.6 %slice-start.1 = ((s8[8388608]{0:T(1024)(128)(4,1)}), s8[4194304]{0:T(1024)(128)(4,1)S(1)}, s32[]{:S(2)}) async-start(s8[8388608]{0:T(1024)(128)(4,1)} %bitcast.3), calls=%async_computation.1 | async-start | bytes 8388608
  7.9 6.6 %copy-start = (s32[512]{0:T(512)S(1)}, s32[512]{0:T(512)}, u32[]{:S(2)}) copy-start(s32[512]{0:T(512)} %param.11) | copy-start | bytes 6148
  7.9 5.5 %collective-permute-start.8 = (bf16[2,2,48,128]{3,2,1,0:T(8,128)(2,1)S(1)}, bf16[2,2,48,128]{3,2,1,0:T(8,128)(2,1)S(1)}, u32[]{:S(2)}, u32[]{:S(2)}) collective-permute-start(bf16[2,2,48,128]{3,2,1,0:T(8,128)(2,1)S(1)} %get-tuple-element.22), channel_id=1, source_target_pairs={{0,2},{1,3},{2,0},{3,1},{4,6},{5,7},{6,4},{7,5},{8,10},{9,11},{10,... | collective-permute-start | bytes 147464 | tf_op jit(solution)/shard_map/ppermute | solution.py:373
  10.5 3.0 %collective-permute-start.5 = (bf16[8,8320]{1,0:T(8,128)(2,1)S(1)}, bf16[8,8320]{1,0:T(8,128)(2,1)S(1)}, u32[]{:S(2)}, u32[]{:S(2)}) collective-permute-start(bf16[8,8320]{1,0:T(8,128)(2,1)S(1)} %get-tuple-element.18.refs_0_), channel_id=1, source_target_pairs={{0,4},{4,0},{8,12},{12,8},{16,20},{20,16},{24,28},{28,24},{1,5},{5... | collective-permute-start | bytes 399368 | tf_op jit(solution)/shard_map/ppermute | solution.py:357
  10.6 2.9 %collective-permute-start.7 = (bf16[8,8320]{1,0:T(8,128)(2,1)S(1)}, bf16[8,8320]{1,0:T(8,128)(2,1)S(1)}, u32[]{:S(2)}, u32[]{:S(2)}) collective-permute-start(bf16[8,8320]{1,0:T(8,128)(2,1)S(1)} %collective-permute-done.6.refs_2_), channel_id=1, source_target_pairs={{0,4},{4,0},{8,12},{12,8},{16,20},{20,16},{24,28},{28,24},{1,5},{5... | collective-permute-start | bytes 399368 | tf_op jit(solution)/shard_map/ppermute | solution.py:357
  12.9 1.5 %collective-permute-start.1 = (bf16[8,8320]{1,0:T(8,128)(2,1)S(1)}, bf16[8,8320]{1,0:T(8,128)(2,1)S(1)}, u32[]{:S(2)}, u32[]{:S(2)}) collective-permute-start(bf16[8,8320]{1,0:T(8,128)(2,1)S(1)} %collective-permute-done.refs_0_), channel_id=1, source_target_pairs={{0,4},{4,0},{8,12},{12,8},{16,20},{20,16},{24,28},{28,24},{1,5},{5... | collective-permute-start | bytes 399368 | tf_op jit(solution)/shard_map/ppermute | solution.py:357
  12.9 1.5 %collective-permute-start.4 = (bf16[8,8320]{1,0:T(8,128)(2,1)S(1)}, bf16[8,8320]{1,0:T(8,128)(2,1)S(1)}, u32[]{:S(2)}, u32[]{:S(2)}) collective-permute-start(bf16[8,8320]{1,0:T(8,128)(2,1)S(1)} %collective-permute-done.3.refs_2_), channel_id=1, source_target_pairs={{0,4},{4,0},{8,12},{12,8},{16,20},{20,16},{24,28},{28,24},{1,5},{5... | collective-permute-start | bytes 399368 | tf_op jit(solution)/shard_map/ppermute | solution.py:357
  17.7 4.7 %collective-permute-start.11 = (bf16[2,8,512]{2,1,0:T(8,128)(2,1)S(1)}, bf16[2,8,512]{2,1,0:T(8,128)(2,1)S(1)}, u32[]{:S(2)}, u32[]{:S(2)}) collective-permute-start(bf16[2,8,512]{2,1,0:T(8,128)(2,1)S(1)} %get-tuple-element.28), channel_id=1, source_target_pairs={{0,24},{4,28},{8,16},{12,20},{16,8},{20,12},{24,0},{28,4},{1,25},{... | collective-permute-start | bytes 49160 | tf_op jit(solution)/shard_map/ppermute | solution.py:357
  20.0 3.7 %collective-permute-start.12 = (bf16[2,8,512]{2,1,0:T(8,128)(2,1)S(1)}, bf16[2,8,512]{2,1,0:T(8,128)(2,1)S(1)}, u32[]{:S(2)}, u32[]{:S(2)}) collective-permute-start(bf16[2,8,512]{2,1,0:T(8,128)(2,1)S(1)} %get-tuple-element.29), channel_id=1, source_target_pairs={{0,16},{4,20},{8,24},{12,28},{16,0},{20,4},{24,8},{28,12},{1,17},{... | collective-permute-start | bytes 49160 | tf_op jit(solution)/shard_map/ppermute | solution.py:357
  20.8 3.1 %collective-permute-start.10 = (bf16[8,512]{1,0:T(8,128)(2,1)S(1)}, bf16[8,512]{1,0:T(8,128)(2,1)S(1)}, u32[]{:S(2)}, u32[]{:S(2)}) collective-permute-start(bf16[8,512]{1,0:T(8,128)(2,1)S(1)} %get-tuple-element.27), channel_id=1, source_target_pairs={{0,12},{4,8},{8,4},{12,0},{16,28},{20,24},{24,20},{28,16},{1,13},{... | collective-permute-start | bytes 24584 | tf_op jit(solution)/shard_map/ppermute | solution.py:357
  20.8 3.7 %collective-permute-start.9 = (bf16[8,512]{1,0:T(8,128)(2,1)S(1)}, bf16[8,512]{1,0:T(8,128)(2,1)S(1)}, u32[]{:S(2)}, u32[]{:S(2)}) collective-permute-start(bf16[8,512]{1,0:T(8,128)(2,1)S(1)} %get-tuple-element.26), channel_id=1, source_target_pairs={{0,8},{4,12},{8,0},{12,4},{16,24},{20,28},{24,16},{28,20},{1,9},{5... | collective-permute-start | bytes 24584 | tf_op jit(solution)/shard_map/ppermute | solution.py:357
  23.7 1.2 %collective-permute-start.13 = (bf16[3,8,512]{2,1,0:T(8,128)(2,1)S(1)}, bf16[3,8,512]{2,1,0:T(8,128)(2,1)S(1)}, u32[]{:S(2)}, u32[]{:S(2)}) collective-permute-start(bf16[3,8,512]{2,1,0:T(8,128)(2,1)S(1)} %shard_map.70), channel_id=1, source_target_pairs={{0,4},{4,0},{8,12},{12,8},{16,20},{20,16},{24,28},{28,24},{1,5},{5... | collective-permute-start | bytes 73736 | tf_op jit(solution)/shard_map/ppermute | solution.py:357

commit v5 on v4

--- a/solution.py
+++ b/solution.py
@@ -11,7 +11,6 @@
 SOME_VMEM = 16 << 20
 VMEM = pl.BlockSpec(memory_space=pltpu.VMEM)
 HBM = pl.BlockSpec(memory_space=pltpu.HBM)
-ANY = pl.BlockSpec(memory_space=pl.ANY)
 F32 = jnp.float32
 BF16 = jnp.bfloat16
 
@@ -44,33 +43,35 @@
     return lax.all_to_all(tiles * factor[None, None, :], "own", split_axis=1, concat_axis=2, tiled=True)
 
 
-def pack_kernel(q_hbm, ids_hbm, left_hbm, right_hbm, row_ref, again_ref, fac_ref, ids_s, left_s, right_s, sems):
+def pack_kernel(q_hbm, ids_hbm, left_hbm, right_hbm, row_ref, fac_ref, ids_s, left_s, sems):
     rows, width = q_hbm.shape
     blocks, cut, order_a = left_s.shape
     copies = [
-        pltpu.make_async_copy(left_hbm, left_s, sems.at[0]),
-        pltpu.make_async_copy(right_hbm, right_s, sems.at[1]),
-        pltpu.make_async_copy(ids_hbm, ids_s, sems.at[2]),
-        pltpu.make_async_copy(q_hbm, row_ref.at[:, :width], sems.at[3]),
-        pltpu.make_async_copy(q_hbm, again_ref.at[:, :width], sems.at[4]),
+        pltpu.make_async_copy(ids_hbm, ids_s, sems.at[1]),
+        pltpu.make_async_copy(left_hbm, left_s, sems.at[2]),
+        pltpu.make_async_copy(right_hbm, fac_ref.at[0, :, cut:, :], sems.at[3]),
     ]
-    for copy in copies[::-1]:
+    part = width // 4
+    copies = [
+        pltpu.make_async_copy(
+            q_hbm.at[:, i * part : (i + 1) * part], row_ref.at[:, i * part : (i + 1) * part], sems.at[4 + i]
+        )
+        for i in range(4)
+    ] + copies
+    for copy in copies:
         copy.start()
-    copies[2].wait()
+    fac_ref[0, :, :cut, order_a:] = jnp.zeros((blocks, cut, LANES - order_a), BF16)
     square = (rows, rows)
     diagonal = lax.broadcasted_iota(jnp.int32, square, 0) == lax.broadcasted_iota(jnp.int32, square, 1)
+    copies[4].wait()
     labels = jnp.where(diagonal, jnp.broadcast_to(ids_s[...].astype(F32), square), 0.0)
     column = jnp.sum(labels, axis=1, keepdims=True)
     column = jnp.broadcast_to(column, (rows, LANES)).astype(BF16)
     row_ref[:, width:] = column
-    again_ref[:, width:] = column
-    copies[0].wait()
-    copies[1].wait()
+    copies[5].wait()
     fac_ref[0, :, :cut, :order_a] = left_s[...]
-    fac_ref[0, :, :cut, order_a:] = jnp.zeros((blocks, cut, LANES - order_a), BF16)
-    fac_ref[0, :, cut:, :] = right_s[...]
-    copies[3].wait()
-    copies[4].wait()
+    for copy in copies[:4] + copies[6:]:
+        copy.wait()
 
 
 def pack(queries, block_ids, left, right):
@@ -81,16 +82,14 @@
         pack_kernel,
         out_shape=(
             jax.ShapeDtypeStruct((rows, width + LANES), BF16),
-            jax.ShapeDtypeStruct((rows, width + LANES), BF16),
             jax.ShapeDtypeStruct((1, blocks, depth, LANES), BF16),
         ),
         in_specs=[HBM] * 4,
-        out_specs=(VMEM,) * 3,
+        out_specs=(VMEM, VMEM),
         scratch_shapes=[
             pltpu.VMEM(block_ids.shape, block_ids.dtype),
             pltpu.VMEM(left.shape, left.dtype),
-            pltpu.VMEM(right.shape, right.dtype),
-            pltpu.SemaphoreType.DMA((5,)),
+            pltpu.SemaphoreType.DMA((8,)),
         ],
         compiler_params=pltpu.CompilerParams(vmem_limit_bytes=SOME_VMEM),
     )(*(pltpu.with_memory_space_constraint(x, pltpu.HBM) for x in (queries, block_ids, left, right)))
@@ -260,11 +259,11 @@
     return pltpu.with_memory_space_constraint(x, pltpu.HBM)
 
 
-def join_kernel(first_ref, second_ref, row_ref, both_ref, same_ref):
-    del row_ref, same_ref
+def join_kernel(first_ref, second_ref, row_ref, both_ref, again_ref):
     count = first_ref.shape[0]
     both_ref[:count] = first_ref[...]
     both_ref[count:] = second_ref[...]
+    again_ref[...] = row_ref[...]
 
 
 def join(first, second, row):
@@ -274,9 +273,8 @@
             jax.ShapeDtypeStruct((2 * first.shape[0],) + first.shape[1:], first.dtype),
             jax.ShapeDtypeStruct(row.shape, row.dtype),
         ),
-        in_specs=[VMEM, VMEM, ANY],
-        out_specs=(VMEM, ANY),
-        input_output_aliases={2: 1},
+        in_specs=[VMEM] * 3,
+        out_specs=(VMEM, VMEM),
         compiler_params=pltpu.CompilerParams(vmem_limit_bytes=8 << 20),
     )(first, second, row)
 
@@ -363,17 +361,17 @@
         return move(x, lambda chip, core: (chip ^ flips[core]) * CORES + core)
 
     flips_a, flips_b = (1, 2), (2, 1)
-    row, again, fac = pack(queries[0], block_ids, left_factor, right_factor)
+    row, fac = pack(queries[0], block_ids, left_factor, right_factor)
     slot_d = across(row, (3, 3))
     slot_a = across(row, flips_a)
     factors = [fac]
-    held = fac
+    held, again = fac, row
     step = 1
     while step < planes:
         got = lax.ppermute(held, "qry", [(i, i ^ step) for i in range(planes)])
         factors.append(got)
         if step * 2 < planes:
-            held, again = join(held, got, again)
+            held, again = join(held, got, row)
         step *= 2
     slot_b = across(again, flips_b)
     order_a, order_b = left_factor.shape[2], right_factor.shape[2]

time: 25.8 us -> 25.7 us (level)
  transfers between devices with their start and end apart: 14 -> 14, of which waited for: 8 -> 7; matrix products, arithmetic and copies ran while one was open for 0% -> 0% of each run, Pallas kernels for 4% -> 4%
where the time goes in v5:
time: 25.7 us; the launch traced here: 25.5 us
  starting transfers between devices  15 us (58%)
  Pallas kernels  5.76 us (22%)
  waiting for transfers between devices  4.64 us (18%)
    ppermute x12, starting transfers between devices, move(): lax.ppermute(x, 'own', [(i, to(i // CORES, i % CORES)) for i in range(siz...  9.31 us
    ppermute x2, starting transfers between devices, per_device_exchanged(): got = lax.ppermute(held, 'qry', [(i, i ^ step) for i in range(planes)])  5.68 us
    ppermute x12, waiting for transfers between devices, move(): lax.ppermute(x, 'own', [(i, to(i // CORES, i % CORES)) for i in range(siz...  4.64 us
    pallas_call x1, Pallas kernels, score(): pl.pallas_call(lambda *refs: score_kernel(len(slots), *refs), out_shape=(...  3.25 us
    pallas_call x1, Pallas kernels, pack(): pl.pallas_call(pack_kernel, out_shape=(jax.ShapeDtypeStruct((rows, width...  0.89 us
    pallas_call x1, Pallas kernels, early(): pl.pallas_call(lambda *refs: early_kernel(len(slots), *refs), out_shape=j...  0.88 us
    pallas_call x1, Pallas kernels, place(): pl.pallas_call(place_kernel, out_shape=jax.ShapeDtypeStruct(wide, F32), i...  0.68 us
  transfers between devices with their start and end apart: 14, of which 7 were waited for; matrix products, arithmetic and copies ran while one was open for 0% of the time, Pallas kernels for 4%

profile of v5, /device:TPU:0, one launch (start us, length us, event | category | flops | bytes accessed | tf_op | source)
XLA Modules:
  0.0 25.5 jit_solution(14015772503538455420)
XLA Ops:
  0.0 0.9 %shard_map.64 = (bf16[8,8320]{1,0:T(8,128)(2,1)S(1)}, bf16[1,2,48,128]{3,2,1,0:T(8,128)(2,1)S(1)}) custom-call(bf16[8,8192]{1,0:T(8,128)(2,1)} %bitcast.6, s32[1,8]{1,0:T(1,128)} %ids_hbm.1, bf16[2,16,64]{2,1,0:T(8,128)(2,1)} %left_hbm.1, bf16[2,32,128]{2,1,0:T(8,128)(2,1)} %right_hbm.1), custom_call_target="tpu_custom_call" | custom-call | tf_op jit(solution)/shard_map/pallas_call | solution.py:81
  0.9 3.1 %collective-permute-start.2 = (bf16[1,2,48,128]{3,2,1,0:T(8,128)(2,1)S(1)}, bf16[1,2,48,128]{3,2,1,0:T(8,128)(2,1)S(1)}, u32[]{:S(2)}, u32[]{:S(2)}) collective-permute-start(bf16[1,2,48,128]{3,2,1,0:T(8,128)(2,1)S(1)} %get-tuple-element.18.first_ref.refs_0_), channel_id=1, source_target_pairs={{0,1},{1,0},{2,3},{3,2},{4,5},{5,4},{6,7},{7,6},{8,9},{9,8},{10,11... | collective-permute-start | bytes 73736 | tf_op jit(solution)/shard_map/ppermute | solution.py:371
  4.0 2.4 %collective-permute-start.6 = (bf16[8,8320]{1,0:T(8,128)(2,1)S(1)}, bf16[8,8320]{1,0:T(8,128)(2,1)S(1)}, u32[]{:S(2)}, u32[]{:S(2)}) collective-permute-start(bf16[8,8320]{1,0:T(8,128)(2,1)S(1)} %get-tuple-element.17.row_ref.refs_0_), channel_id=1, source_target_pairs={{0,24},{4,28},{8,16},{12,20},{16,8},{20,12},{24,0},{28,4},{1,25},{... | collective-permute-start | bytes 399368 | tf_op jit(solution)/shard_map/ppermute | solution.py:355
  6.4 0.5 %collective-permute-start = (bf16[8,8320]{1,0:T(8,128)(2,1)S(1)}, bf16[8,8320]{1,0:T(8,128)(2,1)S(1)}, u32[]{:S(2)}, u32[]{:S(2)}) collective-permute-start(bf16[8,8320]{1,0:T(8,128)(2,1)S(1)} %get-tuple-element.17.row_ref.refs_0_), channel_id=1, source_target_pairs={{0,8},{4,20},{8,0},{12,28},{16,24},{20,4},{24,16},{28,12},{1,9},{5... | collective-permute-start | bytes 399368 | tf_op jit(solution)/shard_map/ppermute | solution.py:355
  7.0 0.8 %collective-permute-start.3 = (bf16[8,8320]{1,0:T(8,128)(2,1)S(1)}, bf16[8,8320]{1,0:T(8,128)(2,1)S(1)}, u32[]{:S(2)}, u32[]{:S(2)}) collective-permute-start(bf16[8,8320]{1,0:T(8,128)(2,1)S(1)} %get-tuple-element.19), channel_id=1, source_target_pairs={{0,16},{4,12},{8,24},{12,4},{16,0},{20,28},{24,8},{28,20},{1,17},{... | collective-permute-start | bytes 399368 | tf_op jit(solution)/shard_map/ppermute | solution.py:355
  7.8 2.6 %collective-permute-start.8 = (bf16[2,2,48,128]{3,2,1,0:T(8,128)(2,1)S(1)}, bf16[2,2,48,128]{3,2,1,0:T(8,128)(2,1)S(1)}, u32[]{:S(2)}, u32[]{:S(2)}) collective-permute-start(bf16[2,2,48,128]{3,2,1,0:T(8,128)(2,1)S(1)} %get-tuple-element.20), channel_id=1, source_target_pairs={{0,2},{1,3},{2,0},{3,1},{4,6},{5,7},{6,4},{7,5},{8,10},{9,11},{10,... | collective-permute-start | bytes 147464 | tf_op jit(solution)/shard_map/ppermute | solution.py:371
  10.4 0.0 collective-permute-start.5
  10.4 0.5 %collective-permute-start.7 = (bf16[8,8320]{1,0:T(8,128)(2,1)S(1)}, bf16[8,8320]{1,0:T(8,128)(2,1)S(1)}, u32[]{:S(2)}, u32[]{:S(2)}) collective-permute-start(bf16[8,8320]{1,0:T(8,128)(2,1)S(1)} %collective-permute-done.6.refs_2_), channel_id=1, source_target_pairs={{0,4},{4,0},{8,12},{12,8},{16,20},{20,16},{24,28},{28,24},{1,5},{5... | collective-permute-start | bytes 399368 | tf_op jit(solution)/shard_map/ppermute | solution.py:355
  11.0 1.8 %collective-permute-done.refs_0_ = bf16[8,8320]{1,0:T(8,128)(2,1)S(1)} collective-permute-done((bf16[8,8320]{1,0:T(8,128)(2,1)S(1)}, bf16[8,8320]{1,0:T(8,128)(2,1)S(1)}, u32[]{:S(2)}, u32[]{:S(2)}) %collective-permute-start) | collective-permute-done | bytes 133152 | tf_op jit(solution)/shard_map/ppermute | solution.py:355
  12.8 0.0 collective-permute-start.1
  12.8 0.0 collective-permute-done.3.refs_2_
  12.8 0.5 %collective-permute-start.4 = (bf16[8,8320]{1,0:T(8,128)(2,1)S(1)}, bf16[8,8320]{1,0:T(8,128)(2,1)S(1)}, u32[]{:S(2)}, u32[]{:S(2)}) collective-permute-start(bf16[8,8320]{1,0:T(8,128)(2,1)S(1)} %collective-permute-done.3.refs_2_), channel_id=1, source_target_pairs={{0,4},{4,0},{8,12},{12,8},{16,20},{20,16},{24,28},{28,24},{1,5},{5... | collective-permute-start | bytes 399368 | tf_op jit(solution)/shard_map/ppermute | solution.py:355
  13.4 0.9 %shard_map.67.refs_4_ = bf16[32,8192]{1,0:T(8,128)(2,1)S(1)} custom-call(bf16[8,8320]{1,0:T(8,128)(2,1)S(1)} %get-tuple-element.17.row_ref.refs_0_, bf16[8,8320]{1,0:T(8,128)(2,1)S(1)} %collective-permute-done.5.refs_1_, bf16[8,8320]{1,0:T(8,128)(2,1)S(1)} %collective-permute-done.6.refs_2_, bf16[8,8320]{1,0:T(8,128)(2,1)S(1)} %collective-permute-done.7.refs_3_, ...), custom_call_target="tpu_custom_call" | custom-call | flops 268435456 | bytes 1048576 | tf_op jit(solution)/shard_map/pallas_call | solution.py:194
  14.3 0.1 collective-permute-done.4.refs_3_
  14.4 3.3 %shard_map.68 = (f32[8,512]{1,0:T(8,128)S(1)}, bf16[8,512]{1,0:T(8,128)(2,1)S(1)}, bf16[8,512]{1,0:T(8,128)(2,1)S(1)}, bf16[8,512]{1,0:T(8,128)(2,1)S(1)}, bf16[...) custom-call(bf16[8,8320]{1,0:T(8,128)(2,1)S(1)} %collective-permute-done.refs_0_, ...), custom_call_target="tpu_custom_call" | custom-call | flops 1585446912 | bytes 8388608 | tf_op jit(solution)/shard_map/pallas_call | solution.py:238
  17.6 2.2 %collective-permute-start.11 = (bf16[2,8,512]{2,1,0:T(8,128)(2,1)S(1)}, bf16[2,8,512]{2,1,0:T(8,128)(2,1)S(1)}, u32[]{:S(2)}, u32[]{:S(2)}) collective-permute-start(bf16[2,8,512]{2,1,0:T(8,128)(2,1)S(1)} %get-tuple-element.26), channel_id=1, source_target_pairs={{0,24},{4,28},{8,16},{12,20},{16,8},{20,12},{24,0},{28,4},{1,25},{... | collective-permute-start | bytes 49160 | tf_op jit(solution)/shard_map/ppermute | solution.py:355
  19.9 0.8 %collective-permute-start.12 = (bf16[2,8,512]{2,1,0:T(8,128)(2,1)S(1)}, bf16[2,8,512]{2,1,0:T(8,128)(2,1)S(1)}, u32[]{:S(2)}, u32[]{:S(2)}) collective-permute-start(bf16[2,8,512]{2,1,0:T(8,128)(2,1)S(1)} %get-tuple-element.27), channel_id=1, source_target_pairs={{0,16},{4,20},{8,24},{12,28},{16,0},{20,4},{24,8},{28,12},{1,17},{... | collective-permute-start | bytes 49160 | tf_op jit(solution)/shard_map/ppermute | solution.py:355
  20.7 1.4 %collective-permute-start.9 = (bf16[8,512]{1,0:T(8,128)(2,1)S(1)}, bf16[8,512]{1,0:T(8,128)(2,1)S(1)}, u32[]{:S(2)}, u32[]{:S(2)}) collective-permute-start(bf16[8,512]{1,0:T(8,128)(2,1)S(1)} %get-tuple-element.24), channel_id=1, source_target_pairs={{0,8},{4,12},{8,0},{12,4},{16,24},{20,28},{24,16},{28,20},{1,9},{5... | collective-permute-start | bytes 24584 | tf_op jit(solution)/shard_map/ppermute | solution.py:355
  22.1 0.2 collective-permute-done.11.d_ref
  22.3 1.3 %collective-permute-done.12.y_ref = bf16[2,8,512]{2,1,0:T(8,128)(2,1)S(1)} collective-permute-done((bf16[2,8,512]{2,1,0:T(8,128)(2,1)S(1)}, bf16[2,8,512]{2,1,0:T(8,128)(2,1)S(1)}, u32[]{:S(2)}, u32[]{:S(2)}) %collective-permute-start.12) | collective-permute-done | bytes 16416 | tf_op jit(solution)/shard_map/ppermute | solution.py:355
  23.6 0.2 collective-permute-done.10.cross_ref
  23.8 0.6 %collective-permute-done.9.x_ref = bf16[8,512]{1,0:T(8,128)(2,1)S(1)} collective-permute-done((bf16[8,512]{1,0:T(8,128)(2,1)S(1)}, bf16[8,512]{1,0:T(8,128)(2,1)S(1)}, u32[]{:S(2)}, u32[]{:S(2)}) %collective-permute-start.9) | collective-permute-done | bytes 8224 | tf_op jit(solution)/shard_map/ppermute | solution.py:355
  24.4 0.4 %collective-permute-done.13.relayed_ref = bf16[3,8,512]{2,1,0:T(8,128)(2,1)S(1)} collective-permute-done((bf16[3,8,512]{2,1,0:T(8,128)(2,1)S(1)}, bf16[3,8,512]{2,1,0:T(8,128)(2,1)S(1)}, u32[]{:S(2)}, u32[]{:S(2)}) %collective-permute-start.13) | collective-permute-done | bytes 24608 | tf_op jit(solution)/shard_map/ppermute | solution.py:355
  24.8 0.7 %shard_map.71 = f32[8,4096]{1,0:T(8,128)} custom-call(f32[3,8,512]{2,1,0:T(8,128)S(1)} %shard_map.69.wide_ref, bf16[2,8,512]{2,1,0:T(8,128)(2,1)S(1)} %collective-permute-done.11.d_ref, bf16[2,8,512]{2,1,0:T(8,128)(2,1)S(1)} %collective-permute-done.12.y_ref, bf16[3,8,512]{2,1,0:T(8,128)(2,1)S(1)} %collective-permute-done.13.relayed_ref), custom_call_target="tpu_custom_call" | custom-call | tf_op jit(solution)/shard_map/pallas_call | solution.py:341
  (19 shorter events, 0.1 us)
Async XLA Ops:
  0.9 6.1 %collective-permute-start.2 = (bf16[1,2,48,128]{3,2,1,0:T(8,128)(2,1)S(1)}, bf16[1,2,48,128]{3,2,1,0:T(8,128)(2,1)S(1)}, u32[]{:S(2)}, u32[]{:S(2)}) collective-permute-start(bf16[1,2,48,128]{3,2,1,0:T(8,128)(2,1)S(1)} %get-tuple-element.18.first_ref.refs_0_), channel_id=1, source_target_pairs={{0,1},{1,0},{2,3},{3,2},{4,5},{5,4},{6,7},{7,6},{8,9},{9,8},{10,11... | collective-permute-start | bytes 73736 | tf_op jit(solution)/shard_map/ppermute | solution.py:371
  4.0 6.5 %collective-permute-start.6 = (bf16[8,8320]{1,0:T(8,128)(2,1)S(1)}, bf16[8,8320]{1,0:T(8,128)(2,1)S(1)}, u32[]{:S(2)}, u32[]{:S(2)}) collective-permute-start(bf16[8,8320]{1,0:T(8,128)(2,1)S(1)} %get-tuple-element.17.row_ref.refs_0_), channel_id=1, source_target_pairs={{0,24},{4,28},{8,16},{12,20},{16,8},{20,12},{24,0},{28,4},{1,25},{... | collective-permute-start | bytes 399368 | tf_op jit(solution)/shard_map/ppermute | solution.py:355
  6.4 6.4 %collective-permute-start = (bf16[8,8320]{1,0:T(8,128)(2,1)S(1)}, bf16[8,8320]{1,0:T(8,128)(2,1)S(1)}, u32[]{:S(2)}, u32[]{:S(2)}) collective-permute-start(bf16[8,8320]{1,0:T(8,128)(2,1)S(1)} %get-tuple-element.17.row_ref.refs_0_), channel_id=1, source_target_pairs={{0,8},{4,20},{8,0},{12,28},{16,24},{20,4},{24,16},{28,12},{1,9},{5... | collective-permute-start | bytes 399368 | tf_op jit(solution)/shard_map/ppermute | solution.py:355
  7.0 5.8 %collective-permute-start.3 = (bf16[8,8320]{1,0:T(8,128)(2,1)S(1)}, bf16[8,8320]{1,0:T(8,128)(2,1)S(1)}, u32[]{:S(2)}, u32[]{:S(2)}) collective-permute-start(bf16[8,8320]{1,0:T(8,128)(2,1)S(1)} %get-tuple-element.19), channel_id=1, source_target_pairs={{0,16},{4,12},{8,24},{12,4},{16,0},{20,28},{24,8},{28,20},{1,17},{... | collective-permute-start | bytes 399368 | tf_op jit(solution)/shard_map/ppermute | solution.py:355
  7.8 6.5 %slice-start = ((s8[8388608]{0:T(1024)(128)(4,1)}), s8[4194304]{0:T(1024)(128)(4,1)S(1)}, s32[]{:S(2)}) async-start(s8[8388608]{0:T(1024)(128)(4,1)} %bitcast.3), calls=%async_computation | async-start | bytes 8388608
  7.8 6.5 %slice-start.1 = ((s8[8388608]{0:T(1024)(128)(4,1)}), s8[4194304]{0:T(1024)(128)(4,1)S(1)}, s32[]{:S(2)}) async-start(s8[8388608]{0:T(1024)(128)(4,1)} %bitcast.3), calls=%async_computation.1 | async-start | bytes 8388608
  7.8 6.5 %copy-start = (s32[512]{0:T(512)S(1)}, s32[512]{0:T(512)}, u32[]{:S(2)}) copy-start(s32[512]{0:T(512)} %param.11) | copy-start | bytes 6148
  7.8 5.5 %collective-permute-start.8 = (bf16[2,2,48,128]{3,2,1,0:T(8,128)(2,1)S(1)}, bf16[2,2,48,128]{3,2,1,0:T(8,128)(2,1)S(1)}, u32[]{:S(2)}, u32[]{:S(2)}) collective-permute-start(bf16[2,2,48,128]{3,2,1,0:T(8,128)(2,1)S(1)} %get-tuple-element.20), channel_id=1, source_target_pairs={{0,2},{1,3},{2,0},{3,1},{4,6},{5,7},{6,4},{7,5},{8,10},{9,11},{10,... | collective-permute-start | bytes 147464 | tf_op jit(solution)/shard_map/ppermute | solution.py:371
  10.4 2.9 %collective-permute-start.5 = (bf16[8,8320]{1,0:T(8,128)(2,1)S(1)}, bf16[8,8320]{1,0:T(8,128)(2,1)S(1)}, u32[]{:S(2)}, u32[]{:S(2)}) collective-permute-start(bf16[8,8320]{1,0:T(8,128)(2,1)S(1)} %get-tuple-element.17.row_ref.refs_0_), channel_id=1, source_target_pairs={{0,4},{4,0},{8,12},{12,8},{16,20},{20,16},{24,28},{28,24},{1,5},{5... | collective-permute-start | bytes 399368 | tf_op jit(solution)/shard_map/ppermute | solution.py:355
  10.4 2.9 %collective-permute-start.7 = (bf16[8,8320]{1,0:T(8,128)(2,1)S(1)}, bf16[8,8320]{1,0:T(8,128)(2,1)S(1)}, u32[]{:S(2)}, u32[]{:S(2)}) collective-permute-start(bf16[8,8320]{1,0:T(8,128)(2,1)S(1)} %collective-permute-done.6.refs_2_), channel_id=1, source_target_pairs={{0,4},{4,0},{8,12},{12,8},{16,20},{20,16},{24,28},{28,24},{1,5},{5... | collective-permute-start | bytes 399368 | tf_op jit(solution)/shard_map/ppermute | solution.py:355
  12.8 1.5 %collective-permute-start.1 = (bf16[8,8320]{1,0:T(8,128)(2,1)S(1)}, bf16[8,8320]{1,0:T(8,128)(2,1)S(1)}, u32[]{:S(2)}, u32[]{:S(2)}) collective-permute-start(bf16[8,8320]{1,0:T(8,128)(2,1)S(1)} %collective-permute-done.refs_0_), channel_id=1, source_target_pairs={{0,4},{4,0},{8,12},{12,8},{16,20},{20,16},{24,28},{28,24},{1,5},{5... | collective-permute-start | bytes 399368 | tf_op jit(solution)/shard_map/ppermute | solution.py:355
  12.8 1.5 %collective-permute-start.4 = (bf16[8,8320]{1,0:T(8,128)(2,1)S(1)}, bf16[8,8320]{1,0:T(8,128)(2,1)S(1)}, u32[]{:S(2)}, u32[]{:S(2)}) collective-permute-start(bf16[8,8320]{1,0:T(8,128)(2,1)S(1)} %collective-permute-done.3.refs_2_), channel_id=1, source_target_pairs={{0,4},{4,0},{8,12},{12,8},{16,20},{20,16},{24,28},{28,24},{1,5},{5... | collective-permute-start | bytes 399368 | tf_op jit(solution)/shard_map/ppermute | solution.py:355
  17.6 4.7 %collective-permute-start.11 = (bf16[2,8,512]{2,1,0:T(8,128)(2,1)S(1)}, bf16[2,8,512]{2,1,0:T(8,128)(2,1)S(1)}, u32[]{:S(2)}, u32[]{:S(2)}) collective-permute-start(bf16[2,8,512]{2,1,0:T(8,128)(2,1)S(1)} %get-tuple-element.26), channel_id=1, source_target_pairs={{0,24},{4,28},{8,16},{12,20},{16,8},{20,12},{24,0},{28,4},{1,25},{... | collective-permute-start | bytes 49160 | tf_op jit(solution)/shard_map/ppermute | solution.py:355
  19.9 3.7 %collective-permute-start.12 = (bf16[2,8,512]{2,1,0:T(8,128)(2,1)S(1)}, bf16[2,8,512]{2,1,0:T(8,128)(2,1)S(1)}, u32[]{:S(2)}, u32[]{:S(2)}) collective-permute-start(bf16[2,8,512]{2,1,0:T(8,128)(2,1)S(1)} %get-tuple-element.27), channel_id=1, source_target_pairs={{0,16},{4,20},{8,24},{12,28},{16,0},{20,4},{24,8},{28,12},{1,17},{... | collective-permute-start | bytes 49160 | tf_op jit(solution)/shard_map/ppermute | solution.py:355
  20.7 3.1 %collective-permute-start.10 = (bf16[8,512]{1,0:T(8,128)(2,1)S(1)}, bf16[8,512]{1,0:T(8,128)(2,1)S(1)}, u32[]{:S(2)}, u32[]{:S(2)}) collective-permute-start(bf16[8,512]{1,0:T(8,128)(2,1)S(1)} %get-tuple-element.25), channel_id=1, source_target_pairs={{0,12},{4,8},{8,4},{12,0},{16,28},{20,24},{24,20},{28,16},{1,13},{... | collective-permute-start | bytes 24584 | tf_op jit(solution)/shard_map/ppermute | solution.py:355
  20.7 3.7 %collective-permute-start.9 = (bf16[8,512]{1,0:T(8,128)(2,1)S(1)}, bf16[8,512]{1,0:T(8,128)(2,1)S(1)}, u32[]{:S(2)}, u32[]{:S(2)}) collective-permute-start(bf16[8,512]{1,0:T(8,128)(2,1)S(1)} %get-tuple-element.24), channel_id=1, source_target_pairs={{0,8},{4,12},{8,0},{12,4},{16,24},{20,28},{24,16},{28,20},{1,9},{5... | collective-permute-start | bytes 24584 | tf_op jit(solution)/shard_map/ppermute | solution.py:355
  23.6 1.2 %collective-permute-start.13 = (bf16[3,8,512]{2,1,0:T(8,128)(2,1)S(1)}, bf16[3,8,512]{2,1,0:T(8,128)(2,1)S(1)}, u32[]{:S(2)}, u32[]{:S(2)}) collective-permute-start(bf16[3,8,512]{2,1,0:T(8,128)(2,1)S(1)} %shard_map.70), channel_id=1, source_target_pairs={{0,4},{4,0},{8,12},{12,8},{16,20},{20,16},{24,28},{28,24},{1,5},{5... | collective-permute-start | bytes 73736 | tf_op jit(solution)/shard_map/ppermute | solution.py:355

commit v6 on v5

--- a/solution.py
+++ b/solution.py
@@ -146,30 +146,29 @@
             prep_ref[group * pair : (group + 1) * pair, a * order_b : (a + 1) * order_b] = turned[a]
 
 
-def factor_kernel(order_a, order_b, steps, *refs):
-    fac_refs = refs[: steps + 1]
-    left_ref, right_ref = refs[steps + 1 :]
-    blocks = fac_refs[0].shape[1]
-    planes = 2**steps
-    cut_a, cut_b = order_a // planes, order_b // planes
+def factor_kernel(order_a, order_b, *refs):
+    left_ref, right_ref = refs[-2:]
+    pieces = [(ref, i) for ref in refs[:-2] for i in range(ref.shape[0])]
+    blocks = right_ref.shape[1] // order_b
+    cut_a, cut_b = order_a // len(pieces), order_b // len(pieces)
     plane = lax.axis_index("qry")
-    for m in range(planes):
-        step = m.bit_length()
-        piece = fac_refs[step][m - (1 << (step - 1)) if step else 0]
+    for m, (ref, i) in enumerate(pieces):
+        piece = ref[i]
         at = lax.bitwise_xor(plane, m)
         for k in range(blocks):
-            left_ref[pl.ds(pl.multiple_of(k * order_a + at * cut_a, 16), cut_a), :] = piece[k, :cut_a, :order_a]
+            left_ref[pl.ds(pl.multiple_of(k * order_a + at * cut_a, 16), cut_a), :] = piece[
+                :cut_a, k * order_a : (k + 1) * order_a
+            ]
             for half in range(2):
                 right_ref[
                     pl.ds(pl.multiple_of(half * order_b + at * cut_b, 16), cut_b),
                     k * order_b : (k + 1) * order_b,
-                ] = piece[k, cut_a:, :]
-
-
-def place_factors(factors, order_a, order_b):
-    blocks = factors[0].shape[1]
-    return pl.pallas_call(
-        lambda *refs: factor_kernel(order_a, order_b, len(factors) - 1, *refs),
+                ] = piece[cut_a + k * cut_b : cut_a + (k + 1) * cut_b, :]
+
+
+def place_factors(factors, blocks, order_a, order_b):
+    return pl.pallas_call(
+        lambda *refs: factor_kernel(order_a, order_b, *refs),
         out_shape=(
             jax.ShapeDtypeStruct((blocks * order_a, order_a), BF16),
             jax.ShapeDtypeStruct((2 * order_b, blocks * order_b), BF16),
@@ -177,7 +176,7 @@
         in_specs=[VMEM] * len(factors),
         out_specs=(VMEM, VMEM),
         compiler_params=pltpu.CompilerParams(vmem_limit_bytes=8 << 20),
-        cost_estimate=pl.CostEstimate(flops=6*10**9, bytes_accessed=10**6, transcendentals=0),
+        cost_estimate=pl.CostEstimate(flops=6 * 10**9, bytes_accessed=10**6, transcendentals=0),
     )(*factors)
 
 
@@ -259,18 +258,23 @@
     return pltpu.with_memory_space_constraint(x, pltpu.HBM)
 
 
-def join_kernel(first_ref, second_ref, row_ref, both_ref, again_ref):
-    count = first_ref.shape[0]
-    both_ref[:count] = first_ref[...]
-    both_ref[count:] = second_ref[...]
+def join_kernel(order_a, cut, first_ref, second_ref, row_ref, both_ref, again_ref):
+    blocks, depth = first_ref.shape[1:3]
+    for j, ref in enumerate((first_ref, second_ref)):
+        for k in range(blocks):
+            both_ref[j, :cut, k * order_a : (k + 1) * order_a] = ref[0, k, :cut, :order_a]
+            at = cut + k * (depth - cut)
+            both_ref[j, at : at + depth - cut, :] = ref[0, k, cut:, :]
     again_ref[...] = row_ref[...]
 
 
-def join(first, second, row):
-    return pl.pallas_call(
-        join_kernel,
+def join(first, second, row, left):
+    blocks, cut, order_a = left.shape
+    rows = cut + blocks * (first.shape[2] - cut)
+    return pl.pallas_call(
+        lambda *refs: join_kernel(order_a, cut, *refs),
         out_shape=(
-            jax.ShapeDtypeStruct((2 * first.shape[0],) + first.shape[1:], first.dtype),
+            jax.ShapeDtypeStruct((2, rows, LANES), first.dtype),
             jax.ShapeDtypeStruct(row.shape, row.dtype),
         ),
         in_specs=[VMEM] * 3,
@@ -364,18 +368,21 @@
     row, fac = pack(queries[0], block_ids, left_factor, right_factor)
     slot_d = across(row, (3, 3))
     slot_a = across(row, flips_a)
-    factors = [fac]
-    held, again = fac, row
-    step = 1
+    def plane(x, step):
+        return lax.ppermute(x, "qry", [(i, i ^ step) for i in range(planes)])
+
+    held, again = join(fac, plane(fac, 1), row, left_factor)
+    factors = [held]
+    step = 2
     while step < planes:
-        got = lax.ppermute(held, "qry", [(i, i ^ step) for i in range(planes)])
+        got = plane(held, step)
         factors.append(got)
         if step * 2 < planes:
-            held, again = join(held, got, row)
+            held = jnp.concatenate([held, got])
         step *= 2
     slot_b = across(again, flips_b)
     order_a, order_b = left_factor.shape[2], right_factor.shape[2]
-    left_all, right_all = place_factors(factors, order_a, order_b)
+    left_all, right_all = place_factors(factors, left_factor.shape[0], order_a, order_b)
     prepared = early(
         [row, sibling(row), slot_d, sibling(slot_d)], left_all, right_all, order_a, order_b
     )
@@ -390,7 +397,8 @@
 
     def per_device(queries, block_ids, left_factor, right_factor, clip_grads, lengths):
         whole_tiles = left_factor.shape[1] % 16 == 0 and right_factor.shape[1] % 16 == 0
-        if owners == 4 * CORES and planes & (planes - 1) == 0 and whole_tiles:
+        whole_tiles = whole_tiles and left_factor.shape[0] * left_factor.shape[2] == LANES == right_factor.shape[2]
+        if owners == 4 * CORES and planes > 1 and planes & (planes - 1) == 0 and whole_tiles:
             return per_device_exchanged(
                 planes, queries, block_ids, left_factor, right_factor, clip_grads, lengths
             )

time: 25.7 us -> 25.6 us (level)
  transfers between devices with their start and end apart: 14 -> 14, of which waited for: 7 -> 6; matrix products, arithmetic and copies ran while one was open for 0% -> 0% of each run, Pallas kernels for 4% -> 4%
where the time goes in v6:
time: 25.6 us; the launch traced here: 25.3 us
  starting transfers between devices  14.9 us (58%)
  Pallas kernels  5.86 us (23%)
  waiting for transfers between devices  4.47 us (17%)
    ppermute x12, starting transfers between devices, move(): lax.ppermute(x, 'own', [(i, to(i // CORES, i % CORES)) for i in range(siz...  9.26 us
    ppermute x2, starting transfers between devices, plane(): return lax.ppermute(x, 'qry', [(i, i ^ step) for i in range(planes)])  5.68 us
    ppermute x12, waiting for transfers between devices, move(): lax.ppermute(x, 'own', [(i, to(i // CORES, i % CORES)) for i in range(siz...  4.46 us
    pallas_call x1, Pallas kernels, score(): pl.pallas_call(lambda *refs: score_kernel(len(slots), *refs), out_shape=(...  3.25 us
    pallas_call x1, Pallas kernels, pack(): pl.pallas_call(pack_kernel, out_shape=(jax.ShapeDtypeStruct((rows, width...  0.89 us
    pallas_call x1, Pallas kernels, early(): pl.pallas_call(lambda *refs: early_kernel(len(slots), *refs), out_shape=j...  0.88 us
    pallas_call x1, Pallas kernels, place(): pl.pallas_call(place_kernel, out_shape=jax.ShapeDtypeStruct(wide, F32), i...  0.68 us
  transfers between devices with their start and end apart: 14, of which 6 were waited for; matrix products, arithmetic and copies ran while one was open for 0% of the time, Pallas kernels for 4%

profile of v6, /device:TPU:0, one launch (start us, length us, event | category | flops | bytes accessed | tf_op | source)
XLA Modules:
  0.0 25.3 jit_solution(7813151313876996687)
XLA Ops:
  0.0 0.9 %shard_map.64 = (bf16[8,8320]{1,0:T(8,128)(2,1)S(1)}, bf16[1,2,48,128]{3,2,1,0:T(8,128)(2,1)S(1)}) custom-call(bf16[8,8192]{1,0:T(8,128)(2,1)} %bitcast.6, s32[1,8]{1,0:T(1,128)} %ids_hbm.1, bf16[2,16,64]{2,1,0:T(8,128)(2,1)} %left_hbm.1, bf16[2,32,128]{2,1,0:T(8,128)(2,1)} %right_hbm.1), custom_call_target="tpu_custom_call" | custom-call | tf_op jit(solution)/shard_map/pallas_call | solution.py:81
  0.9 3.1 %collective-permute-start.2 = (bf16[1,2,48,128]{3,2,1,0:T(8,128)(2,1)S(1)}, bf16[1,2,48,128]{3,2,1,0:T(8,128)(2,1)S(1)}, u32[]{:S(2)}, u32[]{:S(2)}) collective-permute-start(bf16[1,2,48,128]{3,2,1,0:T(8,128)(2,1)S(1)} %get-tuple-element.18.refs_0_), channel_id=1, source_target_pairs={{0,1},{1,0},{2,3},{3,2},{4,5},{5,4},{6,7},{7,6},{8,9},{9,8},{10,11... | collective-permute-start | bytes 73736 | tf_op jit(solution)/shard_map/ppermute | solution.py:372
  4.0 2.4 %collective-permute-start.6 = (bf16[8,8320]{1,0:T(8,128)(2,1)S(1)}, bf16[8,8320]{1,0:T(8,128)(2,1)S(1)}, u32[]{:S(2)}, u32[]{:S(2)}) collective-permute-start(bf16[8,8320]{1,0:T(8,128)(2,1)S(1)} %get-tuple-element.17.refs_2_.refs_0_), channel_id=1, source_target_pairs={{0,24},{4,28},{8,16},{12,20},{16,8},{20,12},{24,0},{28,4},{1,25},{... | collective-permute-start | bytes 399368 | tf_op jit(solution)/shard_map/ppermute | solution.py:359
  6.4 0.5 %collective-permute-start = (bf16[8,8320]{1,0:T(8,128)(2,1)S(1)}, bf16[8,8320]{1,0:T(8,128)(2,1)S(1)}, u32[]{:S(2)}, u32[]{:S(2)}) collective-permute-start(bf16[8,8320]{1,0:T(8,128)(2,1)S(1)} %get-tuple-element.17.refs_2_.refs_0_), channel_id=1, source_target_pairs={{0,8},{4,20},{8,0},{12,28},{16,24},{20,4},{24,16},{28,12},{1,9},{5... | collective-permute-start | bytes 399368 | tf_op jit(solution)/shard_map/ppermute | solution.py:359
  7.0 0.0 collective-permute-done.2.refs_1_
  7.0 0.1 shard_map.65
  7.0 0.8 %collective-permute-start.3 = (bf16[8,8320]{1,0:T(8,128)(2,1)S(1)}, bf16[8,8320]{1,0:T(8,128)(2,1)S(1)}, u32[]{:S(2)}, u32[]{:S(2)}) collective-permute-start(bf16[8,8320]{1,0:T(8,128)(2,1)S(1)} %get-tuple-element.19), channel_id=1, source_target_pairs={{0,16},{4,12},{8,24},{12,4},{16,0},{20,28},{24,8},{28,20},{1,17},{... | collective-permute-start | bytes 399368 | tf_op jit(solution)/shard_map/ppermute | solution.py:359
  7.9 2.6 %collective-permute-start.8 = (bf16[2,80,128]{2,1,0:T(8,128)(2,1)S(1)}, bf16[2,80,128]{2,1,0:T(8,128)(2,1)S(1)}, u32[]{:S(2)}, u32[]{:S(2)}) collective-permute-start(bf16[2,80,128]{2,1,0:T(8,128)(2,1)S(1)} %get-tuple-element.20.refs_0_), channel_id=1, source_target_pairs={{0,2},{1,3},{2,0},{3,1},{4,6},{5,7},{6,4},{7,5},{8,10},{9,11},{10,... | collective-permute-start | bytes 122888 | tf_op jit(solution)/shard_map/ppermute | solution.py:372
  10.4 0.5 %collective-permute-start.7 = (bf16[8,8320]{1,0:T(8,128)(2,1)S(1)}, bf16[8,8320]{1,0:T(8,128)(2,1)S(1)}, u32[]{:S(2)}, u32[]{:S(2)}) collective-permute-start(bf16[8,8320]{1,0:T(8,128)(2,1)S(1)} %collective-permute-done.6.refs_2_), channel_id=1, source_target_pairs={{0,4},{4,0},{8,12},{12,8},{16,20},{20,16},{24,28},{28,24},{1,5},{5... | collective-permute-start | bytes 399368 | tf_op jit(solution)/shard_map/ppermute | solution.py:359
  11.0 1.8 %collective-permute-done.refs_0_ = bf16[8,8320]{1,0:T(8,128)(2,1)S(1)} collective-permute-done((bf16[8,8320]{1,0:T(8,128)(2,1)S(1)}, bf16[8,8320]{1,0:T(8,128)(2,1)S(1)}, u32[]{:S(2)}, u32[]{:S(2)}) %collective-permute-start) | collective-permute-done | bytes 133152 | tf_op jit(solution)/shard_map/ppermute | solution.py:359
  12.8 0.5 %collective-permute-start.4 = (bf16[8,8320]{1,0:T(8,128)(2,1)S(1)}, bf16[8,8320]{1,0:T(8,128)(2,1)S(1)}, u32[]{:S(2)}, u32[]{:S(2)}) collective-permute-start(bf16[8,8320]{1,0:T(8,128)(2,1)S(1)} %collective-permute-done.3.refs_2_), channel_id=1, source_target_pairs={{0,4},{4,0},{8,12},{12,8},{16,20},{20,16},{24,28},{28,24},{1,5},{5... | collective-permute-start | bytes 399368 | tf_op jit(solution)/shard_map/ppermute | solution.py:359
  13.3 0.1 shard_map.66
  13.4 0.9 %shard_map.67.refs_4_ = bf16[32,8192]{1,0:T(8,128)(2,1)S(1)} custom-call(bf16[8,8320]{1,0:T(8,128)(2,1)S(1)} %get-tuple-element.17.refs_2_.refs_0_, bf16[8,8320]{1,0:T(8,128)(2,1)S(1)} %collective-permute-done.5.refs_1_, bf16[8,8320]{1,0:T(8,128)(2,1)S(1)} %collective-permute-done.6.refs_2_, bf16[8,8320]{1,0:T(8,128)(2,1)S(1)} %collective-permute-done.7.refs_3_, ...), custom_call_target="tpu_custom_call" | custom-call | flops 268435456 | bytes 1048576 | tf_op jit(solution)/shard_map/pallas_call | solution.py:193
  14.3 0.0 collective-permute-done.4.refs_3_
  14.4 3.3 %shard_map.68 = (f32[8,512]{1,0:T(8,128)S(1)}, bf16[8,512]{1,0:T(8,128)(2,1)S(1)}, bf16[8,512]{1,0:T(8,128)(2,1)S(1)}, bf16[8,512]{1,0:T(8,128)(2,1)S(1)}, bf16[...) custom-call(bf16[8,8320]{1,0:T(8,128)(2,1)S(1)} %collective-permute-done.refs_0_, ...), custom_call_target="tpu_custom_call" | custom-call | flops 1585446912 | bytes 8388608 | tf_op jit(solution)/shard_map/pallas_call | solution.py:237
  17.6 2.1 %collective-permute-start.11 = (bf16[2,8,512]{2,1,0:T(8,128)(2,1)S(1)}, bf16[2,8,512]{2,1,0:T(8,128)(2,1)S(1)}, u32[]{:S(2)}, u32[]{:S(2)}) collective-permute-start(bf16[2,8,512]{2,1,0:T(8,128)(2,1)S(1)} %get-tuple-element.26), channel_id=1, source_target_pairs={{0,24},{4,28},{8,16},{12,20},{16,8},{20,12},{24,0},{28,4},{1,25},{... | collective-permute-start | bytes 49160 | tf_op jit(solution)/shard_map/ppermute | solution.py:359
  19.7 1.0 %collective-permute-start.12 = (bf16[2,8,512]{2,1,0:T(8,128)(2,1)S(1)}, bf16[2,8,512]{2,1,0:T(8,128)(2,1)S(1)}, u32[]{:S(2)}, u32[]{:S(2)}) collective-permute-start(bf16[2,8,512]{2,1,0:T(8,128)(2,1)S(1)} %get-tuple-element.27), channel_id=1, source_target_pairs={{0,16},{4,20},{8,24},{12,28},{16,0},{20,4},{24,8},{28,12},{1,17},{... | collective-permute-start | bytes 49160 | tf_op jit(solution)/shard_map/ppermute | solution.py:359
  20.7 1.4 %collective-permute-start.9 = (bf16[8,512]{1,0:T(8,128)(2,1)S(1)}, bf16[8,512]{1,0:T(8,128)(2,1)S(1)}, u32[]{:S(2)}, u32[]{:S(2)}) collective-permute-start(bf16[8,512]{1,0:T(8,128)(2,1)S(1)} %get-tuple-element.24), channel_id=1, source_target_pairs={{0,8},{4,12},{8,0},{12,4},{16,24},{20,28},{24,16},{28,20},{1,9},{5... | collective-permute-start | bytes 24584 | tf_op jit(solution)/shard_map/ppermute | solution.py:359
  22.1 0.2 collective-permute-done.11.d_ref
  22.3 1.1 %collective-permute-done.12.y_ref = bf16[2,8,512]{2,1,0:T(8,128)(2,1)S(1)} collective-permute-done((bf16[2,8,512]{2,1,0:T(8,128)(2,1)S(1)}, bf16[2,8,512]{2,1,0:T(8,128)(2,1)S(1)}, u32[]{:S(2)}, u32[]{:S(2)}) %collective-permute-start.12) | collective-permute-done | bytes 16416 | tf_op jit(solution)/shard_map/ppermute | solution.py:359
  23.5 0.3 %collective-permute-done.10.cross_ref = bf16[8,512]{1,0:T(8,128)(2,1)S(1)} collective-permute-done((bf16[8,512]{1,0:T(8,128)(2,1)S(1)}, bf16[8,512]{1,0:T(8,128)(2,1)S(1)}, u32[]{:S(2)}, u32[]{:S(2)}) %collective-permute-start.10) | collective-permute-done | bytes 8224 | tf_op jit(solution)/shard_map/ppermute | solution.py:359
  23.8 0.6 %collective-permute-done.9.x_ref = bf16[8,512]{1,0:T(8,128)(2,1)S(1)} collective-permute-done((bf16[8,512]{1,0:T(8,128)(2,1)S(1)}, bf16[8,512]{1,0:T(8,128)(2,1)S(1)}, u32[]{:S(2)}, u32[]{:S(2)}) %collective-permute-start.9) | collective-permute-done | bytes 8224 | tf_op jit(solution)/shard_map/ppermute | solution.py:359
  24.4 0.3 %collective-permute-done.13.relayed_ref = bf16[3,8,512]{2,1,0:T(8,128)(2,1)S(1)} collective-permute-done((bf16[3,8,512]{2,1,0:T(8,128)(2,1)S(1)}, bf16[3,8,512]{2,1,0:T(8,128)(2,1)S(1)}, u32[]{:S(2)}, u32[]{:S(2)}) %collective-permute-start.13) | collective-permute-done | bytes 24608 | tf_op jit(solution)/shard_map/ppermute | solution.py:359
  24.7 0.7 %shard_map.71 = f32[8,4096]{1,0:T(8,128)} custom-call(f32[3,8,512]{2,1,0:T(8,128)S(1)} %shard_map.69.wide_ref, bf16[2,8,512]{2,1,0:T(8,128)(2,1)S(1)} %collective-permute-done.11.d_ref, bf16[2,8,512]{2,1,0:T(8,128)(2,1)S(1)} %collective-permute-done.12.y_ref, bf16[3,8,512]{2,1,0:T(8,128)(2,1)S(1)} %collective-permute-done.13.relayed_ref), custom_call_target="tpu_custom_call" | custom-call | tf_op jit(solution)/shard_map/pallas_call | solution.py:345
  (19 shorter events, 0.0 us)
Async XLA Ops:
  0.9 6.1 %collective-permute-start.2 = (bf16[1,2,48,128]{3,2,1,0:T(8,128)(2,1)S(1)}, bf16[1,2,48,128]{3,2,1,0:T(8,128)(2,1)S(1)}, u32[]{:S(2)}, u32[]{:S(2)}) collective-permute-start(bf16[1,2,48,128]{3,2,1,0:T(8,128)(2,1)S(1)} %get-tuple-element.18.refs_0_), channel_id=1, source_target_pairs={{0,1},{1,0},{2,3},{3,2},{4,5},{5,4},{6,7},{7,6},{8,9},{9,8},{10,11... | collective-permute-start | bytes 73736 | tf_op jit(solution)/shard_map/ppermute | solution.py:372
  4.0 6.5 %collective-permute-start.6 = (bf16[8,8320]{1,0:T(8,128)(2,1)S(1)}, bf16[8,8320]{1,0:T(8,128)(2,1)S(1)}, u32[]{:S(2)}, u32[]{:S(2)}) collective-permute-start(bf16[8,8320]{1,0:T(8,128)(2,1)S(1)} %get-tuple-element.17.refs_2_.refs_0_), channel_id=1, source_target_pairs={{0,24},{4,28},{8,16},{12,20},{16,8},{20,12},{24,0},{28,4},{1,25},{... | collective-permute-start | bytes 399368 | tf_op jit(solution)/shard_map/ppermute | solution.py:359
  6.4 6.4 %collective-permute-start = (bf16[8,8320]{1,0:T(8,128)(2,1)S(1)}, bf16[8,8320]{1,0:T(8,128)(2,1)S(1)}, u32[]{:S(2)}, u32[]{:S(2)}) collective-permute-start(bf16[8,8320]{1,0:T(8,128)(2,1)S(1)} %get-tuple-element.17.refs_2_.refs_0_), channel_id=1, source_target_pairs={{0,8},{4,20},{8,0},{12,28},{16,24},{20,4},{24,16},{28,12},{1,9},{5... | collective-permute-start | bytes 399368 | tf_op jit(solution)/shard_map/ppermute | solution.py:359
  7.0 5.8 %collective-permute-start.3 = (bf16[8,8320]{1,0:T(8,128)(2,1)S(1)}, bf16[8,8320]{1,0:T(8,128)(2,1)S(1)}, u32[]{:S(2)}, u32[]{:S(2)}) collective-permute-start(bf16[8,8320]{1,0:T(8,128)(2,1)S(1)} %get-tuple-element.19), channel_id=1, source_target_pairs={{0,16},{4,12},{8,24},{12,4},{16,0},{20,28},{24,8},{28,20},{1,17},{... | collective-permute-start | bytes 399368 | tf_op jit(solution)/shard_map/ppermute | solution.py:359
  7.8 6.5 %slice-start = ((s8[8388608]{0:T(1024)(128)(4,1)}), s8[4194304]{0:T(1024)(128)(4,1)S(1)}, s32[]{:S(2)}) async-start(s8[8388608]{0:T(1024)(128)(4,1)} %bitcast.3), calls=%async_computation | async-start | bytes 8388608
  7.8 6.5 %slice-start.1 = ((s8[8388608]{0:T(1024)(128)(4,1)}), s8[4194304]{0:T(1024)(128)(4,1)S(1)}, s32[]{:S(2)}) async-start(s8[8388608]{0:T(1024)(128)(4,1)} %bitcast.3), calls=%async_computation.1 | async-start | bytes 8388608
  7.9 6.5 %copy-start = (s32[512]{0:T(512)S(1)}, s32[512]{0:T(512)}, u32[]{:S(2)}) copy-start(s32[512]{0:T(512)} %param.11) | copy-start | bytes 6148
  7.9 5.5 %collective-permute-start.8 = (bf16[2,80,128]{2,1,0:T(8,128)(2,1)S(1)}, bf16[2,80,128]{2,1,0:T(8,128)(2,1)S(1)}, u32[]{:S(2)}, u32[]{:S(2)}) collective-permute-start(bf16[2,80,128]{2,1,0:T(8,128)(2,1)S(1)} %get-tuple-element.20.refs_0_), channel_id=1, source_target_pairs={{0,2},{1,3},{2,0},{3,1},{4,6},{5,7},{6,4},{7,5},{8,10},{9,11},{10,... | collective-permute-start | bytes 122888 | tf_op jit(solution)/shard_map/ppermute | solution.py:372
  10.4 3.0 %collective-permute-start.5 = (bf16[8,8320]{1,0:T(8,128)(2,1)S(1)}, bf16[8,8320]{1,0:T(8,128)(2,1)S(1)}, u32[]{:S(2)}, u32[]{:S(2)}) collective-permute-start(bf16[8,8320]{1,0:T(8,128)(2,1)S(1)} %get-tuple-element.17.refs_2_.refs_0_), channel_id=1, source_target_pairs={{0,4},{4,0},{8,12},{12,8},{16,20},{20,16},{24,28},{28,24},{1,5},{5... | collective-permute-start | bytes 399368 | tf_op jit(solution)/shard_map/ppermute | solution.py:359
  10.4 3.0 %collective-permute-start.7 = (bf16[8,8320]{1,0:T(8,128)(2,1)S(1)}, bf16[8,8320]{1,0:T(8,128)(2,1)S(1)}, u32[]{:S(2)}, u32[]{:S(2)}) collective-permute-start(bf16[8,8320]{1,0:T(8,128)(2,1)S(1)} %collective-permute-done.6.refs_2_), channel_id=1, source_target_pairs={{0,4},{4,0},{8,12},{12,8},{16,20},{20,16},{24,28},{28,24},{1,5},{5... | collective-permute-start | bytes 399368 | tf_op jit(solution)/shard_map/ppermute | solution.py:359
  12.8 1.5 %collective-permute-start.1 = (bf16[8,8320]{1,0:T(8,128)(2,1)S(1)}, bf16[8,8320]{1,0:T(8,128)(2,1)S(1)}, u32[]{:S(2)}, u32[]{:S(2)}) collective-permute-start(bf16[8,8320]{1,0:T(8,128)(2,1)S(1)} %collective-permute-done.refs_0_), channel_id=1, source_target_pairs={{0,4},{4,0},{8,12},{12,8},{16,20},{20,16},{24,28},{28,24},{1,5},{5... | collective-permute-start | bytes 399368 | tf_op jit(solution)/shard_map/ppermute | solution.py:359
  12.8 1.5 %collective-permute-start.4 = (bf16[8,8320]{1,0:T(8,128)(2,1)S(1)}, bf16[8,8320]{1,0:T(8,128)(2,1)S(1)}, u32[]{:S(2)}, u32[]{:S(2)}) collective-permute-start(bf16[8,8320]{1,0:T(8,128)(2,1)S(1)} %collective-permute-done.3.refs_2_), channel_id=1, source_target_pairs={{0,4},{4,0},{8,12},{12,8},{16,20},{20,16},{24,28},{28,24},{1,5},{5... | collective-permute-start | bytes 399368 | tf_op jit(solution)/shard_map/ppermute | solution.py:359
  17.6 4.7 %collective-permute-start.11 = (bf16[2,8,512]{2,1,0:T(8,128)(2,1)S(1)}, bf16[2,8,512]{2,1,0:T(8,128)(2,1)S(1)}, u32[]{:S(2)}, u32[]{:S(2)}) collective-permute-start(bf16[2,8,512]{2,1,0:T(8,128)(2,1)S(1)} %get-tuple-element.26), channel_id=1, source_target_pairs={{0,24},{4,28},{8,16},{12,20},{16,8},{20,12},{24,0},{28,4},{1,25},{... | collective-permute-start | bytes 49160 | tf_op jit(solution)/shard_map/ppermute | solution.py:359
  19.7 3.7 %collective-permute-start.12 = (bf16[2,8,512]{2,1,0:T(8,128)(2,1)S(1)}, bf16[2,8,512]{2,1,0:T(8,128)(2,1)S(1)}, u32[]{:S(2)}, u32[]{:S(2)}) collective-permute-start(bf16[2,8,512]{2,1,0:T(8,128)(2,1)S(1)} %get-tuple-element.27), channel_id=1, source_target_pairs={{0,16},{4,20},{8,24},{12,28},{16,0},{20,4},{24,8},{28,12},{1,17},{... | collective-permute-start | bytes 49160 | tf_op jit(solution)/shard_map/ppermute | solution.py:359
  20.7 3.1 %collective-permute-start.10 = (bf16[8,512]{1,0:T(8,128)(2,1)S(1)}, bf16[8,512]{1,0:T(8,128)(2,1)S(1)}, u32[]{:S(2)}, u32[]{:S(2)}) collective-permute-start(bf16[8,512]{1,0:T(8,128)(2,1)S(1)} %get-tuple-element.25), channel_id=1, source_target_pairs={{0,12},{4,8},{8,4},{12,0},{16,28},{20,24},{24,20},{28,16},{1,13},{... | collective-permute-start | bytes 24584 | tf_op jit(solution)/shard_map/ppermute | solution.py:359
  20.7 3.7 %collective-permute-start.9 = (bf16[8,512]{1,0:T(8,128)(2,1)S(1)}, bf16[8,512]{1,0:T(8,128)(2,1)S(1)}, u32[]{:S(2)}, u32[]{:S(2)}) collective-permute-start(bf16[8,512]{1,0:T(8,128)(2,1)S(1)} %get-tuple-element.24), channel_id=1, source_target_pairs={{0,8},{4,12},{8,0},{12,4},{16,24},{20,28},{24,16},{28,20},{1,9},{5... | collective-permute-start | bytes 24584 | tf_op jit(solution)/shard_map/ppermute | solution.py:359
  23.5 1.2 %collective-permute-start.13 = (bf16[3,8,512]{2,1,0:T(8,128)(2,1)S(1)}, bf16[3,8,512]{2,1,0:T(8,128)(2,1)S(1)}, u32[]{:S(2)}, u32[]{:S(2)}) collective-permute-start(bf16[3,8,512]{2,1,0:T(8,128)(2,1)S(1)} %shard_map.70), channel_id=1, source_target_pairs={{0,4},{4,0},{8,12},{12,8},{16,20},{20,16},{24,28},{28,24},{1,5},{5... | collective-permute-start | bytes 73736 | tf_op jit(solution)/shard_map/ppermute | solution.py:359

commit v7 on v6

--- a/solution.py
+++ b/solution.py
@@ -7,8 +7,10 @@
 
 LANES = 128
 CORES = 2
-HEAD = 256
 SOME_VMEM = 16 << 20
+SMALL_VMEM = 8 << 20
+FACTORS_FIRST = 6 * 10**9
+STRAIGHT_FIRST = 10**10
 VMEM = pl.BlockSpec(memory_space=pltpu.VMEM)
 HBM = pl.BlockSpec(memory_space=pltpu.HBM)
 F32 = jnp.float32
@@ -74,6 +76,10 @@
         copy.wait()
 
 
+def in_hbm(x):
+    return pltpu.with_memory_space_constraint(x, pltpu.HBM)
+
+
 def pack(queries, block_ids, left, right):
     rows, width = queries.shape
     blocks, cut = left.shape[:2]
@@ -92,7 +98,7 @@
             pltpu.SemaphoreType.DMA((8,)),
         ],
         compiler_params=pltpu.CompilerParams(vmem_limit_bytes=SOME_VMEM),
-    )(*(pltpu.with_memory_space_constraint(x, pltpu.HBM) for x in (queries, block_ids, left, right)))
+    )(*(in_hbm(x) for x in (queries, block_ids, left, right)))
 
 
 def prepare(slots, left_all, right_all, in_s, mid_s, out_s, prep_ref):
@@ -175,8 +181,8 @@
         ),
         in_specs=[VMEM] * len(factors),
         out_specs=(VMEM, VMEM),
-        compiler_params=pltpu.CompilerParams(vmem_limit_bytes=8 << 20),
-        cost_estimate=pl.CostEstimate(flops=6 * 10**9, bytes_accessed=10**6, transcendentals=0),
+        compiler_params=pltpu.CompilerParams(vmem_limit_bytes=SMALL_VMEM),
+        cost_estimate=pl.CostEstimate(flops=FACTORS_FIRST, bytes_accessed=10**6, transcendentals=0),
     )(*factors)
 
 
@@ -210,6 +216,7 @@
     width = clips_ref.shape[1]
     rows = slots[0].shape[0]
     prepare(slots, left_ref[...], right_ref[...], in_s, mid_s, out_s, prep_s)
+
     @pl.when(lax.axis_index("qry") >= 0)
     def _():
         queries = jnp.concatenate([early_ref[...], prep_s[...]], axis=0)
@@ -218,9 +225,10 @@
         scores = raw.T * factor
         core = lax.rem(lax.axis_index("own"), CORES)
         for j, (mine, other) in enumerate(((0, 0), (3, 3), (1 + core, 2 - core), (2 - core, 1 + core))):
-            at = 2 * j * rows
+            at = j * rows
             all_s[mine, core] = scores[at : at + rows].astype(BF16)
-            all_s[other, 1 - core] = scores[at + rows : at + 2 * rows].astype(BF16)
+            at += scores.shape[0] // 2
+            all_s[other, 1 - core] = scores[at : at + rows].astype(BF16)
         home_ref[...] = scores[:rows]
         near_ref[...] = all_s[0, 1 - core]
         x_ref[...] = all_s[1, core]
@@ -254,10 +262,6 @@
     )(*slots, prepared, left_all, right_all, clip_grads, lengths.reshape(1, clips))
 
 
-def in_hbm(x):
-    return pltpu.with_memory_space_constraint(x, pltpu.HBM)
-
-
 def join_kernel(order_a, cut, first_ref, second_ref, row_ref, both_ref, again_ref):
     blocks, depth = first_ref.shape[1:3]
     for j, ref in enumerate((first_ref, second_ref)):
@@ -279,7 +283,7 @@
         ),
         in_specs=[VMEM] * 3,
         out_specs=(VMEM, VMEM),
-        compiler_params=pltpu.CompilerParams(vmem_limit_bytes=8 << 20),
+        compiler_params=pltpu.CompilerParams(vmem_limit_bytes=SMALL_VMEM),
     )(first, second, row)
 
 
@@ -296,7 +300,7 @@
         out_shape=jax.ShapeDtypeStruct((3,) + near.shape, near.dtype),
         in_specs=[VMEM] * 3,
         out_specs=VMEM,
-        compiler_params=pltpu.CompilerParams(vmem_limit_bytes=8 << 20),
+        compiler_params=pltpu.CompilerParams(vmem_limit_bytes=SMALL_VMEM),
     )(d, y, near)
 
 
@@ -311,8 +315,8 @@
         out_shape=jax.ShapeDtypeStruct((len(parts),) + parts[0].shape, F32),
         in_specs=[VMEM] * len(parts),
         out_specs=VMEM,
-        compiler_params=pltpu.CompilerParams(vmem_limit_bytes=8 << 20),
-        cost_estimate=pl.CostEstimate(flops=10**10, bytes_accessed=10**6, transcendentals=0),
+        compiler_params=pltpu.CompilerParams(vmem_limit_bytes=SMALL_VMEM),
+        cost_estimate=pl.CostEstimate(flops=STRAIGHT_FIRST, bytes_accessed=10**6, transcendentals=0),
     )(*parts)
 
 
@@ -348,7 +352,7 @@
         in_specs=[VMEM] * len(parts),
         out_specs=HBM,
         scratch_shapes=[pltpu.VMEM(wide, F32), pltpu.SemaphoreType.DMA(())],
-        compiler_params=pltpu.CompilerParams(vmem_limit_bytes=8 << 20),
+        compiler_params=pltpu.CompilerParams(vmem_limit_bytes=SMALL_VMEM),
     )(*parts)
 
 
@@ -363,14 +367,14 @@
 
     def across(x, flips):
         return move(x, lambda chip, core: (chip ^ flips[core]) * CORES + core)
+
+    def plane(x, step):
+        return lax.ppermute(x, "qry", [(i, i ^ step) for i in range(planes)])
 
     flips_a, flips_b = (1, 2), (2, 1)
     row, fac = pack(queries[0], block_ids, left_factor, right_factor)
     slot_d = across(row, (3, 3))
     slot_a = across(row, flips_a)
-    def plane(x, step):
-        return lax.ppermute(x, "qry", [(i, i ^ step) for i in range(planes)])
-
     held, again = join(fac, plane(fac, 1), row, left_factor)
     factors = [held]
     step = 2
@@ -383,10 +387,9 @@
     slot_b = across(again, flips_b)
     order_a, order_b = left_factor.shape[2], right_factor.shape[2]
     left_all, right_all = place_factors(factors, left_factor.shape[0], order_a, order_b)
-    prepared = early(
-        [row, sibling(row), slot_d, sibling(slot_d)], left_all, right_all, order_a, order_b
-    )
-    home, near, x, cross, y, d = score([slot_a, sibling(slot_a), slot_b, sibling(slot_b)], prepared, left_all, right_all, clip_grads, lengths)
+    prepared = early([row, slot_d, slot_a, slot_b], left_all, right_all, order_a, order_b)
+    passed = [sibling(row), sibling(slot_d), sibling(slot_a), sibling(slot_b)]
+    home, near, x, cross, y, d = score(passed, prepared, left_all, right_all, clip_grads, lengths)
     y, d = across(y, (2, 2)), across(d, (3, 3))
     x, cross = across(x, (1, 1)), move(cross, lambda chip, core: (chip ^ 1) * CORES + 1 - core)
     return place(widen(home, x, cross), d, y, sibling(relay(d, y, near)))[None]

time: 25.6 us -> 25.6 us (level)
  no operation moved by 1% of the time
where the time goes in v7:
time: 25.6 us; the launch traced here: 25.4 us
  starting transfers between devices  14.9 us (58%)
  Pallas kernels  5.86 us (23%)
  waiting for transfers between devices  4.47 us (17%)
    ppermute x12, starting transfers between devices, move(): lax.ppermute(x, 'own', [(i, to(i // CORES, i % CORES)) for i in range(siz...  9.26 us
    ppermute x2, starting transfers between devices, plane(): return lax.ppermute(x, 'qry', [(i, i ^ step) for i in range(planes)])  5.68 us
    ppermute x12, waiting for transfers between devices, move(): lax.ppermute(x, 'own', [(i, to(i // CORES, i % CORES)) for i in range(siz...  4.46 us
    pallas_call x1, Pallas kernels, score(): pl.pallas_call(lambda *refs: score_kernel(len(slots), *refs), out_shape=(...  3.26 us
    pallas_call x1, Pallas kernels, pack(): pl.pallas_call(pack_kernel, out_shape=(jax.ShapeDtypeStruct((rows, width...  0.89 us
    pallas_call x1, Pallas kernels, early(): pl.pallas_call(lambda *refs: early_kernel(len(slots), *refs), out_shape=j...  0.88 us
    pallas_call x1, Pallas kernels, place(): pl.pallas_call(place_kernel, out_shape=jax.ShapeDtypeStruct(wide, F32), i...  0.68 us
  transfers between devices with their start and end apart: 14, of which 6 were waited for; matrix products, arithmetic and copies ran while one was open for 0% of the time, Pallas kernels for 4%

profile of v7, /device:TPU:0, one launch (start us, length us, event | category | flops | bytes accessed | tf_op | source)
XLA Modules:
  0.0 25.4 jit_solution(67595367752949648)
XLA Ops:
  0.0 0.9 %shard_map.64 = (bf16[8,8320]{1,0:T(8,128)(2,1)S(1)}, bf16[1,2,48,128]{3,2,1,0:T(8,128)(2,1)S(1)}) custom-call(bf16[8,8192]{1,0:T(8,128)(2,1)} %bitcast.6, s32[1,8]{1,0:T(1,128)} %ids_hbm.1, bf16[2,16,64]{2,1,0:T(8,128)(2,1)} %left_hbm.1, bf16[2,32,128]{2,1,0:T(8,128)(2,1)} %right_hbm.1), custom_call_target="tpu_custom_call" | custom-call | tf_op jit(solution)/shard_map/pallas_call | solution.py:87
  0.9 3.1 %collective-permute-start.5 = (bf16[1,2,48,128]{3,2,1,0:T(8,128)(2,1)S(1)}, bf16[1,2,48,128]{3,2,1,0:T(8,128)(2,1)S(1)}, u32[]{:S(2)}, u32[]{:S(2)}) collective-permute-start(bf16[1,2,48,128]{3,2,1,0:T(8,128)(2,1)S(1)} %get-tuple-element.18.refs_0_), channel_id=1, source_target_pairs={{0,1},{1,0},{2,3},{3,2},{4,5},{5,4},{6,7},{7,6},{8,9},{9,8},{10,11... | collective-permute-start | bytes 73736 | tf_op jit(solution)/shard_map/ppermute | solution.py:372
  4.0 2.4 %collective-permute-start.1 = (bf16[8,8320]{1,0:T(8,128)(2,1)S(1)}, bf16[8,8320]{1,0:T(8,128)(2,1)S(1)}, u32[]{:S(2)}, u32[]{:S(2)}) collective-permute-start(bf16[8,8320]{1,0:T(8,128)(2,1)S(1)} %get-tuple-element.17.refs_2_.refs_0_), channel_id=1, source_target_pairs={{0,24},{4,28},{8,16},{12,20},{16,8},{20,12},{24,0},{28,4},{1,25},{... | collective-permute-start | bytes 399368 | tf_op jit(solution)/shard_map/ppermute | solution.py:363
  6.4 0.5 %collective-permute-start.3 = (bf16[8,8320]{1,0:T(8,128)(2,1)S(1)}, bf16[8,8320]{1,0:T(8,128)(2,1)S(1)}, u32[]{:S(2)}, u32[]{:S(2)}) collective-permute-start(bf16[8,8320]{1,0:T(8,128)(2,1)S(1)} %get-tuple-element.17.refs_2_.refs_0_), channel_id=1, source_target_pairs={{0,8},{4,20},{8,0},{12,28},{16,24},{20,4},{24,16},{28,12},{1,9},{5... | collective-permute-start | bytes 399368 | tf_op jit(solution)/shard_map/ppermute | solution.py:363
  7.0 0.1 shard_map.65
  7.0 0.8 %collective-permute-start.6 = (bf16[8,8320]{1,0:T(8,128)(2,1)S(1)}, bf16[8,8320]{1,0:T(8,128)(2,1)S(1)}, u32[]{:S(2)}, u32[]{:S(2)}) collective-permute-start(bf16[8,8320]{1,0:T(8,128)(2,1)S(1)} %get-tuple-element.19), channel_id=1, source_target_pairs={{0,16},{4,12},{8,24},{12,4},{16,0},{20,28},{24,8},{28,20},{1,17},{... | collective-permute-start | bytes 399368 | tf_op jit(solution)/shard_map/ppermute | solution.py:363
  7.9 2.6 %collective-permute-start.8 = (bf16[2,80,128]{2,1,0:T(8,128)(2,1)S(1)}, bf16[2,80,128]{2,1,0:T(8,128)(2,1)S(1)}, u32[]{:S(2)}, u32[]{:S(2)}) collective-permute-start(bf16[2,80,128]{2,1,0:T(8,128)(2,1)S(1)} %get-tuple-element.20.refs_0_), channel_id=1, source_target_pairs={{0,2},{1,3},{2,0},{3,1},{4,6},{5,7},{6,4},{7,5},{8,10},{9,11},{10,... | collective-permute-start | bytes 122888 | tf_op jit(solution)/shard_map/ppermute | solution.py:372
  10.4 0.0 collective-permute-start
  10.5 0.5 %collective-permute-start.2 = (bf16[8,8320]{1,0:T(8,128)(2,1)S(1)}, bf16[8,8320]{1,0:T(8,128)(2,1)S(1)}, u32[]{:S(2)}, u32[]{:S(2)}) collective-permute-start(bf16[8,8320]{1,0:T(8,128)(2,1)S(1)} %collective-permute-done.1.refs_1_), channel_id=1, source_target_pairs={{0,4},{4,0},{8,12},{12,8},{16,20},{20,16},{24,28},{28,24},{1,5},{5... | collective-permute-start | bytes 399368 | tf_op jit(solution)/shard_map/ppermute | solution.py:363
  11.0 1.8 %collective-permute-done.3.refs_2_ = bf16[8,8320]{1,0:T(8,128)(2,1)S(1)} collective-permute-done((bf16[8,8320]{1,0:T(8,128)(2,1)S(1)}, bf16[8,8320]{1,0:T(8,128)(2,1)S(1)}, u32[]{:S(2)}, u32[]{:S(2)}) %collective-permute-start.3) | collective-permute-done | bytes 133152 | tf_op jit(solution)/shard_map/ppermute | solution.py:363
  12.8 0.5 %collective-permute-start.7 = (bf16[8,8320]{1,0:T(8,128)(2,1)S(1)}, bf16[8,8320]{1,0:T(8,128)(2,1)S(1)}, u32[]{:S(2)}, u32[]{:S(2)}) collective-permute-start(bf16[8,8320]{1,0:T(8,128)(2,1)S(1)} %collective-permute-done.6.refs_3_), channel_id=1, source_target_pairs={{0,4},{4,0},{8,12},{12,8},{16,20},{20,16},{24,28},{28,24},{1,5},{5... | collective-permute-start | bytes 399368 | tf_op jit(solution)/shard_map/ppermute | solution.py:363
  13.3 0.1 shard_map.66
  13.4 0.9 %shard_map.67.refs_4_ = bf16[32,8192]{1,0:T(8,128)(2,1)S(1)} custom-call(bf16[8,8320]{1,0:T(8,128)(2,1)S(1)} %get-tuple-element.17.refs_2_.refs_0_, bf16[8,8320]{1,0:T(8,128)(2,1)S(1)} %collective-permute-done.1.refs_1_, bf16[8,8320]{1,0:T(8,128)(2,1)S(1)} %collective-permute-done.3.refs_2_, bf16[8,8320]{1,0:T(8,128)(2,1)S(1)} %collective-permute-done.6.refs_3_, ...), custom_call_target="tpu_custom_call" | custom-call | flops 268435456 | bytes 1048576 | tf_op jit(solution)/shard_map/pallas_call | solution.py:199
  14.3 0.0 collective-permute-done.7.refs_3_
  14.4 3.3 %shard_map.68 = (f32[8,512]{1,0:T(8,128)S(1)}, bf16[8,512]{1,0:T(8,128)(2,1)S(1)}, bf16[8,512]{1,0:T(8,128)(2,1)S(1)}, bf16[8,512]{1,0:T(8,128)(2,1)S(1)}, bf16[...) custom-call(bf16[8,8320]{1,0:T(8,128)(2,1)S(1)} %collective-permute-done.refs_0_, ...), custom_call_target="tpu_custom_call" | custom-call | flops 1585446912 | bytes 8388608 | tf_op jit(solution)/shard_map/pallas_call | solution.py:245
  17.6 2.1 %collective-permute-start.11 = (bf16[2,8,512]{2,1,0:T(8,128)(2,1)S(1)}, bf16[2,8,512]{2,1,0:T(8,128)(2,1)S(1)}, u32[]{:S(2)}, u32[]{:S(2)}) collective-permute-start(bf16[2,8,512]{2,1,0:T(8,128)(2,1)S(1)} %get-tuple-element.26), channel_id=1, source_target_pairs={{0,24},{4,28},{8,16},{12,20},{16,8},{20,12},{24,0},{28,4},{1,25},{... | collective-permute-start | bytes 49160 | tf_op jit(solution)/shard_map/ppermute | solution.py:363
  19.7 1.0 %collective-permute-start.12 = (bf16[2,8,512]{2,1,0:T(8,128)(2,1)S(1)}, bf16[2,8,512]{2,1,0:T(8,128)(2,1)S(1)}, u32[]{:S(2)}, u32[]{:S(2)}) collective-permute-start(bf16[2,8,512]{2,1,0:T(8,128)(2,1)S(1)} %get-tuple-element.27), channel_id=1, source_target_pairs={{0,16},{4,20},{8,24},{12,28},{16,0},{20,4},{24,8},{28,12},{1,17},{... | collective-permute-start | bytes 49160 | tf_op jit(solution)/shard_map/ppermute | solution.py:363
  20.7 1.4 %collective-permute-start.9 = (bf16[8,512]{1,0:T(8,128)(2,1)S(1)}, bf16[8,512]{1,0:T(8,128)(2,1)S(1)}, u32[]{:S(2)}, u32[]{:S(2)}) collective-permute-start(bf16[8,512]{1,0:T(8,128)(2,1)S(1)} %get-tuple-element.24), channel_id=1, source_target_pairs={{0,8},{4,12},{8,0},{12,4},{16,24},{20,28},{24,16},{28,20},{1,9},{5... | collective-permute-start | bytes 24584 | tf_op jit(solution)/shard_map/ppermute | solution.py:363
  22.1 0.2 collective-permute-done.11.d_ref
  22.3 1.1 %collective-permute-done.12.y_ref = bf16[2,8,512]{2,1,0:T(8,128)(2,1)S(1)} collective-permute-done((bf16[2,8,512]{2,1,0:T(8,128)(2,1)S(1)}, bf16[2,8,512]{2,1,0:T(8,128)(2,1)S(1)}, u32[]{:S(2)}, u32[]{:S(2)}) %collective-permute-start.12) | collective-permute-done | bytes 16416 | tf_op jit(solution)/shard_map/ppermute | solution.py:363
  23.5 0.3 %collective-permute-done.10.cross_ref = bf16[8,512]{1,0:T(8,128)(2,1)S(1)} collective-permute-done((bf16[8,512]{1,0:T(8,128)(2,1)S(1)}, bf16[8,512]{1,0:T(8,128)(2,1)S(1)}, u32[]{:S(2)}, u32[]{:S(2)}) %collective-permute-start.10) | collective-permute-done | bytes 8224 | tf_op jit(solution)/shard_map/ppermute | solution.py:363
  23.8 0.6 %collective-permute-done.9.x_ref = bf16[8,512]{1,0:T(8,128)(2,1)S(1)} collective-permute-done((bf16[8,512]{1,0:T(8,128)(2,1)S(1)}, bf16[8,512]{1,0:T(8,128)(2,1)S(1)}, u32[]{:S(2)}, u32[]{:S(2)}) %collective-permute-start.9) | collective-permute-done | bytes 8224 | tf_op jit(solution)/shard_map/ppermute | solution.py:363
  24.4 0.3 %collective-permute-done.13.relayed_ref = bf16[3,8,512]{2,1,0:T(8,128)(2,1)S(1)} collective-permute-done((bf16[3,8,512]{2,1,0:T(8,128)(2,1)S(1)}, bf16[3,8,512]{2,1,0:T(8,128)(2,1)S(1)}, u32[]{:S(2)}, u32[]{:S(2)}) %collective-permute-start.13) | collective-permute-done | bytes 24608 | tf_op jit(solution)/shard_map/ppermute | solution.py:363
  24.7 0.7 %shard_map.71 = f32[8,4096]{1,0:T(8,128)} custom-call(f32[3,8,512]{2,1,0:T(8,128)S(1)} %shard_map.69.wide_ref, bf16[2,8,512]{2,1,0:T(8,128)(2,1)S(1)} %collective-permute-done.11.d_ref, bf16[2,8,512]{2,1,0:T(8,128)(2,1)S(1)} %collective-permute-done.12.y_ref, bf16[3,8,512]{2,1,0:T(8,128)(2,1)S(1)} %collective-permute-done.13.relayed_ref), custom_call_target="tpu_custom_call" | custom-call | tf_op jit(solution)/shard_map/pallas_call | solution.py:349
  (19 shorter events, 0.0 us)
Async XLA Ops:
  0.9 6.1 %collective-permute-start.5 = (bf16[1,2,48,128]{3,2,1,0:T(8,128)(2,1)S(1)}, bf16[1,2,48,128]{3,2,1,0:T(8,128)(2,1)S(1)}, u32[]{:S(2)}, u32[]{:S(2)}) collective-permute-start(bf16[1,2,48,128]{3,2,1,0:T(8,128)(2,1)S(1)} %get-tuple-element.18.refs_0_), channel_id=1, source_target_pairs={{0,1},{1,0},{2,3},{3,2},{4,5},{5,4},{6,7},{7,6},{8,9},{9,8},{10,11... | collective-permute-start | bytes 73736 | tf_op jit(solution)/shard_map/ppermute | solution.py:372
  4.0 6.5 %collective-permute-start.1 = (bf16[8,8320]{1,0:T(8,128)(2,1)S(1)}, bf16[8,8320]{1,0:T(8,128)(2,1)S(1)}, u32[]{:S(2)}, u32[]{:S(2)}) collective-permute-start(bf16[8,8320]{1,0:T(8,128)(2,1)S(1)} %get-tuple-element.17.refs_2_.refs_0_), channel_id=1, source_target_pairs={{0,24},{4,28},{8,16},{12,20},{16,8},{20,12},{24,0},{28,4},{1,25},{... | collective-permute-start | bytes 399368 | tf_op jit(solution)/shard_map/ppermute | solution.py:363
  6.4 6.4 %collective-permute-start.3 = (bf16[8,8320]{1,0:T(8,128)(2,1)S(1)}, bf16[8,8320]{1,0:T(8,128)(2,1)S(1)}, u32[]{:S(2)}, u32[]{:S(2)}) collective-permute-start(bf16[8,8320]{1,0:T(8,128)(2,1)S(1)} %get-tuple-element.17.refs_2_.refs_0_), channel_id=1, source_target_pairs={{0,8},{4,20},{8,0},{12,28},{16,24},{20,4},{24,16},{28,12},{1,9},{5... | collective-permute-start | bytes 399368 | tf_op jit(solution)/shard_map/ppermute | solution.py:363
  7.0 5.8 %collective-permute-start.6 = (bf16[8,8320]{1,0:T(8,128)(2,1)S(1)}, bf16[8,8320]{1,0:T(8,128)(2,1)S(1)}, u32[]{:S(2)}, u32[]{:S(2)}) collective-permute-start(bf16[8,8320]{1,0:T(8,128)(2,1)S(1)} %get-tuple-element.19), channel_id=1, source_target_pairs={{0,16},{4,12},{8,24},{12,4},{16,0},{20,28},{24,8},{28,20},{1,17},{... | collective-permute-start | bytes 399368 | tf_op jit(solution)/shard_map/ppermute | solution.py:363
  7.8 6.5 %slice-start = ((s8[8388608]{0:T(1024)(128)(4,1)}), s8[4194304]{0:T(1024)(128)(4,1)S(1)}, s32[]{:S(2)}) async-start(s8[8388608]{0:T(1024)(128)(4,1)} %bitcast.3), calls=%async_computation | async-start | bytes 8388608
  7.9 6.5 %slice-start.1 = ((s8[8388608]{0:T(1024)(128)(4,1)}), s8[4194304]{0:T(1024)(128)(4,1)S(1)}, s32[]{:S(2)}) async-start(s8[8388608]{0:T(1024)(128)(4,1)} %bitcast.3), calls=%async_computation.1 | async-start | bytes 8388608
  7.9 6.5 %copy-start = (s32[512]{0:T(512)S(1)}, s32[512]{0:T(512)}, u32[]{:S(2)}) copy-start(s32[512]{0:T(512)} %param.11) | copy-start | bytes 6148
  7.9 5.5 %collective-permute-start.8 = (bf16[2,80,128]{2,1,0:T(8,128)(2,1)S(1)}, bf16[2,80,128]{2,1,0:T(8,128)(2,1)S(1)}, u32[]{:S(2)}, u32[]{:S(2)}) collective-permute-start(bf16[2,80,128]{2,1,0:T(8,128)(2,1)S(1)} %get-tuple-element.20.refs_0_), channel_id=1, source_target_pairs={{0,2},{1,3},{2,0},{3,1},{4,6},{5,7},{6,4},{7,5},{8,10},{9,11},{10,... | collective-permute-start | bytes 122888 | tf_op jit(solution)/shard_map/ppermute | solution.py:372
  10.4 3.8 %collective-permute-start = (bf16[8,8320]{1,0:T(8,128)(2,1)S(1)}, bf16[8,8320]{1,0:T(8,128)(2,1)S(1)}, u32[]{:S(2)}, u32[]{:S(2)}) collective-permute-start(bf16[8,8320]{1,0:T(8,128)(2,1)S(1)} %get-tuple-element.17.refs_2_.refs_0_), channel_id=1, source_target_pairs={{0,4},{4,0},{8,12},{12,8},{16,20},{20,16},{24,28},{28,24},{1,5},{5... | collective-permute-start | bytes 399368 | tf_op jit(solution)/shard_map/ppermute | solution.py:363
  10.5 3.8 %collective-permute-start.2 = (bf16[8,8320]{1,0:T(8,128)(2,1)S(1)}, bf16[8,8320]{1,0:T(8,128)(2,1)S(1)}, u32[]{:S(2)}, u32[]{:S(2)}) collective-permute-start(bf16[8,8320]{1,0:T(8,128)(2,1)S(1)} %collective-permute-done.1.refs_1_), channel_id=1, source_target_pairs={{0,4},{4,0},{8,12},{12,8},{16,20},{20,16},{24,28},{28,24},{1,5},{5... | collective-permute-start | bytes 399368 | tf_op jit(solution)/shard_map/ppermute | solution.py:363
  12.8 1.5 %collective-permute-start.4 = (bf16[8,8320]{1,0:T(8,128)(2,1)S(1)}, bf16[8,8320]{1,0:T(8,128)(2,1)S(1)}, u32[]{:S(2)}, u32[]{:S(2)}) collective-permute-start(bf16[8,8320]{1,0:T(8,128)(2,1)S(1)} %collective-permute-done.3.refs_2_), channel_id=1, source_target_pairs={{0,4},{4,0},{8,12},{12,8},{16,20},{20,16},{24,28},{28,24},{1,5},{5... | collective-permute-start | bytes 399368 | tf_op jit(solution)/shard_map/ppermute | solution.py:363
  12.8 1.5 %collective-permute-start.7 = (bf16[8,8320]{1,0:T(8,128)(2,1)S(1)}, bf16[8,8320]{1,0:T(8,128)(2,1)S(1)}, u32[]{:S(2)}, u32[]{:S(2)}) collective-permute-start(bf16[8,8320]{1,0:T(8,128)(2,1)S(1)} %collective-permute-done.6.refs_3_), channel_id=1, source_target_pairs={{0,4},{4,0},{8,12},{12,8},{16,20},{20,16},{24,28},{28,24},{1,5},{5... | collective-permute-start | bytes 399368 | tf_op jit(solution)/shard_map/ppermute | solution.py:363
  17.6 4.7 %collective-permute-start.11 = (bf16[2,8,512]{2,1,0:T(8,128)(2,1)S(1)}, bf16[2,8,512]{2,1,0:T(8,128)(2,1)S(1)}, u32[]{:S(2)}, u32[]{:S(2)}) collective-permute-start(bf16[2,8,512]{2,1,0:T(8,128)(2,1)S(1)} %get-tuple-element.26), channel_id=1, source_target_pairs={{0,24},{4,28},{8,16},{12,20},{16,8},{20,12},{24,0},{28,4},{1,25},{... | collective-permute-start | bytes 49160 | tf_op jit(solution)/shard_map/ppermute | solution.py:363
  19.7 3.7 %collective-permute-start.12 = (bf16[2,8,512]{2,1,0:T(8,128)(2,1)S(1)}, bf16[2,8,512]{2,1,0:T(8,128)(2,1)S(1)}, u32[]{:S(2)}, u32[]{:S(2)}) collective-permute-start(bf16[2,8,512]{2,1,0:T(8,128)(2,1)S(1)} %get-tuple-element.27), channel_id=1, source_target_pairs={{0,16},{4,20},{8,24},{12,28},{16,0},{20,4},{24,8},{28,12},{1,17},{... | collective-permute-start | bytes 49160 | tf_op jit(solution)/shard_map/ppermute | solution.py:363
  20.7 3.1 %collective-permute-start.10 = (bf16[8,512]{1,0:T(8,128)(2,1)S(1)}, bf16[8,512]{1,0:T(8,128)(2,1)S(1)}, u32[]{:S(2)}, u32[]{:S(2)}) collective-permute-start(bf16[8,512]{1,0:T(8,128)(2,1)S(1)} %get-tuple-element.25), channel_id=1, source_target_pairs={{0,12},{4,8},{8,4},{12,0},{16,28},{20,24},{24,20},{28,16},{1,13},{... | collective-permute-start | bytes 24584 | tf_op jit(solution)/shard_map/ppermute | solution.py:363
  20.7 3.7 %collective-permute-start.9 = (bf16[8,512]{1,0:T(8,128)(2,1)S(1)}, bf16[8,512]{1,0:T(8,128)(2,1)S(1)}, u32[]{:S(2)}, u32[]{:S(2)}) collective-permute-start(bf16[8,512]{1,0:T(8,128)(2,1)S(1)} %get-tuple-element.24), channel_id=1, source_target_pairs={{0,8},{4,12},{8,0},{12,4},{16,24},{20,28},{24,16},{28,20},{1,9},{5... | collective-permute-start | bytes 24584 | tf_op jit(solution)/shard_map/ppermute | solution.py:363
  23.5 1.2 %collective-permute-start.13 = (bf16[3,8,512]{2,1,0:T(8,128)(2,1)S(1)}, bf16[3,8,512]{2,1,0:T(8,128)(2,1)S(1)}, u32[]{:S(2)}, u32[]{:S(2)}) collective-permute-start(bf16[3,8,512]{2,1,0:T(8,128)(2,1)S(1)} %shard_map.70), channel_id=1, source_target_pairs={{0,4},{4,0},{8,12},{12,8},{16,20},{20,16},{24,28},{28,24},{1,5},{5... | collective-permute-start | bytes 73736 | tf_op jit(solution)/shard_map/ppermute | solution.py:363

commit v8 on v7

--- a/solution.py
+++ b/solution.py
@@ -7,6 +7,7 @@
 
 LANES = 128
 CORES = 2
+SIDE = 8
 SOME_VMEM = 16 << 20
 SMALL_VMEM = 8 << 20
 FACTORS_FIRST = 6 * 10**9
@@ -136,16 +137,19 @@
                 mid_s[group, n + j, :, :order_b] = high
                 mid_s[group, n + j, :, order_b:] = (one - high.astype(F32)).astype(BF16)
     for group in range(len(slots) // 2):
-        middle = mid_s[group].reshape(pair * order_a, 2 * order_b)
-        outer = jnp.dot(middle, right_all, preferred_element_type=F32)
-        for n in range(pair):
-            label = label_of(group, n)
-            one = outer[n * order_a : (n + 1) * order_a, :order_b]
-            for k in range(1, blocks):
-                one = jnp.where(
-                    label > k - 0.5, outer[n * order_a : (n + 1) * order_a, k * order_b : (k + 1) * order_b], one
-                )
-            out_s[group, n] = one.astype(BF16)
+        for first in range(0, pair, SIDE):
+            middle = mid_s[group, first : first + SIDE].reshape(SIDE * order_a, 2 * order_b)
+            outer = jnp.dot(middle, right_all, preferred_element_type=F32)
+            for j in range(SIDE):
+                label = label_of(group, first + j)
+                one = outer[j * order_a : (j + 1) * order_a, :order_b]
+                for k in range(1, blocks):
+                    one = jnp.where(
+                        label > k - 0.5,
+                        outer[j * order_a : (j + 1) * order_a, k * order_b : (k + 1) * order_b],
+                        one,
+                    )
+                out_s[group, first + j] = one.astype(BF16)
     for group in range(len(slots) // 2):
         turned = jnp.swapaxes(out_s[group], 0, 1)
         for a in range(order_a):

time: 25.6 us -> 25.6 us (level)
  no operation moved by 1% of the time
where the time goes in v8:
time: 25.6 us; the launch traced here: 25.4 us
  starting transfers between devices  14.9 us (58%)
  Pallas kernels  5.87 us (23%)
  waiting for transfers between devices  4.47 us (17%)
    ppermute x12, starting transfers between devices, move(): lax.ppermute(x, 'own', [(i, to(i // CORES, i % CORES)) for i in range(siz...  9.26 us
    ppermute x2, starting transfers between devices, plane(): return lax.ppermute(x, 'qry', [(i, i ^ step) for i in range(planes)])  5.68 us
    ppermute x12, waiting for transfers between devices, move(): lax.ppermute(x, 'own', [(i, to(i // CORES, i % CORES)) for i in range(siz...  4.47 us
    pallas_call x1, Pallas kernels, score(): pl.pallas_call(lambda *refs: score_kernel(len(slots), *refs), out_shape=(...  3.26 us
    pallas_call x1, Pallas kernels, pack(): pl.pallas_call(pack_kernel, out_shape=(jax.ShapeDtypeStruct((rows, width...  0.89 us
    pallas_call x1, Pallas kernels, early(): pl.pallas_call(lambda *refs: early_kernel(len(slots), *refs), out_shape=j...  0.88 us
    pallas_call x1, Pallas kernels, place(): pl.pallas_call(place_kernel, out_shape=jax.ShapeDtypeStruct(wide, F32), i...  0.68 us
  transfers between devices with their start and end apart: 14, of which 6 were waited for; matrix products, arithmetic and copies ran while one was open for 0% of the time, Pallas kernels for 4%

profile of v8, /device:TPU:0, one launch (start us, length us, event | category | flops | bytes accessed | tf_op | source)
XLA Modules:
  0.0 25.4 jit_solution(10507051105484342571)
XLA Ops:
  0.0 0.9 %shard_map.64 = (bf16[8,8320]{1,0:T(8,128)(2,1)S(1)}, bf16[1,2,48,128]{3,2,1,0:T(8,128)(2,1)S(1)}) custom-call(bf16[8,8192]{1,0:T(8,128)(2,1)} %bitcast.6, s32[1,8]{1,0:T(1,128)} %ids_hbm.1, bf16[2,16,64]{2,1,0:T(8,128)(2,1)} %left_hbm.1, bf16[2,32,128]{2,1,0:T(8,128)(2,1)} %right_hbm.1), custom_call_target="tpu_custom_call" | custom-call | tf_op jit(solution)/shard_map/pallas_call | solution.py:88
  0.9 3.1 %collective-permute-start.5 = (bf16[1,2,48,128]{3,2,1,0:T(8,128)(2,1)S(1)}, bf16[1,2,48,128]{3,2,1,0:T(8,128)(2,1)S(1)}, u32[]{:S(2)}, u32[]{:S(2)}) collective-permute-start(bf16[1,2,48,128]{3,2,1,0:T(8,128)(2,1)S(1)} %get-tuple-element.18.refs_0_), channel_id=1, source_target_pairs={{0,1},{1,0},{2,3},{3,2},{4,5},{5,4},{6,7},{7,6},{8,9},{9,8},{10,11... | collective-permute-start | bytes 73736 | tf_op jit(solution)/shard_map/ppermute | solution.py:376
  4.0 2.4 %collective-permute-start.1 = (bf16[8,8320]{1,0:T(8,128)(2,1)S(1)}, bf16[8,8320]{1,0:T(8,128)(2,1)S(1)}, u32[]{:S(2)}, u32[]{:S(2)}) collective-permute-start(bf16[8,8320]{1,0:T(8,128)(2,1)S(1)} %get-tuple-element.17.refs_2_.refs_0_), channel_id=1, source_target_pairs={{0,24},{4,28},{8,16},{12,20},{16,8},{20,12},{24,0},{28,4},{1,25},{... | collective-permute-start | bytes 399368 | tf_op jit(solution)/shard_map/ppermute | solution.py:367
  6.4 0.5 %collective-permute-start.3 = (bf16[8,8320]{1,0:T(8,128)(2,1)S(1)}, bf16[8,8320]{1,0:T(8,128)(2,1)S(1)}, u32[]{:S(2)}, u32[]{:S(2)}) collective-permute-start(bf16[8,8320]{1,0:T(8,128)(2,1)S(1)} %get-tuple-element.17.refs_2_.refs_0_), channel_id=1, source_target_pairs={{0,8},{4,20},{8,0},{12,28},{16,24},{20,4},{24,16},{28,12},{1,9},{5... | collective-permute-start | bytes 399368 | tf_op jit(solution)/shard_map/ppermute | solution.py:367
  7.0 0.1 shard_map.65
  7.0 0.8 %collective-permute-start.6 = (bf16[8,8320]{1,0:T(8,128)(2,1)S(1)}, bf16[8,8320]{1,0:T(8,128)(2,1)S(1)}, u32[]{:S(2)}, u32[]{:S(2)}) collective-permute-start(bf16[8,8320]{1,0:T(8,128)(2,1)S(1)} %get-tuple-element.19), channel_id=1, source_target_pairs={{0,16},{4,12},{8,24},{12,4},{16,0},{20,28},{24,8},{28,20},{1,17},{... | collective-permute-start | bytes 399368 | tf_op jit(solution)/shard_map/ppermute | solution.py:367
  7.9 2.6 %collective-permute-start.8 = (bf16[2,80,128]{2,1,0:T(8,128)(2,1)S(1)}, bf16[2,80,128]{2,1,0:T(8,128)(2,1)S(1)}, u32[]{:S(2)}, u32[]{:S(2)}) collective-permute-start(bf16[2,80,128]{2,1,0:T(8,128)(2,1)S(1)} %get-tuple-element.20.refs_0_), channel_id=1, source_target_pairs={{0,2},{1,3},{2,0},{3,1},{4,6},{5,7},{6,4},{7,5},{8,10},{9,11},{10,... | collective-permute-start | bytes 122888 | tf_op jit(solution)/shard_map/ppermute | solution.py:376
  10.5 0.5 %collective-permute-start.2 = (bf16[8,8320]{1,0:T(8,128)(2,1)S(1)}, bf16[8,8320]{1,0:T(8,128)(2,1)S(1)}, u32[]{:S(2)}, u32[]{:S(2)}) collective-permute-start(bf16[8,8320]{1,0:T(8,128)(2,1)S(1)} %collective-permute-done.1.refs_1_), channel_id=1, source_target_pairs={{0,4},{4,0},{8,12},{12,8},{16,20},{20,16},{24,28},{28,24},{1,5},{5... | collective-permute-start | bytes 399368 | tf_op jit(solution)/shard_map/ppermute | solution.py:367
  11.0 1.8 %collective-permute-done.3.refs_2_ = bf16[8,8320]{1,0:T(8,128)(2,1)S(1)} collective-permute-done((bf16[8,8320]{1,0:T(8,128)(2,1)S(1)}, bf16[8,8320]{1,0:T(8,128)(2,1)S(1)}, u32[]{:S(2)}, u32[]{:S(2)}) %collective-permute-start.3) | collective-permute-done | bytes 133152 | tf_op jit(solution)/shard_map/ppermute | solution.py:367
  12.8 0.0 collective-permute-start.4
  12.8 0.5 %collective-permute-start.7 = (bf16[8,8320]{1,0:T(8,128)(2,1)S(1)}, bf16[8,8320]{1,0:T(8,128)(2,1)S(1)}, u32[]{:S(2)}, u32[]{:S(2)}) collective-permute-start(bf16[8,8320]{1,0:T(8,128)(2,1)S(1)} %collective-permute-done.6.refs_3_), channel_id=1, source_target_pairs={{0,4},{4,0},{8,12},{12,8},{16,20},{20,16},{24,28},{28,24},{1,5},{5... | collective-permute-start | bytes 399368 | tf_op jit(solution)/shard_map/ppermute | solution.py:367
  13.3 0.1 shard_map.66
  13.4 0.9 %shard_map.67.refs_4_ = bf16[32,8192]{1,0:T(8,128)(2,1)S(1)} custom-call(bf16[8,8320]{1,0:T(8,128)(2,1)S(1)} %get-tuple-element.17.refs_2_.refs_0_, bf16[8,8320]{1,0:T(8,128)(2,1)S(1)} %collective-permute-done.1.refs_1_, bf16[8,8320]{1,0:T(8,128)(2,1)S(1)} %collective-permute-done.3.refs_2_, bf16[8,8320]{1,0:T(8,128)(2,1)S(1)} %collective-permute-done.6.refs_3_, ...), custom_call_target="tpu_custom_call" | custom-call | flops 268435456 | bytes 1048576 | tf_op jit(solution)/shard_map/pallas_call | solution.py:203
  14.3 0.0 collective-permute-done.7.refs_3_
  14.4 3.3 %shard_map.68 = (f32[8,512]{1,0:T(8,128)S(1)}, bf16[8,512]{1,0:T(8,128)(2,1)S(1)}, bf16[8,512]{1,0:T(8,128)(2,1)S(1)}, bf16[8,512]{1,0:T(8,128)(2,1)S(1)}, bf16[...) custom-call(bf16[8,8320]{1,0:T(8,128)(2,1)S(1)} %collective-permute-done.refs_0_, ...), custom_call_target="tpu_custom_call" | custom-call | flops 1585446912 | bytes 8388608 | tf_op jit(solution)/shard_map/pallas_call | solution.py:249
  17.6 2.1 %collective-permute-start.11 = (bf16[2,8,512]{2,1,0:T(8,128)(2,1)S(1)}, bf16[2,8,512]{2,1,0:T(8,128)(2,1)S(1)}, u32[]{:S(2)}, u32[]{:S(2)}) collective-permute-start(bf16[2,8,512]{2,1,0:T(8,128)(2,1)S(1)} %get-tuple-element.26), channel_id=1, source_target_pairs={{0,24},{4,28},{8,16},{12,20},{16,8},{20,12},{24,0},{28,4},{1,25},{... | collective-permute-start | bytes 49160 | tf_op jit(solution)/shard_map/ppermute | solution.py:367
  19.7 0.9 %collective-permute-start.12 = (bf16[2,8,512]{2,1,0:T(8,128)(2,1)S(1)}, bf16[2,8,512]{2,1,0:T(8,128)(2,1)S(1)}, u32[]{:S(2)}, u32[]{:S(2)}) collective-permute-start(bf16[2,8,512]{2,1,0:T(8,128)(2,1)S(1)} %get-tuple-element.27), channel_id=1, source_target_pairs={{0,16},{4,20},{8,24},{12,28},{16,0},{20,4},{24,8},{28,12},{1,17},{... | collective-permute-start | bytes 49160 | tf_op jit(solution)/shard_map/ppermute | solution.py:367
  20.7 1.4 %collective-permute-start.9 = (bf16[8,512]{1,0:T(8,128)(2,1)S(1)}, bf16[8,512]{1,0:T(8,128)(2,1)S(1)}, u32[]{:S(2)}, u32[]{:S(2)}) collective-permute-start(bf16[8,512]{1,0:T(8,128)(2,1)S(1)} %get-tuple-element.24), channel_id=1, source_target_pairs={{0,8},{4,12},{8,0},{12,4},{16,24},{20,28},{24,16},{28,20},{1,9},{5... | collective-permute-start | bytes 24584 | tf_op jit(solution)/shard_map/ppermute | solution.py:367
  22.1 0.2 collective-permute-done.11.d_ref
  22.3 1.1 %collective-permute-done.12.y_ref = bf16[2,8,512]{2,1,0:T(8,128)(2,1)S(1)} collective-permute-done((bf16[2,8,512]{2,1,0:T(8,128)(2,1)S(1)}, bf16[2,8,512]{2,1,0:T(8,128)(2,1)S(1)}, u32[]{:S(2)}, u32[]{:S(2)}) %collective-permute-start.12) | collective-permute-done | bytes 16416 | tf_op jit(solution)/shard_map/ppermute | solution.py:367
  23.5 0.3 %collective-permute-done.10.cross_ref = bf16[8,512]{1,0:T(8,128)(2,1)S(1)} collective-permute-done((bf16[8,512]{1,0:T(8,128)(2,1)S(1)}, bf16[8,512]{1,0:T(8,128)(2,1)S(1)}, u32[]{:S(2)}, u32[]{:S(2)}) %collective-permute-start.10) | collective-permute-done | bytes 8224 | tf_op jit(solution)/shard_map/ppermute | solution.py:367
  23.8 0.6 %collective-permute-done.9.x_ref = bf16[8,512]{1,0:T(8,128)(2,1)S(1)} collective-permute-done((bf16[8,512]{1,0:T(8,128)(2,1)S(1)}, bf16[8,512]{1,0:T(8,128)(2,1)S(1)}, u32[]{:S(2)}, u32[]{:S(2)}) %collective-permute-start.9) | collective-permute-done | bytes 8224 | tf_op jit(solution)/shard_map/ppermute | solution.py:367
  24.4 0.3 %collective-permute-done.13.relayed_ref = bf16[3,8,512]{2,1,0:T(8,128)(2,1)S(1)} collective-permute-done((bf16[3,8,512]{2,1,0:T(8,128)(2,1)S(1)}, bf16[3,8,512]{2,1,0:T(8,128)(2,1)S(1)}, u32[]{:S(2)}, u32[]{:S(2)}) %collective-permute-start.13) | collective-permute-done | bytes 24608 | tf_op jit(solution)/shard_map/ppermute | solution.py:367
  24.7 0.7 %shard_map.71 = f32[8,4096]{1,0:T(8,128)} custom-call(f32[3,8,512]{2,1,0:T(8,128)S(1)} %shard_map.69.wide_ref, bf16[2,8,512]{2,1,0:T(8,128)(2,1)S(1)} %collective-permute-done.11.d_ref, bf16[2,8,512]{2,1,0:T(8,128)(2,1)S(1)} %collective-permute-done.12.y_ref, bf16[3,8,512]{2,1,0:T(8,128)(2,1)S(1)} %collective-permute-done.13.relayed_ref), custom_call_target="tpu_custom_call" | custom-call | tf_op jit(solution)/shard_map/pallas_call | solution.py:353
  (19 shorter events, 0.0 us)
Async XLA Ops:
  0.9 6.1 %collective-permute-start.5 = (bf16[1,2,48,128]{3,2,1,0:T(8,128)(2,1)S(1)}, bf16[1,2,48,128]{3,2,1,0:T(8,128)(2,1)S(1)}, u32[]{:S(2)}, u32[]{:S(2)}) collective-permute-start(bf16[1,2,48,128]{3,2,1,0:T(8,128)(2,1)S(1)} %get-tuple-element.18.refs_0_), channel_id=1, source_target_pairs={{0,1},{1,0},{2,3},{3,2},{4,5},{5,4},{6,7},{7,6},{8,9},{9,8},{10,11... | collective-permute-start | bytes 73736 | tf_op jit(solution)/shard_map/ppermute | solution.py:376
  4.0 6.5 %collective-permute-start.1 = (bf16[8,8320]{1,0:T(8,128)(2,1)S(1)}, bf16[8,8320]{1,0:T(8,128)(2,1)S(1)}, u32[]{:S(2)}, u32[]{:S(2)}) collective-permute-start(bf16[8,8320]{1,0:T(8,128)(2,1)S(1)} %get-tuple-element.17.refs_2_.refs_0_), channel_id=1, source_target_pairs={{0,24},{4,28},{8,16},{12,20},{16,8},{20,12},{24,0},{28,4},{1,25},{... | collective-permute-start | bytes 399368 | tf_op jit(solution)/shard_map/ppermute | solution.py:367
  6.4 6.4 %collective-permute-start.3 = (bf16[8,8320]{1,0:T(8,128)(2,1)S(1)}, bf16[8,8320]{1,0:T(8,128)(2,1)S(1)}, u32[]{:S(2)}, u32[]{:S(2)}) collective-permute-start(bf16[8,8320]{1,0:T(8,128)(2,1)S(1)} %get-tuple-element.17.refs_2_.refs_0_), channel_id=1, source_target_pairs={{0,8},{4,20},{8,0},{12,28},{16,24},{20,4},{24,16},{28,12},{1,9},{5... | collective-permute-start | bytes 399368 | tf_op jit(solution)/shard_map/ppermute | solution.py:367
  7.0 5.8 %collective-permute-start.6 = (bf16[8,8320]{1,0:T(8,128)(2,1)S(1)}, bf16[8,8320]{1,0:T(8,128)(2,1)S(1)}, u32[]{:S(2)}, u32[]{:S(2)}) collective-permute-start(bf16[8,8320]{1,0:T(8,128)(2,1)S(1)} %get-tuple-element.19), channel_id=1, source_target_pairs={{0,16},{4,12},{8,24},{12,4},{16,0},{20,28},{24,8},{28,20},{1,17},{... | collective-permute-start | bytes 399368 | tf_op jit(solution)/shard_map/ppermute | solution.py:367
  7.8 6.5 %slice-start = ((s8[8388608]{0:T(1024)(128)(4,1)}), s8[4194304]{0:T(1024)(128)(4,1)S(1)}, s32[]{:S(2)}) async-start(s8[8388608]{0:T(1024)(128)(4,1)} %bitcast.3), calls=%async_computation | async-start | bytes 8388608
  7.9 6.5 %slice-start.1 = ((s8[8388608]{0:T(1024)(128)(4,1)}), s8[4194304]{0:T(1024)(128)(4,1)S(1)}, s32[]{:S(2)}) async-start(s8[8388608]{0:T(1024)(128)(4,1)} %bitcast.3), calls=%async_computation.1 | async-start | bytes 8388608
  7.9 6.5 %copy-start = (s32[512]{0:T(512)S(1)}, s32[512]{0:T(512)}, u32[]{:S(2)}) copy-start(s32[512]{0:T(512)} %param.11) | copy-start | bytes 6148
  7.9 5.5 %collective-permute-start.8 = (bf16[2,80,128]{2,1,0:T(8,128)(2,1)S(1)}, bf16[2,80,128]{2,1,0:T(8,128)(2,1)S(1)}, u32[]{:S(2)}, u32[]{:S(2)}) collective-permute-start(bf16[2,80,128]{2,1,0:T(8,128)(2,1)S(1)} %get-tuple-element.20.refs_0_), channel_id=1, source_target_pairs={{0,2},{1,3},{2,0},{3,1},{4,6},{5,7},{6,4},{7,5},{8,10},{9,11},{10,... | collective-permute-start | bytes 122888 | tf_op jit(solution)/shard_map/ppermute | solution.py:376
  10.4 3.8 %collective-permute-start = (bf16[8,8320]{1,0:T(8,128)(2,1)S(1)}, bf16[8,8320]{1,0:T(8,128)(2,1)S(1)}, u32[]{:S(2)}, u32[]{:S(2)}) collective-permute-start(bf16[8,8320]{1,0:T(8,128)(2,1)S(1)} %get-tuple-element.17.refs_2_.refs_0_), channel_id=1, source_target_pairs={{0,4},{4,0},{8,12},{12,8},{16,20},{20,16},{24,28},{28,24},{1,5},{5... | collective-permute-start | bytes 399368 | tf_op jit(solution)/shard_map/ppermute | solution.py:367
  10.5 3.8 %collective-permute-start.2 = (bf16[8,8320]{1,0:T(8,128)(2,1)S(1)}, bf16[8,8320]{1,0:T(8,128)(2,1)S(1)}, u32[]{:S(2)}, u32[]{:S(2)}) collective-permute-start(bf16[8,8320]{1,0:T(8,128)(2,1)S(1)} %collective-permute-done.1.refs_1_), channel_id=1, source_target_pairs={{0,4},{4,0},{8,12},{12,8},{16,20},{20,16},{24,28},{28,24},{1,5},{5... | collective-permute-start | bytes 399368 | tf_op jit(solution)/shard_map/ppermute | solution.py:367
  12.8 1.5 %collective-permute-start.4 = (bf16[8,8320]{1,0:T(8,128)(2,1)S(1)}, bf16[8,8320]{1,0:T(8,128)(2,1)S(1)}, u32[]{:S(2)}, u32[]{:S(2)}) collective-permute-start(bf16[8,8320]{1,0:T(8,128)(2,1)S(1)} %collective-permute-done.3.refs_2_), channel_id=1, source_target_pairs={{0,4},{4,0},{8,12},{12,8},{16,20},{20,16},{24,28},{28,24},{1,5},{5... | collective-permute-start | bytes 399368 | tf_op jit(solution)/shard_map/ppermute | solution.py:367
  12.8 1.5 %collective-permute-start.7 = (bf16[8,8320]{1,0:T(8,128)(2,1)S(1)}, bf16[8,8320]{1,0:T(8,128)(2,1)S(1)}, u32[]{:S(2)}, u32[]{:S(2)}) collective-permute-start(bf16[8,8320]{1,0:T(8,128)(2,1)S(1)} %collective-permute-done.6.refs_3_), channel_id=1, source_target_pairs={{0,4},{4,0},{8,12},{12,8},{16,20},{20,16},{24,28},{28,24},{1,5},{5... | collective-permute-start | bytes 399368 | tf_op jit(solution)/shard_map/ppermute | solution.py:367
  17.6 4.7 %collective-permute-start.11 = (bf16[2,8,512]{2,1,0:T(8,128)(2,1)S(1)}, bf16[2,8,512]{2,1,0:T(8,128)(2,1)S(1)}, u32[]{:S(2)}, u32[]{:S(2)}) collective-permute-start(bf16[2,8,512]{2,1,0:T(8,128)(2,1)S(1)} %get-tuple-element.26), channel_id=1, source_target_pairs={{0,24},{4,28},{8,16},{12,20},{16,8},{20,12},{24,0},{28,4},{1,25},{... | collective-permute-start | bytes 49160 | tf_op jit(solution)/shard_map/ppermute | solution.py:367
  19.7 3.7 %collective-permute-start.12 = (bf16[2,8,512]{2,1,0:T(8,128)(2,1)S(1)}, bf16[2,8,512]{2,1,0:T(8,128)(2,1)S(1)}, u32[]{:S(2)}, u32[]{:S(2)}) collective-permute-start(bf16[2,8,512]{2,1,0:T(8,128)(2,1)S(1)} %get-tuple-element.27), channel_id=1, source_target_pairs={{0,16},{4,20},{8,24},{12,28},{16,0},{20,4},{24,8},{28,12},{1,17},{... | collective-permute-start | bytes 49160 | tf_op jit(solution)/shard_map/ppermute | solution.py:367
  20.7 3.1 %collective-permute-start.10 = (bf16[8,512]{1,0:T(8,128)(2,1)S(1)}, bf16[8,512]{1,0:T(8,128)(2,1)S(1)}, u32[]{:S(2)}, u32[]{:S(2)}) collective-permute-start(bf16[8,512]{1,0:T(8,128)(2,1)S(1)} %get-tuple-element.25), channel_id=1, source_target_pairs={{0,12},{4,8},{8,4},{12,0},{16,28},{20,24},{24,20},{28,16},{1,13},{... | collective-permute-start | bytes 24584 | tf_op jit(solution)/shard_map/ppermute | solution.py:367
  20.7 3.7 %collective-permute-start.9 = (bf16[8,512]{1,0:T(8,128)(2,1)S(1)}, bf16[8,512]{1,0:T(8,128)(2,1)S(1)}, u32[]{:S(2)}, u32[]{:S(2)}) collective-permute-start(bf16[8,512]{1,0:T(8,128)(2,1)S(1)} %get-tuple-element.24), channel_id=1, source_target_pairs={{0,8},{4,12},{8,0},{12,4},{16,24},{20,28},{24,16},{28,20},{1,9},{5... | collective-permute-start | bytes 24584 | tf_op jit(solution)/shard_map/ppermute | solution.py:367
  23.5 1.2 %collective-permute-start.13 = (bf16[3,8,512]{2,1,0:T(8,128)(2,1)S(1)}, bf16[3,8,512]{2,1,0:T(8,128)(2,1)S(1)}, u32[]{:S(2)}, u32[]{:S(2)}) collective-permute-start(bf16[3,8,512]{2,1,0:T(8,128)(2,1)S(1)} %shard_map.70), channel_id=1, source_target_pairs={{0,4},{4,0},{8,12},{12,8},{16,20},{20,16},{24,28},{28,24},{1,5},{5... | collective-permute-start | bytes 73736 | tf_op jit(solution)/shard_map/ppermute | solution.py:367

commit v9 on v7

--- a/solution.py
+++ b/solution.py
@@ -320,27 +320,30 @@
     )(*parts)
 
 
-def place_kernel(wide_ref, d_ref, y_ref, relayed_ref, out_ref, wide_s, sem):
+def place_kernel(wide_ref, d_ref, y_ref, relayed_ref, out_ref, wide_s, sems):
     _, rows, clips = wide_ref.shape
     index = lax.axis_index("own")
     core = lax.rem(index, CORES)
     chip = lax.div(index, CORES)
 
+    copies = []
+
     def put(value, flip, core_of):
-        at = pl.multiple_of((lax.bitwise_xor(chip, flip) * CORES + core_of) * clips, clips)
-        wide_s[:, pl.ds(at, clips)] = value.astype(F32)
-
+        at = pl.ds(pl.multiple_of((lax.bitwise_xor(chip, flip) * CORES + core_of) * clips, clips), clips)
+        wide_s[:, at] = value.astype(F32)
+        copies.append(pltpu.make_async_copy(wide_s.at[:, at], out_ref.at[:, at], sems.at[len(copies)]))
+        copies[-1].start()
+
+    put(relayed_ref[0], 3, 1 - core)
+    put(relayed_ref[1], 2, 1 - core)
+    put(relayed_ref[2], 0, 1 - core)
+    put(y_ref[core], 2, core)
+    put(d_ref[core], 3, core)
     put(wide_ref[0], 0, core)
     put(wide_ref[1], 1, core)
     put(wide_ref[2], 1, 1 - core)
-    put(y_ref[core], 2, core)
-    put(d_ref[core], 3, core)
-    put(relayed_ref[0], 3, 1 - core)
-    put(relayed_ref[1], 2, 1 - core)
-    put(relayed_ref[2], 0, 1 - core)
-    copy = pltpu.make_async_copy(wide_s, out_ref, sem)
-    copy.start()
-    copy.wait()
+    for copy in copies:
+        copy.wait()
 
 
 def place(*parts):
@@ -351,7 +354,7 @@
         out_shape=jax.ShapeDtypeStruct(wide, F32),
         in_specs=[VMEM] * len(parts),
         out_specs=HBM,
-        scratch_shapes=[pltpu.VMEM(wide, F32), pltpu.SemaphoreType.DMA(())],
+        scratch_shapes=[pltpu.VMEM(wide, F32), pltpu.SemaphoreType.DMA((8,))],
         compiler_params=pltpu.CompilerParams(vmem_limit_bytes=SMALL_VMEM),
     )(*parts)
 

time: 25.6 us -> 25.6 us (level)
  no operation moved by 1% of the time
where the time goes in v9:
time: 25.6 us; the launch traced here: 25.4 us
  starting transfers between devices  14.9 us (58%)
  Pallas kernels  5.9 us (23%)
  waiting for transfers between devices  4.47 us (17%)
    ppermute x12, starting transfers between devices, move(): lax.ppermute(x, 'own', [(i, to(i // CORES, i % CORES)) for i in range(siz...  9.26 us
    ppermute x2, starting transfers between devices, plane(): return lax.ppermute(x, 'qry', [(i, i ^ step) for i in range(planes)])  5.68 us
    ppermute x12, waiting for transfers between devices, move(): lax.ppermute(x, 'own', [(i, to(i // CORES, i % CORES)) for i in range(siz...  4.46 us
    pallas_call x1, Pallas kernels, score(): pl.pallas_call(lambda *refs: score_kernel(len(slots), *refs), out_shape=(...  3.26 us
    pallas_call x1, Pallas kernels, pack(): pl.pallas_call(pack_kernel, out_shape=(jax.ShapeDtypeStruct((rows, width...  0.89 us
    pallas_call x1, Pallas kernels, early(): pl.pallas_call(lambda *refs: early_kernel(len(slots), *refs), out_shape=j...  0.88 us
    pallas_call x1, Pallas kernels, place(): pl.pallas_call(place_kernel, out_shape=jax.ShapeDtypeStruct(wide, F32), i...  0.72 us
  transfers between devices with their start and end apart: 14, of which 6 were waited for; matrix products, arithmetic and copies ran while one was open for 0% of the time, Pallas kernels for 4%

profile of v9, /device:TPU:0, one launch (start us, length us, event | category | flops | bytes accessed | tf_op | source)
XLA Modules:
  0.0 25.4 jit_solution(15887822425815397841)
XLA Ops:
  0.0 0.9 %shard_map.64 = (bf16[8,8320]{1,0:T(8,128)(2,1)S(1)}, bf16[1,2,48,128]{3,2,1,0:T(8,128)(2,1)S(1)}) custom-call(bf16[8,8192]{1,0:T(8,128)(2,1)} %bitcast.6, s32[1,8]{1,0:T(1,128)} %ids_hbm.1, bf16[2,16,64]{2,1,0:T(8,128)(2,1)} %left_hbm.1, bf16[2,32,128]{2,1,0:T(8,128)(2,1)} %right_hbm.1), custom_call_target="tpu_custom_call" | custom-call | tf_op jit(solution)/shard_map/pallas_call | solution.py:87
  0.9 3.1 %collective-permute-start.5 = (bf16[1,2,48,128]{3,2,1,0:T(8,128)(2,1)S(1)}, bf16[1,2,48,128]{3,2,1,0:T(8,128)(2,1)S(1)}, u32[]{:S(2)}, u32[]{:S(2)}) collective-permute-start(bf16[1,2,48,128]{3,2,1,0:T(8,128)(2,1)S(1)} %get-tuple-element.18.refs_0_), channel_id=1, source_target_pairs={{0,1},{1,0},{2,3},{3,2},{4,5},{5,4},{6,7},{7,6},{8,9},{9,8},{10,11... | collective-permute-start | bytes 73736 | tf_op jit(solution)/shard_map/ppermute | solution.py:375
  4.0 2.4 %collective-permute-start.1 = (bf16[8,8320]{1,0:T(8,128)(2,1)S(1)}, bf16[8,8320]{1,0:T(8,128)(2,1)S(1)}, u32[]{:S(2)}, u32[]{:S(2)}) collective-permute-start(bf16[8,8320]{1,0:T(8,128)(2,1)S(1)} %get-tuple-element.17.refs_2_.refs_0_), channel_id=1, source_target_pairs={{0,24},{4,28},{8,16},{12,20},{16,8},{20,12},{24,0},{28,4},{1,25},{... | collective-permute-start | bytes 399368 | tf_op jit(solution)/shard_map/ppermute | solution.py:366
  6.4 0.5 %collective-permute-start.3 = (bf16[8,8320]{1,0:T(8,128)(2,1)S(1)}, bf16[8,8320]{1,0:T(8,128)(2,1)S(1)}, u32[]{:S(2)}, u32[]{:S(2)}) collective-permute-start(bf16[8,8320]{1,0:T(8,128)(2,1)S(1)} %get-tuple-element.17.refs_2_.refs_0_), channel_id=1, source_target_pairs={{0,8},{4,20},{8,0},{12,28},{16,24},{20,4},{24,16},{28,12},{1,9},{5... | collective-permute-start | bytes 399368 | tf_op jit(solution)/shard_map/ppermute | solution.py:366
  7.0 0.1 shard_map.65
  7.0 0.8 %collective-permute-start.6 = (bf16[8,8320]{1,0:T(8,128)(2,1)S(1)}, bf16[8,8320]{1,0:T(8,128)(2,1)S(1)}, u32[]{:S(2)}, u32[]{:S(2)}) collective-permute-start(bf16[8,8320]{1,0:T(8,128)(2,1)S(1)} %get-tuple-element.19), channel_id=1, source_target_pairs={{0,16},{4,12},{8,24},{12,4},{16,0},{20,28},{24,8},{28,20},{1,17},{... | collective-permute-start | bytes 399368 | tf_op jit(solution)/shard_map/ppermute | solution.py:366
  7.9 2.6 %collective-permute-start.8 = (bf16[2,80,128]{2,1,0:T(8,128)(2,1)S(1)}, bf16[2,80,128]{2,1,0:T(8,128)(2,1)S(1)}, u32[]{:S(2)}, u32[]{:S(2)}) collective-permute-start(bf16[2,80,128]{2,1,0:T(8,128)(2,1)S(1)} %get-tuple-element.20.refs_0_), channel_id=1, source_target_pairs={{0,2},{1,3},{2,0},{3,1},{4,6},{5,7},{6,4},{7,5},{8,10},{9,11},{10,... | collective-permute-start | bytes 122888 | tf_op jit(solution)/shard_map/ppermute | solution.py:375
  10.4 0.0 collective-permute-start
  10.5 0.5 %collective-permute-start.2 = (bf16[8,8320]{1,0:T(8,128)(2,1)S(1)}, bf16[8,8320]{1,0:T(8,128)(2,1)S(1)}, u32[]{:S(2)}, u32[]{:S(2)}) collective-permute-start(bf16[8,8320]{1,0:T(8,128)(2,1)S(1)} %collective-permute-done.1.refs_1_), channel_id=1, source_target_pairs={{0,4},{4,0},{8,12},{12,8},{16,20},{20,16},{24,28},{28,24},{1,5},{5... | collective-permute-start | bytes 399368 | tf_op jit(solution)/shard_map/ppermute | solution.py:366
  11.0 1.8 %collective-permute-done.3.refs_2_ = bf16[8,8320]{1,0:T(8,128)(2,1)S(1)} collective-permute-done((bf16[8,8320]{1,0:T(8,128)(2,1)S(1)}, bf16[8,8320]{1,0:T(8,128)(2,1)S(1)}, u32[]{:S(2)}, u32[]{:S(2)}) %collective-permute-start.3) | collective-permute-done | bytes 133152 | tf_op jit(solution)/shard_map/ppermute | solution.py:366
  12.8 0.5 %collective-permute-start.7 = (bf16[8,8320]{1,0:T(8,128)(2,1)S(1)}, bf16[8,8320]{1,0:T(8,128)(2,1)S(1)}, u32[]{:S(2)}, u32[]{:S(2)}) collective-permute-start(bf16[8,8320]{1,0:T(8,128)(2,1)S(1)} %collective-permute-done.6.refs_3_), channel_id=1, source_target_pairs={{0,4},{4,0},{8,12},{12,8},{16,20},{20,16},{24,28},{28,24},{1,5},{5... | collective-permute-start | bytes 399368 | tf_op jit(solution)/shard_map/ppermute | solution.py:366
  13.3 0.1 shard_map.66
  13.4 0.9 %shard_map.67.refs_4_ = bf16[32,8192]{1,0:T(8,128)(2,1)S(1)} custom-call(bf16[8,8320]{1,0:T(8,128)(2,1)S(1)} %get-tuple-element.17.refs_2_.refs_0_, bf16[8,8320]{1,0:T(8,128)(2,1)S(1)} %collective-permute-done.1.refs_1_, bf16[8,8320]{1,0:T(8,128)(2,1)S(1)} %collective-permute-done.3.refs_2_, bf16[8,8320]{1,0:T(8,128)(2,1)S(1)} %collective-permute-done.6.refs_3_, ...), custom_call_target="tpu_custom_call" | custom-call | flops 268435456 | bytes 1048576 | tf_op jit(solution)/shard_map/pallas_call | solution.py:199
  14.3 0.0 collective-permute-done.7.refs_3_
  14.4 3.3 %shard_map.68 = (f32[8,512]{1,0:T(8,128)S(1)}, bf16[8,512]{1,0:T(8,128)(2,1)S(1)}, bf16[8,512]{1,0:T(8,128)(2,1)S(1)}, bf16[8,512]{1,0:T(8,128)(2,1)S(1)}, bf16[...) custom-call(bf16[8,8320]{1,0:T(8,128)(2,1)S(1)} %collective-permute-done.refs_0_, ...), custom_call_target="tpu_custom_call" | custom-call | flops 1585446912 | bytes 8388608 | tf_op jit(solution)/shard_map/pallas_call | solution.py:245
  17.6 2.1 %collective-permute-start.11 = (bf16[2,8,512]{2,1,0:T(8,128)(2,1)S(1)}, bf16[2,8,512]{2,1,0:T(8,128)(2,1)S(1)}, u32[]{:S(2)}, u32[]{:S(2)}) collective-permute-start(bf16[2,8,512]{2,1,0:T(8,128)(2,1)S(1)} %get-tuple-element.26), channel_id=1, source_target_pairs={{0,24},{4,28},{8,16},{12,20},{16,8},{20,12},{24,0},{28,4},{1,25},{... | collective-permute-start | bytes 49160 | tf_op jit(solution)/shard_map/ppermute | solution.py:366
  19.7 1.0 %collective-permute-start.12 = (bf16[2,8,512]{2,1,0:T(8,128)(2,1)S(1)}, bf16[2,8,512]{2,1,0:T(8,128)(2,1)S(1)}, u32[]{:S(2)}, u32[]{:S(2)}) collective-permute-start(bf16[2,8,512]{2,1,0:T(8,128)(2,1)S(1)} %get-tuple-element.27), channel_id=1, source_target_pairs={{0,16},{4,20},{8,24},{12,28},{16,0},{20,4},{24,8},{28,12},{1,17},{... | collective-permute-start | bytes 49160 | tf_op jit(solution)/shard_map/ppermute | solution.py:366
  20.7 1.4 %collective-permute-start.9 = (bf16[8,512]{1,0:T(8,128)(2,1)S(1)}, bf16[8,512]{1,0:T(8,128)(2,1)S(1)}, u32[]{:S(2)}, u32[]{:S(2)}) collective-permute-start(bf16[8,512]{1,0:T(8,128)(2,1)S(1)} %get-tuple-element.24), channel_id=1, source_target_pairs={{0,8},{4,12},{8,0},{12,4},{16,24},{20,28},{24,16},{28,20},{1,9},{5... | collective-permute-start | bytes 24584 | tf_op jit(solution)/shard_map/ppermute | solution.py:366
  22.1 0.2 collective-permute-done.11.d_ref
  22.3 1.1 %collective-permute-done.12.y_ref = bf16[2,8,512]{2,1,0:T(8,128)(2,1)S(1)} collective-permute-done((bf16[2,8,512]{2,1,0:T(8,128)(2,1)S(1)}, bf16[2,8,512]{2,1,0:T(8,128)(2,1)S(1)}, u32[]{:S(2)}, u32[]{:S(2)}) %collective-permute-start.12) | collective-permute-done | bytes 16416 | tf_op jit(solution)/shard_map/ppermute | solution.py:366
  23.5 0.3 %collective-permute-done.10.cross_ref = bf16[8,512]{1,0:T(8,128)(2,1)S(1)} collective-permute-done((bf16[8,512]{1,0:T(8,128)(2,1)S(1)}, bf16[8,512]{1,0:T(8,128)(2,1)S(1)}, u32[]{:S(2)}, u32[]{:S(2)}) %collective-permute-start.10) | collective-permute-done | bytes 8224 | tf_op jit(solution)/shard_map/ppermute | solution.py:366
  23.8 0.6 %collective-permute-done.9.x_ref = bf16[8,512]{1,0:T(8,128)(2,1)S(1)} collective-permute-done((bf16[8,512]{1,0:T(8,128)(2,1)S(1)}, bf16[8,512]{1,0:T(8,128)(2,1)S(1)}, u32[]{:S(2)}, u32[]{:S(2)}) %collective-permute-start.9) | collective-permute-done | bytes 8224 | tf_op jit(solution)/shard_map/ppermute | solution.py:366
  24.4 0.3 %collective-permute-done.13.relayed_ref = bf16[3,8,512]{2,1,0:T(8,128)(2,1)S(1)} collective-permute-done((bf16[3,8,512]{2,1,0:T(8,128)(2,1)S(1)}, bf16[3,8,512]{2,1,0:T(8,128)(2,1)S(1)}, u32[]{:S(2)}, u32[]{:S(2)}) %collective-permute-start.13) | collective-permute-done | bytes 24608 | tf_op jit(solution)/shard_map/ppermute | solution.py:366
  24.7 0.7 %shard_map.71 = f32[8,4096]{1,0:T(8,128)} custom-call(f32[3,8,512]{2,1,0:T(8,128)S(1)} %shard_map.69.wide_ref, bf16[2,8,512]{2,1,0:T(8,128)(2,1)S(1)} %collective-permute-done.11.d_ref, bf16[2,8,512]{2,1,0:T(8,128)(2,1)S(1)} %collective-permute-done.12.y_ref, bf16[3,8,512]{2,1,0:T(8,128)(2,1)S(1)} %collective-permute-done.13.relayed_ref), custom_call_target="tpu_custom_call" | custom-call | tf_op jit(solution)/shard_map/pallas_call | solution.py:352
  (19 shorter events, 0.0 us)
Async XLA Ops:
  0.9 6.1 %collective-permute-start.5 = (bf16[1,2,48,128]{3,2,1,0:T(8,128)(2,1)S(1)}, bf16[1,2,48,128]{3,2,1,0:T(8,128)(2,1)S(1)}, u32[]{:S(2)}, u32[]{:S(2)}) collective-permute-start(bf16[1,2,48,128]{3,2,1,0:T(8,128)(2,1)S(1)} %get-tuple-element.18.refs_0_), channel_id=1, source_target_pairs={{0,1},{1,0},{2,3},{3,2},{4,5},{5,4},{6,7},{7,6},{8,9},{9,8},{10,11... | collective-permute-start | bytes 73736 | tf_op jit(solution)/shard_map/ppermute | solution.py:375
  4.0 6.5 %collective-permute-start.1 = (bf16[8,8320]{1,0:T(8,128)(2,1)S(1)}, bf16[8,8320]{1,0:T(8,128)(2,1)S(1)}, u32[]{:S(2)}, u32[]{:S(2)}) collective-permute-start(bf16[8,8320]{1,0:T(8,128)(2,1)S(1)} %get-tuple-element.17.refs_2_.refs_0_), channel_id=1, source_target_pairs={{0,24},{4,28},{8,16},{12,20},{16,8},{20,12},{24,0},{28,4},{1,25},{... | collective-permute-start | bytes 399368 | tf_op jit(solution)/shard_map/ppermute | solution.py:366
  6.4 6.4 %collective-permute-start.3 = (bf16[8,8320]{1,0:T(8,128)(2,1)S(1)}, bf16[8,8320]{1,0:T(8,128)(2,1)S(1)}, u32[]{:S(2)}, u32[]{:S(2)}) collective-permute-start(bf16[8,8320]{1,0:T(8,128)(2,1)S(1)} %get-tuple-element.17.refs_2_.refs_0_), channel_id=1, source_target_pairs={{0,8},{4,20},{8,0},{12,28},{16,24},{20,4},{24,16},{28,12},{1,9},{5... | collective-permute-start | bytes 399368 | tf_op jit(solution)/shard_map/ppermute | solution.py:366
  7.0 5.8 %collective-permute-start.6 = (bf16[8,8320]{1,0:T(8,128)(2,1)S(1)}, bf16[8,8320]{1,0:T(8,128)(2,1)S(1)}, u32[]{:S(2)}, u32[]{:S(2)}) collective-permute-start(bf16[8,8320]{1,0:T(8,128)(2,1)S(1)} %get-tuple-element.19), channel_id=1, source_target_pairs={{0,16},{4,12},{8,24},{12,4},{16,0},{20,28},{24,8},{28,20},{1,17},{... | collective-permute-start | bytes 399368 | tf_op jit(solution)/shard_map/ppermute | solution.py:366
  7.8 6.5 %slice-start = ((s8[8388608]{0:T(1024)(128)(4,1)}), s8[4194304]{0:T(1024)(128)(4,1)S(1)}, s32[]{:S(2)}) async-start(s8[8388608]{0:T(1024)(128)(4,1)} %bitcast.3), calls=%async_computation | async-start | bytes 8388608
  7.9 6.5 %slice-start.1 = ((s8[8388608]{0:T(1024)(128)(4,1)}), s8[4194304]{0:T(1024)(128)(4,1)S(1)}, s32[]{:S(2)}) async-start(s8[8388608]{0:T(1024)(128)(4,1)} %bitcast.3), calls=%async_computation.1 | async-start | bytes 8388608
  7.9 6.5 %copy-start = (s32[512]{0:T(512)S(1)}, s32[512]{0:T(512)}, u32[]{:S(2)}) copy-start(s32[512]{0:T(512)} %param.11) | copy-start | bytes 6148
  7.9 5.5 %collective-permute-start.8 = (bf16[2,80,128]{2,1,0:T(8,128)(2,1)S(1)}, bf16[2,80,128]{2,1,0:T(8,128)(2,1)S(1)}, u32[]{:S(2)}, u32[]{:S(2)}) collective-permute-start(bf16[2,80,128]{2,1,0:T(8,128)(2,1)S(1)} %get-tuple-element.20.refs_0_), channel_id=1, source_target_pairs={{0,2},{1,3},{2,0},{3,1},{4,6},{5,7},{6,4},{7,5},{8,10},{9,11},{10,... | collective-permute-start | bytes 122888 | tf_op jit(solution)/shard_map/ppermute | solution.py:375
  10.4 3.8 %collective-permute-start = (bf16[8,8320]{1,0:T(8,128)(2,1)S(1)}, bf16[8,8320]{1,0:T(8,128)(2,1)S(1)}, u32[]{:S(2)}, u32[]{:S(2)}) collective-permute-start(bf16[8,8320]{1,0:T(8,128)(2,1)S(1)} %get-tuple-element.17.refs_2_.refs_0_), channel_id=1, source_target_pairs={{0,4},{4,0},{8,12},{12,8},{16,20},{20,16},{24,28},{28,24},{1,5},{5... | collective-permute-start | bytes 399368 | tf_op jit(solution)/shard_map/ppermute | solution.py:366
  10.5 3.8 %collective-permute-start.2 = (bf16[8,8320]{1,0:T(8,128)(2,1)S(1)}, bf16[8,8320]{1,0:T(8,128)(2,1)S(1)}, u32[]{:S(2)}, u32[]{:S(2)}) collective-permute-start(bf16[8,8320]{1,0:T(8,128)(2,1)S(1)} %collective-permute-done.1.refs_1_), channel_id=1, source_target_pairs={{0,4},{4,0},{8,12},{12,8},{16,20},{20,16},{24,28},{28,24},{1,5},{5... | collective-permute-start | bytes 399368 | tf_op jit(solution)/shard_map/ppermute | solution.py:366
  12.8 1.5 %collective-permute-start.4 = (bf16[8,8320]{1,0:T(8,128)(2,1)S(1)}, bf16[8,8320]{1,0:T(8,128)(2,1)S(1)}, u32[]{:S(2)}, u32[]{:S(2)}) collective-permute-start(bf16[8,8320]{1,0:T(8,128)(2,1)S(1)} %collective-permute-done.3.refs_2_), channel_id=1, source_target_pairs={{0,4},{4,0},{8,12},{12,8},{16,20},{20,16},{24,28},{28,24},{1,5},{5... | collective-permute-start | bytes 399368 | tf_op jit(solution)/shard_map/ppermute | solution.py:366
  12.8 1.5 %collective-permute-start.7 = (bf16[8,8320]{1,0:T(8,128)(2,1)S(1)}, bf16[8,8320]{1,0:T(8,128)(2,1)S(1)}, u32[]{:S(2)}, u32[]{:S(2)}) collective-permute-start(bf16[8,8320]{1,0:T(8,128)(2,1)S(1)} %collective-permute-done.6.refs_3_), channel_id=1, source_target_pairs={{0,4},{4,0},{8,12},{12,8},{16,20},{20,16},{24,28},{28,24},{1,5},{5... | collective-permute-start | bytes 399368 | tf_op jit(solution)/shard_map/ppermute | solution.py:366
  17.6 4.7 %collective-permute-start.11 = (bf16[2,8,512]{2,1,0:T(8,128)(2,1)S(1)}, bf16[2,8,512]{2,1,0:T(8,128)(2,1)S(1)}, u32[]{:S(2)}, u32[]{:S(2)}) collective-permute-start(bf16[2,8,512]{2,1,0:T(8,128)(2,1)S(1)} %get-tuple-element.26), channel_id=1, source_target_pairs={{0,24},{4,28},{8,16},{12,20},{16,8},{20,12},{24,0},{28,4},{1,25},{... | collective-permute-start | bytes 49160 | tf_op jit(solution)/shard_map/ppermute | solution.py:366
  19.7 3.7 %collective-permute-start.12 = (bf16[2,8,512]{2,1,0:T(8,128)(2,1)S(1)}, bf16[2,8,512]{2,1,0:T(8,128)(2,1)S(1)}, u32[]{:S(2)}, u32[]{:S(2)}) collective-permute-start(bf16[2,8,512]{2,1,0:T(8,128)(2,1)S(1)} %get-tuple-element.27), channel_id=1, source_target_pairs={{0,16},{4,20},{8,24},{12,28},{16,0},{20,4},{24,8},{28,12},{1,17},{... | collective-permute-start | bytes 49160 | tf_op jit(solution)/shard_map/ppermute | solution.py:366
  20.7 3.1 %collective-permute-start.10 = (bf16[8,512]{1,0:T(8,128)(2,1)S(1)}, bf16[8,512]{1,0:T(8,128)(2,1)S(1)}, u32[]{:S(2)}, u32[]{:S(2)}) collective-permute-start(bf16[8,512]{1,0:T(8,128)(2,1)S(1)} %get-tuple-element.25), channel_id=1, source_target_pairs={{0,12},{4,8},{8,4},{12,0},{16,28},{20,24},{24,20},{28,16},{1,13},{... | collective-permute-start | bytes 24584 | tf_op jit(solution)/shard_map/ppermute | solution.py:366
  20.7 3.7 %collective-permute-start.9 = (bf16[8,512]{1,0:T(8,128)(2,1)S(1)}, bf16[8,512]{1,0:T(8,128)(2,1)S(1)}, u32[]{:S(2)}, u32[]{:S(2)}) collective-permute-start(bf16[8,512]{1,0:T(8,128)(2,1)S(1)} %get-tuple-element.24), channel_id=1, source_target_pairs={{0,8},{4,12},{8,0},{12,4},{16,24},{20,28},{24,16},{28,20},{1,9},{5... | collective-permute-start | bytes 24584 | tf_op jit(solution)/shard_map/ppermute | solution.py:366
  23.5 1.2 %collective-permute-start.13 = (bf16[3,8,512]{2,1,0:T(8,128)(2,1)S(1)}, bf16[3,8,512]{2,1,0:T(8,128)(2,1)S(1)}, u32[]{:S(2)}, u32[]{:S(2)}) collective-permute-start(bf16[3,8,512]{2,1,0:T(8,128)(2,1)S(1)} %shard_map.70), channel_id=1, source_target_pairs={{0,4},{4,0},{8,12},{12,8},{16,20},{20,16},{24,28},{28,24},{1,5},{5... | collective-permute-start | bytes 73736 | tf_op jit(solution)/shard_map/ppermute | solution.py:366

commit v10 on v7

--- a/solution.py
+++ b/solution.py
@@ -212,7 +212,7 @@
 def score_kernel(nslots, *refs):
     slots = refs[:nslots]
     early_ref, left_ref, right_ref, clips_ref, len_ref = refs[nslots : nslots + 5]
-    home_ref, near_ref, x_ref, cross_ref, y_ref, d_ref, in_s, mid_s, out_s, prep_s, all_s = refs[nslots + 5 :]
+    home_ref, near_ref, x_ref, cross_ref, y_ref, d_ref, in_s, mid_s, out_s, prep_s = refs[nslots + 5 :]
     width = clips_ref.shape[1]
     rows = slots[0].shape[0]
     prepare(slots, left_ref[...], right_ref[...], in_s, mid_s, out_s, prep_s)
@@ -224,17 +224,24 @@
         factor = lax.rsqrt(F32(width) * len_ref[...].astype(F32))
         scores = raw.T * factor
         core = lax.rem(lax.axis_index("own"), CORES)
-        for j, (mine, other) in enumerate(((0, 0), (3, 3), (1 + core, 2 - core), (2 - core, 1 + core))):
-            at = j * rows
-            all_s[mine, core] = scores[at : at + rows].astype(BF16)
-            at += scores.shape[0] // 2
-            all_s[other, 1 - core] = scores[at : at + rows].astype(BF16)
         home_ref[...] = scores[:rows]
-        near_ref[...] = all_s[0, 1 - core]
-        x_ref[...] = all_s[1, core]
-        cross_ref[...] = all_s[1, 1 - core]
-        y_ref[...] = all_s[2]
-        d_ref[...] = all_s[3]
+
+        def send(own):
+            block = {}
+            for j, (mine, other) in enumerate(((0, 0), (3, 3), (1 + own, 2 - own), (2 - own, 1 + own))):
+                at = j * rows
+                block[mine, own] = scores[at : at + rows].astype(BF16)
+                at += scores.shape[0] // 2
+                block[other, 1 - own] = scores[at : at + rows].astype(BF16)
+            near_ref[...] = block[0, 1 - own]
+            x_ref[...] = block[1, own]
+            cross_ref[...] = block[1, 1 - own]
+            for of in range(CORES):
+                y_ref[of] = block[2, of]
+                d_ref[of] = block[3, of]
+
+        for own in range(CORES):
+            pl.when(core == own)(lambda own=own: send(own))
 
 
 def score(slots, prepared, left_all, right_all, clip_grads, lengths):
@@ -254,7 +261,7 @@
         scratch_shapes=[
             pltpu.VMEM((len(slots) // 2, 2 * rows, order_a, wide * width // order_a), BF16) for wide in (1, 2, 1)
         ]
-        + [pltpu.VMEM((len(slots) * rows, width), BF16), pltpu.VMEM((4, 2, rows, clips), BF16)],
+        + [pltpu.VMEM((len(slots) * rows, width), BF16)],
         compiler_params=pltpu.CompilerParams(vmem_limit_bytes=SOME_VMEM),
         cost_estimate=pl.CostEstimate(
             flops=2 * total * width * (clips + 1000), bytes_accessed=clips * width * 2, transcendentals=0

time: 25.6 us -> 25.6 us (level)
  no operation moved by 1% of the time
where the time goes in v10:
time: 25.6 us; the launch traced here: 25.4 us
  starting transfers between devices  14.9 us (58%)
  Pallas kernels  5.86 us (23%)
  waiting for transfers between devices  4.47 us (17%)
    ppermute x12, starting transfers between devices, move(): lax.ppermute(x, 'own', [(i, to(i // CORES, i % CORES)) for i in range(siz...  9.26 us
    ppermute x2, starting transfers between devices, plane(): return lax.ppermute(x, 'qry', [(i, i ^ step) for i in range(planes)])  5.68 us
    ppermute x12, waiting for transfers between devices, move(): lax.ppermute(x, 'own', [(i, to(i // CORES, i % CORES)) for i in range(siz...  4.46 us
    pallas_call x1, Pallas kernels, score(): pl.pallas_call(lambda *refs: score_kernel(len(slots), *refs), out_shape=(...  3.25 us
    pallas_call x1, Pallas kernels, pack(): pl.pallas_call(pack_kernel, out_shape=(jax.ShapeDtypeStruct((rows, width...  0.89 us
    pallas_call x1, Pallas kernels, early(): pl.pallas_call(lambda *refs: early_kernel(len(slots), *refs), out_shape=j...  0.88 us
    pallas_call x1, Pallas kernels, place(): pl.pallas_call(place_kernel, out_shape=jax.ShapeDtypeStruct(wide, F32), i...  0.68 us
  transfers between devices with their start and end apart: 14, of which 6 were waited for; matrix products, arithmetic and copies ran while one was open for 0% of the time, Pallas kernels for 4%

profile of v10, /device:TPU:0, one launch (start us, length us, event | category | flops | bytes accessed | tf_op | source)
XLA Modules:
  0.0 25.4 jit_solution(15523504873881412579)
XLA Ops:
  0.0 0.9 %shard_map.64 = (bf16[8,8320]{1,0:T(8,128)(2,1)S(1)}, bf16[1,2,48,128]{3,2,1,0:T(8,128)(2,1)S(1)}) custom-call(bf16[8,8192]{1,0:T(8,128)(2,1)} %bitcast.6, s32[1,8]{1,0:T(1,128)} %ids_hbm.1, bf16[2,16,64]{2,1,0:T(8,128)(2,1)} %left_hbm.1, bf16[2,32,128]{2,1,0:T(8,128)(2,1)} %right_hbm.1), custom_call_target="tpu_custom_call" | custom-call | tf_op jit(solution)/shard_map/pallas_call | solution.py:87
  0.9 3.1 %collective-permute-start.5 = (bf16[1,2,48,128]{3,2,1,0:T(8,128)(2,1)S(1)}, bf16[1,2,48,128]{3,2,1,0:T(8,128)(2,1)S(1)}, u32[]{:S(2)}, u32[]{:S(2)}) collective-permute-start(bf16[1,2,48,128]{3,2,1,0:T(8,128)(2,1)S(1)} %get-tuple-element.18.refs_0_), channel_id=1, source_target_pairs={{0,1},{1,0},{2,3},{3,2},{4,5},{5,4},{6,7},{7,6},{8,9},{9,8},{10,11... | collective-permute-start | bytes 73736 | tf_op jit(solution)/shard_map/ppermute | solution.py:379
  4.0 2.4 %collective-permute-start.1 = (bf16[8,8320]{1,0:T(8,128)(2,1)S(1)}, bf16[8,8320]{1,0:T(8,128)(2,1)S(1)}, u32[]{:S(2)}, u32[]{:S(2)}) collective-permute-start(bf16[8,8320]{1,0:T(8,128)(2,1)S(1)} %get-tuple-element.17.refs_2_.refs_0_), channel_id=1, source_target_pairs={{0,24},{4,28},{8,16},{12,20},{16,8},{20,12},{24,0},{28,4},{1,25},{... | collective-permute-start | bytes 399368 | tf_op jit(solution)/shard_map/ppermute | solution.py:370
  6.4 0.5 %collective-permute-start.3 = (bf16[8,8320]{1,0:T(8,128)(2,1)S(1)}, bf16[8,8320]{1,0:T(8,128)(2,1)S(1)}, u32[]{:S(2)}, u32[]{:S(2)}) collective-permute-start(bf16[8,8320]{1,0:T(8,128)(2,1)S(1)} %get-tuple-element.17.refs_2_.refs_0_), channel_id=1, source_target_pairs={{0,8},{4,20},{8,0},{12,28},{16,24},{20,4},{24,16},{28,12},{1,9},{5... | collective-permute-start | bytes 399368 | tf_op jit(solution)/shard_map/ppermute | solution.py:370
  7.0 0.1 shard_map.65
  7.0 0.8 %collective-permute-start.6 = (bf16[8,8320]{1,0:T(8,128)(2,1)S(1)}, bf16[8,8320]{1,0:T(8,128)(2,1)S(1)}, u32[]{:S(2)}, u32[]{:S(2)}) collective-permute-start(bf16[8,8320]{1,0:T(8,128)(2,1)S(1)} %get-tuple-element.19), channel_id=1, source_target_pairs={{0,16},{4,12},{8,24},{12,4},{16,0},{20,28},{24,8},{28,20},{1,17},{... | collective-permute-start | bytes 399368 | tf_op jit(solution)/shard_map/ppermute | solution.py:370
  7.9 2.6 %collective-permute-start.8 = (bf16[2,80,128]{2,1,0:T(8,128)(2,1)S(1)}, bf16[2,80,128]{2,1,0:T(8,128)(2,1)S(1)}, u32[]{:S(2)}, u32[]{:S(2)}) collective-permute-start(bf16[2,80,128]{2,1,0:T(8,128)(2,1)S(1)} %get-tuple-element.20.refs_0_), channel_id=1, source_target_pairs={{0,2},{1,3},{2,0},{3,1},{4,6},{5,7},{6,4},{7,5},{8,10},{9,11},{10,... | collective-permute-start | bytes 122888 | tf_op jit(solution)/shard_map/ppermute | solution.py:379
  10.4 0.0 collective-permute-start
  10.5 0.5 %collective-permute-start.2 = (bf16[8,8320]{1,0:T(8,128)(2,1)S(1)}, bf16[8,8320]{1,0:T(8,128)(2,1)S(1)}, u32[]{:S(2)}, u32[]{:S(2)}) collective-permute-start(bf16[8,8320]{1,0:T(8,128)(2,1)S(1)} %collective-permute-done.1.refs_1_), channel_id=1, source_target_pairs={{0,4},{4,0},{8,12},{12,8},{16,20},{20,16},{24,28},{28,24},{1,5},{5... | collective-permute-start | bytes 399368 | tf_op jit(solution)/shard_map/ppermute | solution.py:370
  11.0 1.8 %collective-permute-done.3.refs_2_ = bf16[8,8320]{1,0:T(8,128)(2,1)S(1)} collective-permute-done((bf16[8,8320]{1,0:T(8,128)(2,1)S(1)}, bf16[8,8320]{1,0:T(8,128)(2,1)S(1)}, u32[]{:S(2)}, u32[]{:S(2)}) %collective-permute-start.3) | collective-permute-done | bytes 133152 | tf_op jit(solution)/shard_map/ppermute | solution.py:370
  12.8 0.5 %collective-permute-start.7 = (bf16[8,8320]{1,0:T(8,128)(2,1)S(1)}, bf16[8,8320]{1,0:T(8,128)(2,1)S(1)}, u32[]{:S(2)}, u32[]{:S(2)}) collective-permute-start(bf16[8,8320]{1,0:T(8,128)(2,1)S(1)} %collective-permute-done.6.refs_3_), channel_id=1, source_target_pairs={{0,4},{4,0},{8,12},{12,8},{16,20},{20,16},{24,28},{28,24},{1,5},{5... | collective-permute-start | bytes 399368 | tf_op jit(solution)/shard_map/ppermute | solution.py:370
  13.3 0.1 shard_map.66
  13.4 0.9 %shard_map.67.refs_4_ = bf16[32,8192]{1,0:T(8,128)(2,1)S(1)} custom-call(bf16[8,8320]{1,0:T(8,128)(2,1)S(1)} %get-tuple-element.17.refs_2_.refs_0_, bf16[8,8320]{1,0:T(8,128)(2,1)S(1)} %collective-permute-done.1.refs_1_, bf16[8,8320]{1,0:T(8,128)(2,1)S(1)} %collective-permute-done.3.refs_2_, bf16[8,8320]{1,0:T(8,128)(2,1)S(1)} %collective-permute-done.6.refs_3_, ...), custom_call_target="tpu_custom_call" | custom-call | flops 268435456 | bytes 1048576 | tf_op jit(solution)/shard_map/pallas_call | solution.py:199
  14.3 0.0 collective-permute-done.7.refs_3_
  14.4 3.3 %shard_map.68 = (f32[8,512]{1,0:T(8,128)S(1)}, bf16[8,512]{1,0:T(8,128)(2,1)S(1)}, bf16[8,512]{1,0:T(8,128)(2,1)S(1)}, bf16[8,512]{1,0:T(8,128)(2,1)S(1)}, bf16[...) custom-call(bf16[8,8320]{1,0:T(8,128)(2,1)S(1)} %collective-permute-done.refs_0_, ...), custom_call_target="tpu_custom_call" | custom-call | flops 1585446912 | bytes 8388608 | tf_op jit(solution)/shard_map/pallas_call | solution.py:252
  17.6 2.1 %collective-permute-start.11 = (bf16[2,8,512]{2,1,0:T(8,128)(2,1)S(1)}, bf16[2,8,512]{2,1,0:T(8,128)(2,1)S(1)}, u32[]{:S(2)}, u32[]{:S(2)}) collective-permute-start(bf16[2,8,512]{2,1,0:T(8,128)(2,1)S(1)} %get-tuple-element.26), channel_id=1, source_target_pairs={{0,24},{4,28},{8,16},{12,20},{16,8},{20,12},{24,0},{28,4},{1,25},{... | collective-permute-start | bytes 49160 | tf_op jit(solution)/shard_map/ppermute | solution.py:370
  19.7 1.0 %collective-permute-start.12 = (bf16[2,8,512]{2,1,0:T(8,128)(2,1)S(1)}, bf16[2,8,512]{2,1,0:T(8,128)(2,1)S(1)}, u32[]{:S(2)}, u32[]{:S(2)}) collective-permute-start(bf16[2,8,512]{2,1,0:T(8,128)(2,1)S(1)} %get-tuple-element.27), channel_id=1, source_target_pairs={{0,16},{4,20},{8,24},{12,28},{16,0},{20,4},{24,8},{28,12},{1,17},{... | collective-permute-start | bytes 49160 | tf_op jit(solution)/shard_map/ppermute | solution.py:370
  20.7 1.4 %collective-permute-start.9 = (bf16[8,512]{1,0:T(8,128)(2,1)S(1)}, bf16[8,512]{1,0:T(8,128)(2,1)S(1)}, u32[]{:S(2)}, u32[]{:S(2)}) collective-permute-start(bf16[8,512]{1,0:T(8,128)(2,1)S(1)} %get-tuple-element.24), channel_id=1, source_target_pairs={{0,8},{4,12},{8,0},{12,4},{16,24},{20,28},{24,16},{28,20},{1,9},{5... | collective-permute-start | bytes 24584 | tf_op jit(solution)/shard_map/ppermute | solution.py:370
  22.1 0.2 collective-permute-done.11.d_ref
  22.3 1.1 %collective-permute-done.12.y_ref = bf16[2,8,512]{2,1,0:T(8,128)(2,1)S(1)} collective-permute-done((bf16[2,8,512]{2,1,0:T(8,128)(2,1)S(1)}, bf16[2,8,512]{2,1,0:T(8,128)(2,1)S(1)}, u32[]{:S(2)}, u32[]{:S(2)}) %collective-permute-start.12) | collective-permute-done | bytes 16416 | tf_op jit(solution)/shard_map/ppermute | solution.py:370
  23.5 0.3 %collective-permute-done.10.cross_ref = bf16[8,512]{1,0:T(8,128)(2,1)S(1)} collective-permute-done((bf16[8,512]{1,0:T(8,128)(2,1)S(1)}, bf16[8,512]{1,0:T(8,128)(2,1)S(1)}, u32[]{:S(2)}, u32[]{:S(2)}) %collective-permute-start.10) | collective-permute-done | bytes 8224 | tf_op jit(solution)/shard_map/ppermute | solution.py:370
  23.8 0.6 %collective-permute-done.9.x_ref = bf16[8,512]{1,0:T(8,128)(2,1)S(1)} collective-permute-done((bf16[8,512]{1,0:T(8,128)(2,1)S(1)}, bf16[8,512]{1,0:T(8,128)(2,1)S(1)}, u32[]{:S(2)}, u32[]{:S(2)}) %collective-permute-start.9) | collective-permute-done | bytes 8224 | tf_op jit(solution)/shard_map/ppermute | solution.py:370
  24.4 0.3 %collective-permute-done.13.relayed_ref = bf16[3,8,512]{2,1,0:T(8,128)(2,1)S(1)} collective-permute-done((bf16[3,8,512]{2,1,0:T(8,128)(2,1)S(1)}, bf16[3,8,512]{2,1,0:T(8,128)(2,1)S(1)}, u32[]{:S(2)}, u32[]{:S(2)}) %collective-permute-start.13) | collective-permute-done | bytes 24608 | tf_op jit(solution)/shard_map/ppermute | solution.py:370
  24.7 0.7 %shard_map.71 = f32[8,4096]{1,0:T(8,128)} custom-call(f32[3,8,512]{2,1,0:T(8,128)S(1)} %shard_map.69.wide_ref, bf16[2,8,512]{2,1,0:T(8,128)(2,1)S(1)} %collective-permute-done.11.d_ref, bf16[2,8,512]{2,1,0:T(8,128)(2,1)S(1)} %collective-permute-done.12.y_ref, bf16[3,8,512]{2,1,0:T(8,128)(2,1)S(1)} %collective-permute-done.13.relayed_ref), custom_call_target="tpu_custom_call" | custom-call | tf_op jit(solution)/shard_map/pallas_call | solution.py:356
  (19 shorter events, 0.0 us)
Async XLA Ops:
  0.9 6.1 %collective-permute-start.5 = (bf16[1,2,48,128]{3,2,1,0:T(8,128)(2,1)S(1)}, bf16[1,2,48,128]{3,2,1,0:T(8,128)(2,1)S(1)}, u32[]{:S(2)}, u32[]{:S(2)}) collective-permute-start(bf16[1,2,48,128]{3,2,1,0:T(8,128)(2,1)S(1)} %get-tuple-element.18.refs_0_), channel_id=1, source_target_pairs={{0,1},{1,0},{2,3},{3,2},{4,5},{5,4},{6,7},{7,6},{8,9},{9,8},{10,11... | collective-permute-start | bytes 73736 | tf_op jit(solution)/shard_map/ppermute | solution.py:379
  4.0 6.5 %collective-permute-start.1 = (bf16[8,8320]{1,0:T(8,128)(2,1)S(1)}, bf16[8,8320]{1,0:T(8,128)(2,1)S(1)}, u32[]{:S(2)}, u32[]{:S(2)}) collective-permute-start(bf16[8,8320]{1,0:T(8,128)(2,1)S(1)} %get-tuple-element.17.refs_2_.refs_0_), channel_id=1, source_target_pairs={{0,24},{4,28},{8,16},{12,20},{16,8},{20,12},{24,0},{28,4},{1,25},{... | collective-permute-start | bytes 399368 | tf_op jit(solution)/shard_map/ppermute | solution.py:370
  6.4 6.4 %collective-permute-start.3 = (bf16[8,8320]{1,0:T(8,128)(2,1)S(1)}, bf16[8,8320]{1,0:T(8,128)(2,1)S(1)}, u32[]{:S(2)}, u32[]{:S(2)}) collective-permute-start(bf16[8,8320]{1,0:T(8,128)(2,1)S(1)} %get-tuple-element.17.refs_2_.refs_0_), channel_id=1, source_target_pairs={{0,8},{4,20},{8,0},{12,28},{16,24},{20,4},{24,16},{28,12},{1,9},{5... | collective-permute-start | bytes 399368 | tf_op jit(solution)/shard_map/ppermute | solution.py:370
  7.0 5.8 %collective-permute-start.6 = (bf16[8,8320]{1,0:T(8,128)(2,1)S(1)}, bf16[8,8320]{1,0:T(8,128)(2,1)S(1)}, u32[]{:S(2)}, u32[]{:S(2)}) collective-permute-start(bf16[8,8320]{1,0:T(8,128)(2,1)S(1)} %get-tuple-element.19), channel_id=1, source_target_pairs={{0,16},{4,12},{8,24},{12,4},{16,0},{20,28},{24,8},{28,20},{1,17},{... | collective-permute-start | bytes 399368 | tf_op jit(solution)/shard_map/ppermute | solution.py:370
  7.8 6.5 %slice-start = ((s8[8388608]{0:T(1024)(128)(4,1)}), s8[4194304]{0:T(1024)(128)(4,1)S(1)}, s32[]{:S(2)}) async-start(s8[8388608]{0:T(1024)(128)(4,1)} %bitcast.3), calls=%async_computation | async-start | bytes 8388608
  7.9 6.5 %slice-start.1 = ((s8[8388608]{0:T(1024)(128)(4,1)}), s8[4194304]{0:T(1024)(128)(4,1)S(1)}, s32[]{:S(2)}) async-start(s8[8388608]{0:T(1024)(128)(4,1)} %bitcast.3), calls=%async_computation.1 | async-start | bytes 8388608
  7.9 6.5 %copy-start = (s32[512]{0:T(512)S(1)}, s32[512]{0:T(512)}, u32[]{:S(2)}) copy-start(s32[512]{0:T(512)} %param.11) | copy-start | bytes 6148
  7.9 5.5 %collective-permute-start.8 = (bf16[2,80,128]{2,1,0:T(8,128)(2,1)S(1)}, bf16[2,80,128]{2,1,0:T(8,128)(2,1)S(1)}, u32[]{:S(2)}, u32[]{:S(2)}) collective-permute-start(bf16[2,80,128]{2,1,0:T(8,128)(2,1)S(1)} %get-tuple-element.20.refs_0_), channel_id=1, source_target_pairs={{0,2},{1,3},{2,0},{3,1},{4,6},{5,7},{6,4},{7,5},{8,10},{9,11},{10,... | collective-permute-start | bytes 122888 | tf_op jit(solution)/shard_map/ppermute | solution.py:379
  10.4 3.8 %collective-permute-start = (bf16[8,8320]{1,0:T(8,128)(2,1)S(1)}, bf16[8,8320]{1,0:T(8,128)(2,1)S(1)}, u32[]{:S(2)}, u32[]{:S(2)}) collective-permute-start(bf16[8,8320]{1,0:T(8,128)(2,1)S(1)} %get-tuple-element.17.refs_2_.refs_0_), channel_id=1, source_target_pairs={{0,4},{4,0},{8,12},{12,8},{16,20},{20,16},{24,28},{28,24},{1,5},{5... | collective-permute-start | bytes 399368 | tf_op jit(solution)/shard_map/ppermute | solution.py:370
  10.5 3.8 %collective-permute-start.2 = (bf16[8,8320]{1,0:T(8,128)(2,1)S(1)}, bf16[8,8320]{1,0:T(8,128)(2,1)S(1)}, u32[]{:S(2)}, u32[]{:S(2)}) collective-permute-start(bf16[8,8320]{1,0:T(8,128)(2,1)S(1)} %collective-permute-done.1.refs_1_), channel_id=1, source_target_pairs={{0,4},{4,0},{8,12},{12,8},{16,20},{20,16},{24,28},{28,24},{1,5},{5... | collective-permute-start | bytes 399368 | tf_op jit(solution)/shard_map/ppermute | solution.py:370
  12.8 1.5 %collective-permute-start.4 = (bf16[8,8320]{1,0:T(8,128)(2,1)S(1)}, bf16[8,8320]{1,0:T(8,128)(2,1)S(1)}, u32[]{:S(2)}, u32[]{:S(2)}) collective-permute-start(bf16[8,8320]{1,0:T(8,128)(2,1)S(1)} %collective-permute-done.3.refs_2_), channel_id=1, source_target_pairs={{0,4},{4,0},{8,12},{12,8},{16,20},{20,16},{24,28},{28,24},{1,5},{5... | collective-permute-start | bytes 399368 | tf_op jit(solution)/shard_map/ppermute | solution.py:370
  12.8 1.5 %collective-permute-start.7 = (bf16[8,8320]{1,0:T(8,128)(2,1)S(1)}, bf16[8,8320]{1,0:T(8,128)(2,1)S(1)}, u32[]{:S(2)}, u32[]{:S(2)}) collective-permute-start(bf16[8,8320]{1,0:T(8,128)(2,1)S(1)} %collective-permute-done.6.refs_3_), channel_id=1, source_target_pairs={{0,4},{4,0},{8,12},{12,8},{16,20},{20,16},{24,28},{28,24},{1,5},{5... | collective-permute-start | bytes 399368 | tf_op jit(solution)/shard_map/ppermute | solution.py:370
  17.6 4.7 %collective-permute-start.11 = (bf16[2,8,512]{2,1,0:T(8,128)(2,1)S(1)}, bf16[2,8,512]{2,1,0:T(8,128)(2,1)S(1)}, u32[]{:S(2)}, u32[]{:S(2)}) collective-permute-start(bf16[2,8,512]{2,1,0:T(8,128)(2,1)S(1)} %get-tuple-element.26), channel_id=1, source_target_pairs={{0,24},{4,28},{8,16},{12,20},{16,8},{20,12},{24,0},{28,4},{1,25},{... | collective-permute-start | bytes 49160 | tf_op jit(solution)/shard_map/ppermute | solution.py:370
  19.7 3.7 %collective-permute-start.12 = (bf16[2,8,512]{2,1,0:T(8,128)(2,1)S(1)}, bf16[2,8,512]{2,1,0:T(8,128)(2,1)S(1)}, u32[]{:S(2)}, u32[]{:S(2)}) collective-permute-start(bf16[2,8,512]{2,1,0:T(8,128)(2,1)S(1)} %get-tuple-element.27), channel_id=1, source_target_pairs={{0,16},{4,20},{8,24},{12,28},{16,0},{20,4},{24,8},{28,12},{1,17},{... | collective-permute-start | bytes 49160 | tf_op jit(solution)/shard_map/ppermute | solution.py:370
  20.7 3.1 %collective-permute-start.10 = (bf16[8,512]{1,0:T(8,128)(2,1)S(1)}, bf16[8,512]{1,0:T(8,128)(2,1)S(1)}, u32[]{:S(2)}, u32[]{:S(2)}) collective-permute-start(bf16[8,512]{1,0:T(8,128)(2,1)S(1)} %get-tuple-element.25), channel_id=1, source_target_pairs={{0,12},{4,8},{8,4},{12,0},{16,28},{20,24},{24,20},{28,16},{1,13},{... | collective-permute-start | bytes 24584 | tf_op jit(solution)/shard_map/ppermute | solution.py:370
  20.7 3.7 %collective-permute-start.9 = (bf16[8,512]{1,0:T(8,128)(2,1)S(1)}, bf16[8,512]{1,0:T(8,128)(2,1)S(1)}, u32[]{:S(2)}, u32[]{:S(2)}) collective-permute-start(bf16[8,512]{1,0:T(8,128)(2,1)S(1)} %get-tuple-element.24), channel_id=1, source_target_pairs={{0,8},{4,12},{8,0},{12,4},{16,24},{20,28},{24,16},{28,20},{1,9},{5... | collective-permute-start | bytes 24584 | tf_op jit(solution)/shard_map/ppermute | solution.py:370
  23.5 1.2 %collective-permute-start.13 = (bf16[3,8,512]{2,1,0:T(8,128)(2,1)S(1)}, bf16[3,8,512]{2,1,0:T(8,128)(2,1)S(1)}, u32[]{:S(2)}, u32[]{:S(2)}) collective-permute-start(bf16[3,8,512]{2,1,0:T(8,128)(2,1)S(1)} %shard_map.70), channel_id=1, source_target_pairs={{0,4},{4,0},{8,12},{12,8},{16,20},{20,16},{24,28},{28,24},{1,5},{5... | collective-permute-start | bytes 73736 | tf_op jit(solution)/shard_map/ppermute | solution.py:370
